TPU v7x, 32 devices: a whole 2x2x4 slice. The times are simulated.
32 devices in a mesh: seq: 16 (over z, x, core), tensor: 2 (over y).
Axes of the slice: x: 2, y: 2, z: 4, core: 2. Of those that a mesh axis runs over, the one named last changes fastest.
Arguments:
- keyval: bfloat16 [8192, 8192], P('seq', 'tensor'), may hold values from -6 to 6
- gating: bfloat16 [8192, 8192], P('seq', 'tensor'), may hold values from -6 to 6
- skip_gain: float32 [8192], P('tensor'), may hold values from -4 to 4
- filter_values: float32 [2, 32, 4, 16, 8192], P(None, None, None, 'seq', 'tensor'), may hold values from -12 to 12
- blocks: int32 [64, 32], P('tensor'), may hold values from 0 to 127, as said below
- out_weight: bfloat16 [8192, 8192], P('seq', 'tensor'), may hold values from -0.0625 to 0.0625
Outputs:
- mixed: bfloat16 [8192, 8192], P('seq', 'tensor')
Inputs may be any that keep to these rules, and one draw needn't show every extreme that they name: Each row names 32 different blocks.
All inputs are finite; a program needn't handle non-finite values.
Results may differ from a plain program's by a relative error of at most 0.0063.
Values may be sent and summed in bfloat16 or wider, within the bound.
No kernel may reach another device: no remote copies, remote signals or barrier semaphores. Data moves between devices by JAX's collectives and lax.ppermute only.
A program may use at most 192 MiB of HBM per device.

v0:
```python
import math

import jax
import jax.numpy as jnp
from jax import lax
from jax.sharding import PartitionSpec as P

BLOCK = 64


HIGHEST = lax.Precision.HIGHEST


def tables(first_index, second_index, length):
    phase = first_index * second_index % length
    angle = 2.0 * math.pi / length * phase.astype(jnp.float32)
    return (jnp.cos(angle), jnp.sin(angle))


def rounded(value):
    return lax.optimization_barrier(value.astype(jnp.bfloat16)).astype(jnp.float32)


def whole_conv(signal_group, block_list, filter_group, cycle_size, tokens_local):
    seq_length = cycle_size * tokens_local
    unit = signal_group.shape[1]
    repeat = filter_group.shape[2]
    signal = signal_group.astype(jnp.float32).reshape(cycle_size, tokens_local, unit)
    cycle_index = jnp.arange(cycle_size, dtype=jnp.int32)
    local_index = jnp.arange(tokens_local, dtype=jnp.int32)
    cosine_cycle, sine_cycle = tables(cycle_index[:, None], cycle_index[None, :], cycle_size)
    first_real = jnp.einsum("pa,ajc->pjc", cosine_cycle, signal, precision=HIGHEST)
    first_imaginary = -jnp.einsum("pa,ajc->pjc", sine_cycle, signal, precision=HIGHEST)
    cosine_twist, sine_twist = tables(cycle_index[:, None], local_index[None, :], seq_length)
    cosine_twist = cosine_twist[:, :, None]
    sine_twist = sine_twist[:, :, None]
    twist_real = rounded(first_real * cosine_twist + first_imaginary * sine_twist)
    twist_imaginary = rounded(first_imaginary * cosine_twist - first_real * sine_twist)
    kept_rows = (
        block_list[:, None] * repeat + jnp.arange(repeat, dtype=jnp.int32)[None, :]
    ).reshape(-1)
    cosine_kept, sine_kept = tables(kept_rows[:, None], local_index[None, :], tokens_local)
    spectrum_real = jnp.einsum(
        "qj,pjc->pqc", cosine_kept, twist_real, precision=HIGHEST
    ) + jnp.einsum("qj,pjc->pqc", sine_kept, twist_imaginary, precision=HIGHEST)
    spectrum_imaginary = jnp.einsum(
        "qj,pjc->pqc", cosine_kept, twist_imaginary, precision=HIGHEST
    ) - jnp.einsum("qj,pjc->pqc", sine_kept, twist_real, precision=HIGHEST)
    filter_real = filter_group[0].reshape(-1, cycle_size, unit).transpose(1, 0, 2)
    filter_imaginary = filter_group[1].reshape(-1, cycle_size, unit).transpose(1, 0, 2)
    product_real = filter_real * spectrum_real - filter_imaginary * spectrum_imaginary
    product_imaginary = filter_real * spectrum_imaginary + filter_imaginary * spectrum_real
    back_real = jnp.einsum(
        "qj,pqc->pjc", cosine_kept, product_real, precision=HIGHEST
    ) - jnp.einsum("qj,pqc->pjc", sine_kept, product_imaginary, precision=HIGHEST)
    back_imaginary = jnp.einsum(
        "qj,pqc->pjc", sine_kept, product_real, precision=HIGHEST
    ) + jnp.einsum("qj,pqc->pjc", cosine_kept, product_imaginary, precision=HIGHEST)
    turned_real = rounded(back_real * cosine_twist - back_imaginary * sine_twist)
    turned_imaginary = rounded(back_real * sine_twist + back_imaginary * cosine_twist)
    convolved = (
        jnp.einsum("pa,pjc->ajc", cosine_cycle, turned_real, precision=HIGHEST)
        - jnp.einsum("pa,pjc->ajc", sine_cycle, turned_imaginary, precision=HIGHEST)
    ) / seq_length
    return convolved.astype(jnp.bfloat16).reshape(seq_length, unit)


def body(keyval, gating, skip_gain, filter_values, blocks, out_weight):
    cycle_size = lax.axis_size("seq")
    cycle_pos = lax.axis_index("seq")
    tokens_local, channels = keyval.shape
    seq_length = tokens_local * cycle_size
    repeat = BLOCK // cycle_size
    groups_local = blocks.shape[0]
    group_width = channels // groups_local
    narrow = channels // cycle_size
    unit = min(narrow, group_width)
    subgroups = narrow // unit
    columns = lax.all_to_all(keyval, "seq", split_axis=1, concat_axis=0, tiled=True)
    filter_cols = lax.all_to_all(filter_values, "seq", split_axis=4, concat_axis=3, tiled=True)
    sub_group = (cycle_pos * narrow + jnp.arange(subgroups, dtype=jnp.int32) * unit) // group_width
    match = sub_group[:, None, None] == jnp.arange(groups_local, dtype=jnp.int32)[None, :, None]
    sub_blocks = jnp.sum(jnp.where(match, blocks[None, :, :], 0), axis=1)
    sub_signal = columns.reshape(seq_length, subgroups, unit).transpose(1, 0, 2)
    sub_filters = filter_cols.reshape(
        2, filter_cols.shape[1], repeat, cycle_size, subgroups, unit
    ).transpose(4, 0, 1, 2, 3, 5)

    def sub_step(items):
        return whole_conv(items[0], items[1], items[2], cycle_size, tokens_local)

    done = lax.map(sub_step, (sub_signal, sub_blocks, sub_filters))
    done = done.transpose(1, 0, 2).reshape(seq_length, narrow)
    convolved = lax.all_to_all(done, "seq", split_axis=0, concat_axis=1, tiled=True)
    hidden = (
        gating.astype(jnp.float32)
        * (convolved.astype(jnp.float32) + skip_gain[None, :] * keyval.astype(jnp.float32))
    ).astype(jnp.bfloat16)
    full_hidden = lax.all_gather(hidden, "tensor", axis=1, tiled=True)
    mixed_rows = jnp.dot(
        full_hidden,
        lax.all_gather(out_weight, "seq", axis=0, tiled=True),
        preferred_element_type=jnp.float32,
    )
    return mixed_rows.astype(jnp.bfloat16)


def solution(mesh):
    placed = (
        P("seq", "tensor"),
        P("seq", "tensor"),
        P("tensor"),
        P(None, None, None, "seq", "tensor"),
        P("tensor", None),
        P("seq", "tensor"),
    )
    return jax.shard_map(
        body, mesh=mesh, in_specs=placed, out_specs=P("seq", "tensor"), check_vma=False
    )
```

profile of v0, /device:TPU:9, one launch (start us, length us, event | category | flops | bytes accessed | tf_op | source)
XLA Modules:
  0.0 1063.5 jit_solution(7751110549590279602)
XLA Ops:
  6.5 6.4 copy.153
  12.9 6.6 all-to-all-start.1
  19.5 17.6 %copy.151 = f32[2,32,4,1,4096]{1,2,3,0,4:T(4,128)} copy(f32[2,32,4,1,4096]{4,3,2,1,0:T(1,128)} %param.11) | data formatting | bytes 8388608 | tf_op args[3]
  37.1 17.8 %reshape.154 = f32[16,1,65536]{2,1,0:T(1,128)} reshape(f32[4096,2,1,4,32]{4,3,2,1,0:T(4,128)} %bitcast.169) | data formatting | bytes 8388608
  54.9 55.0 %all-to-all-done.1 = bf16[512,16,256]{0,2,1:T(8,128)(2,1)} async-done(((bf16[512,16,256]{0,2,1:T(8,128)(2,1)}), bf16[512,16,256]{0,2,1:T(8,128)(2,1)}, u32[]{:S(2)}, u32[]{:S(2)}) %all-to-all-start.1) | async-done | bytes 4194336 | tf_op jit(solution)/shard_map/all_to_all | solution.py:79
  109.8 7.1 all-to-all-start
  117.1 6.5 copy.154
  123.6 7.4 reshape.146
  131.0 76.2 %all-to-all-done = f32[16,1,65536]{2,1,0:T(1,128)} async-done(((f32[16,1,65536]{2,1,0:T(1,128)}), f32[16,1,65536]{2,1,0:T(1,128)}, u32[]{:S(2)}, u32[]{:S(2)}) %all-to-all-start) | async-done | bytes 4194336 | tf_op jit(solution)/shard_map/all_to_all | solution.py:80
  207.7 13.7 %reduce = f32[16,65536]{1,0:T(8,128)} reduce(f32[16,1,65536]{2,1,0:T(1,128)} %all-to-all-done, f32[]{:T(128)} %broadcast.347), dimensions={1}, to_apply=%all_to_all.14.reduce_sub_computation | reduce | bytes 8388612 | tf_op jit(solution)/shard_map/all_to_all | solution.py:80
  221.4 18.4 %reshape.155 = f32[4096,2,1,4,32]{4,3,2,1,0:T(4,128)} reshape(f32[16,65536]{1,0:T(8,128)} %reduce) | data formatting | bytes 8388608
  239.8 15.0 %copy.164 = f32[2,32,4,16,2,128]{5,4,3,1,2,0:T(2,128)} copy(f32[2,32,4,16,2,128]{1,2,0,5,4,3:T(4,128)} %bitcast.168) | data formatting | bytes 8388608 | tf_op jit(solution)/shard_map/reshape | solution.py:85
  254.8 203.5 %while.13 = (s32[]{:T(128)}, bf16[2,8192,128]{2,1,0:T(8,128)(2,1)}, f32[2,2,32,4,16,128]{5,0,4,2,3,1:T(2,128)}, bf16[2,8192,128]{1,2,0:T(8,128)(2,1)}, s32[2,32]{1,0:T(2,128)S(1)}, /*index=5*/s32[]{:T(128)}, s32[]{:T(128)}, s32[]{}) while((s32[]{:T(128)}, bf16[2,8192,128]{2,1,0:T(8,128)(2,1)}, f32[2,2,32,4,16,128]{5,0,4,2,3,1:T(2,128)}, ...), condition=%wide.region_2.3_spmd, body=%wide.region_1.2_spmd.sunk | while | flops 13722843136 | bytes 147135024 | solution.py:92
  261.6 7.1 fusion.182
  269.2 10.6 add_convert_fusion.3
  282.9 3.8 fusion.185
  289.9 4.1 fusion.186
  294.0 3.8 fusion.187
  297.8 5.4 constant_dynamic-slice_fusion.6
  311.8 4.7 fusion.188
  316.5 4.6 fusion.189
  321.2 4.4 convolution_add_fusion.3
  325.6 4.9 fusion.190
  330.5 6.7 fusion.191
  340.7 3.8 fusion.192
  347.9 4.2 multiply_convert_fusion.2
  360.7 7.1 fusion.182
  368.2 10.6 add_convert_fusion.3
  382.0 3.8 fusion.185
  389.0 4.1 fusion.186
  393.1 3.8 fusion.187
  396.9 5.4 constant_dynamic-slice_fusion.6
  410.9 4.7 fusion.188
  415.6 4.8 fusion.189
  420.5 4.4 convolution_add_fusion.3
  424.9 4.6 fusion.190
  429.5 6.7 fusion.191
  446.9 4.2 multiply_convert_fusion.2
  458.3 6.4 copy.157
  464.7 4.0 copy.169
  468.8 4.4 copy.158
  473.1 7.1 all-to-all-start.2
  480.3 6.5 copy.150
  486.8 83.7 %all-to-all-done.2 = bf16[16,512,256]{1,2,0:T(8,128)(2,1)} async-done(((bf16[16,512,256]{1,2,0:T(8,128)(2,1)}), bf16[16,512,256]{1,2,0:T(8,128)(2,1)}, u32[]{:S(2)}, u32[]{:S(2)}) %all-to-all-start.2) | async-done | bytes 4194336 | tf_op jit(solution)/shard_map/all_to_all | solution.py:94
  570.5 6.9 fusion.114
  578.2 105.1 %all-gather.3.cloned.1.call-done = bf16[512,8192]{0,1:T(8,128)(2,1)} async-done(((bf16[512,4096]{0,1:T(8,128)(2,1)}), bf16[512,8192]{0,1:T(8,128)(2,1)}) %all-gather.3.cloned.1.call-update) | async-done | bytes 8388624 | tf_op jit(solution)/shard_map/all_gather | solution.py:99
  683.3 328.2 %all-gather.5.cloned.1.call-done = bf16[8192,4096]{1,0:T(8,128)(2,1)} async-done(((bf16[512,4096]{1,0:T(8,128)(2,1)}), bf16[8192,4096]{1,0:T(8,128)(2,1)}) %all-gather.5.cloned.1.call-update) | async-done | bytes 67108880 | tf_op jit(solution)/shard_map/all_gather | solution.py:102
  1011.4 44.7 %convolution_convert_fusion = bf16[512,4096]{1,0:T(8,128)(2,1)} fusion(bf16[512,8192]{0,1:T(8,128)(2,1)} %all-gather.3.cloned.1.call-done, bf16[8192,4096]{1,0:T(8,128)(2,1)} %all-gather.5.cloned.1.call-done), kind=kOutput, calls=%fused_computation.132 | convolution fusion | flops 34361835520 | bytes 79691776 | tf_op jit(solution)/shard_map/dot_general | solution.py:100
  (58 shorter events, 66.6 us)
Async XLA Ops:
  12.9 96.9 %all-to-all-start.1 = ((bf16[512,16,256]{0,2,1:T(8,128)(2,1)}), bf16[512,16,256]{0,2,1:T(8,128)(2,1)}, u32[]{:S(2)}, u32[]{:S(2)}) async-start(bf16[512,16,256]{0,2,1:T(8,128)(2,1)} %bitcast.172), calls=%async_computation.1 | async-start | bytes 8388608 | tf_op jit(solution)/shard_map/all_to_all | solution.py:79
  54.9 62.1 %copy-start.3 = (s32[32,32]{1,0:T(8,128)S(1)}, s32[32,32]{1,0:T(8,128)}, u32[]{:S(2)}) copy-start(s32[32,32]{1,0:T(8,128)} %param.12) | copy-start | bytes 12292
  109.8 97.4 %all-to-all-start = ((f32[16,1,65536]{2,1,0:T(1,128)}), f32[16,1,65536]{2,1,0:T(1,128)}, u32[]{:S(2)}, u32[]{:S(2)}) async-start(f32[16,1,65536]{2,1,0:T(1,128)} %reshape.154), calls=%async_computation | async-start | bytes 8388608 | tf_op jit(solution)/shard_map/all_to_all | solution.py:80
  282.7 4.0 copy-start
  303.2 8.7 copy-start.1
  381.8 4.0 copy-start
  402.2 8.7 copy-start.1
  473.1 97.4 %all-to-all-start.2 = ((bf16[16,512,256]{1,2,0:T(8,128)(2,1)}), bf16[16,512,256]{1,2,0:T(8,128)(2,1)}, u32[]{:S(2)}, u32[]{:S(2)}) async-start(bf16[16,512,256]{1,2,0:T(8,128)(2,1)} %copy.158), calls=%async_computation.2 | async-start | bytes 8388608 | tf_op jit(solution)/shard_map/all_to_all | solution.py:94
  480.2 90.3 %copy-start.2 = (f32[4096]{0:T(1024)S(1)}, f32[4096]{0:T(1024)}, u32[]{:S(2)}) copy-start(f32[4096]{0:T(1024)} %param.10) | copy-start | bytes 49156
  480.2 203.1 %all-gather.3.cloned.1.call-start = ((), (), s32[]{:S(2)}) async-start(), calls=%async_computation.3 | async-start | bytes 12582912 | tf_op jit(solution)/shard_map/all_gather | solution.py:99
  577.5 434.0 %all-gather.5.cloned.1.call-start = ((), (), s32[]{:S(2)}) async-start(), calls=%async_computation.4 | async-start | bytes 71303168 | tf_op jit(solution)/shard_map/all_gather | solution.py:102
Sparse Core Ops, SparseCore 0:
  577.6 105.6 all-gather.2
  684.9 326.5 all-gather.4
where the time goes:
time: 1080 us; the launch traced here: 1060 us
  waiting for transfers between devices  649 us (60%)
  local copies, waits for them, and re-layouts  183 us (17%)
  matrix products  170 us (16%)
  other arithmetic  21.2 us (2%)
  starting transfers between devices  20.8 us (2%)
  between operations  13.9 us (1%)
    all_gather x1, waiting for transfers between devices, body(): lax.all_gather(out_weight, 'seq', axis=0, tiled=True)  328 us
    all_gather x1, waiting for transfers between devices, body(): full_hidden = lax.all_gather(hidden, 'tensor', axis=1, tiled=True)  105 us
    all_to_all x1, waiting for transfers between devices, body(): lax.all_to_all(done, 'seq', split_axis=0, concat_axis=1, tiled=True)  83.7 us
    all_to_all x1, waiting for transfers between devices, body(): lax.all_to_all(filter_values, 'seq', split_axis=4, concat_axis=3, tiled=T...  76.2 us
    unnamed x10, local copies, waits for them, and re-layouts  70.7 us
    all_to_all x1, waiting for transfers between devices, body(): lax.all_to_all(keyval, 'seq', split_axis=1, concat_axis=0, tiled=True)  55 us
    dot_general x1, matrix products, body(): jnp.dot(full_hidden, lax.all_gather(out_weight, 'seq', axis=0, tiled=True...  44.7 us
    optimization_barrier x8, local copies, waits for them, and re-layouts, rounded(): lax.optimization_barrier(value.astype(jnp.bfloat16)).astype(jnp.float32)  26.1 us
  transfers between devices with their start and end apart: 5, of which 5 were waited for; matrix products, arithmetic and copies ran while one was open for 5% of the time, Pallas kernels for 0%

commit v1 on v0

v1 whole, which is shorter than its diff:
```python
import functools
import math

import jax
import jax.numpy as jnp
from jax import lax
from jax.experimental import pallas as pl
from jax.experimental.pallas import tpu as pltpu
from jax.sharding import PartitionSpec as P

BLOCK = 64
ROWS = 16
VMEM = 48 * 2**20
F32 = jnp.float32
BF16 = jnp.bfloat16


def tables(first_index, second_index, length):
    phase = first_index * second_index % length
    angle = 2.0 * math.pi / length * phase.astype(F32)
    return (jnp.cos(angle), jnp.sin(angle))


def real_forward(values):
    n = len(values)
    if n == 2:
        return [(values[0] + values[1], None), (values[0] - values[1], None)]
    even, odd = real_forward(values[0::2]), real_forward(values[1::2])
    half = n // 2
    out = [None] * (half + 1)
    for p in range(half // 2 + 1):
        (er, ei), (dr, di) = even[p], odd[p]
        if p == 0:
            out[0], out[half] = (er + dr, None), (er - dr, None)
        elif 2 * p == half:
            out[p] = (er, -dr)
        else:
            c, s = math.cos(2 * math.pi * p / n), math.sin(2 * math.pi * p / n)
            tr, ti = dr * c + di * s, di * c - dr * s
            out[p], out[half - p] = (er + tr, ei + ti), (er - tr, ti - ei)
    return out


def real_inverse(freqs):
    half = len(freqs) - 1
    if half == 1:
        return [freqs[0][0] + freqs[1][0], freqs[0][0] - freqs[1][0]]
    n = 2 * half
    even, odd = [None] * (half // 2 + 1), [None] * (half // 2 + 1)
    for p in range(half // 2 + 1):
        (ar, ai), (br, bi) = freqs[p], freqs[half - p]
        if p == 0:
            even[0], odd[0] = (ar + br, None), (ar - br, None)
        elif 2 * p == half:
            even[p], odd[p] = (ar + ar, None), (-(ai + ai), None)
        else:
            c, s = math.cos(2 * math.pi * p / n), math.sin(2 * math.pi * p / n)
            dr, di = ar - br, ai + bi
            even[p], odd[p] = (ar + br, ai - bi), (dr * c - di * s, dr * s + di * c)
    out = [None] * n
    out[0::2], out[1::2] = real_inverse(even), real_inverse(odd)
    return out


def conv_kernel(twist_ref, ahead_ref, back_ref, x_ref, filter_ref, out_ref, first_ref, turned_ref):
    cycle, tokens, unit = x_ref.shape
    kept = filter_ref.shape[2] // 2
    per = max(1, 256 // unit)
    width = per * unit

    def twist(rows):
        block = twist_ref[rows, :]
        return [
            (block[:, p : p + 1], block[:, cycle + p : cycle + p + 1]) for p in range(cycle)
        ]

    def ahead(step, carry):
        start = pl.multiple_of(step * ROWS, ROWS)
        rows = pl.ds(start, ROWS)
        freqs = real_forward([x_ref[a, rows, :].astype(F32) for a in range(cycle)])
        for p, (c, s) in enumerate(twist(rows)):
            real, imaginary = freqs[min(p, cycle - p)]
            if imaginary is None:
                fr, fi = real * c, -(real * s)
            elif 2 * p > cycle:
                fr, fi = real * c - imaginary * s, -(imaginary * c + real * s)
            else:
                fr, fi = real * c + imaginary * s, imaginary * c - real * s
            lanes = slice(p * unit, (p + 1) * unit)
            first_ref[rows, lanes] = fr.astype(BF16)
            first_ref[pl.ds(tokens + start, ROWS), lanes] = fi.astype(BF16)
        return carry

    lax.fori_loop(0, tokens // ROWS, ahead, 0)

    def middle(step, carry):
        lanes = pl.ds(pl.multiple_of(step * width, width), width)
        spectrum = jnp.dot(ahead_ref[0], first_ref[:, lanes], preferred_element_type=F32)
        reals, imaginaries = [], []
        for u in range(per):
            part = filter_ref[step * per + u, 0].astype(F32)
            hr, hi = part[:kept], part[kept:]
            own = slice(u * unit, (u + 1) * unit)
            sr, si = spectrum[:kept, own], spectrum[kept:, own]
            reals.append(hr * sr - hi * si)
            imaginaries.append(hr * si + hi * sr)
        product = jnp.concatenate(
            [jnp.concatenate(reals, axis=1), jnp.concatenate(imaginaries, axis=1)], axis=0
        ).astype(BF16)
        turned_ref[:, lanes] = jnp.dot(back_ref[0], product, preferred_element_type=F32)
        return carry

    lax.fori_loop(0, cycle // per, middle, 0)

    def behind(step, carry):
        start = pl.multiple_of(step * ROWS, ROWS)
        rows = pl.ds(start, ROWS)
        parts = []
        for p, (c, s) in enumerate(twist(rows)):
            lanes = slice(p * unit, (p + 1) * unit)
            br = turned_ref[rows, lanes]
            bi = turned_ref[pl.ds(tokens + start, ROWS), lanes]
            parts.append(
                (
                    (br * c - bi * s).astype(BF16).astype(F32),
                    (br * s + bi * c).astype(BF16).astype(F32),
                )
            )
        half = cycle // 2
        freqs = [(parts[0][0] * 2.0, None)]
        for p in range(1, half):
            (ur, ui), (vr, vi) = parts[p], parts[cycle - p]
            freqs.append((ur + vr, ui - vi))
        freqs.append((parts[half][0] * 2.0, None))
        scale = 0.5 / (cycle * tokens)
        for a, value in enumerate(real_inverse(freqs)):
            out_ref[a, rows, :] = (value * scale).astype(BF16)
        return carry

    lax.fori_loop(0, tokens // ROWS, behind, 0)


def convolve(chunk, twist, ahead, back, signal, filters):
    cycle, tokens, unit = signal.shape
    kept = filters.shape[2] // 2
    flops = 4 * 2 * kept * 2 * tokens * cycle * unit
    return pl.pallas_call(
        conv_kernel,
        grid=(1,),
        out_shape=jax.ShapeDtypeStruct(signal.shape, BF16),
        in_specs=[
            pl.BlockSpec(twist.shape, lambda i: (0, 0)),
            pl.BlockSpec((1, *ahead.shape[1:]), lambda i: (chunk, 0, 0)),
            pl.BlockSpec((1, *back.shape[1:]), lambda i: (chunk, 0, 0)),
            pl.BlockSpec(signal.shape, lambda i: (0, 0, 0)),
            pl.BlockSpec((cycle, 1, 2 * kept, unit), lambda i: (0, chunk, 0, 0)),
        ],
        out_specs=pl.BlockSpec(signal.shape, lambda i: (0, 0, 0)),
        scratch_shapes=[
            pltpu.VMEM((2 * tokens, cycle * unit), BF16),
            pltpu.VMEM((2 * tokens, cycle * unit), F32),
        ],
        compiler_params=pltpu.CompilerParams(vmem_limit_bytes=VMEM),
        cost_estimate=pl.CostEstimate(
            flops=flops, bytes_accessed=16 * signal.size, transcendentals=0
        ),
        name="convolve",
    )(twist, ahead, back, signal, filters)


def pack_kernel(unit, x_ref, out_ref):
    for d in range(out_ref.shape[0]):
        out_ref[d] = x_ref[:, d * unit : (d + 1) * unit]


def pack_signal(keyval, chunk, cycle, unit):
    tokens = keyval.shape[0]
    wide = max(1, min(cycle, 512 // unit))
    steps = cycle // wide
    return pl.pallas_call(
        functools.partial(pack_kernel, unit),
        grid=(steps,),
        out_shape=jax.ShapeDtypeStruct((cycle, tokens, unit), BF16),
        in_specs=[pl.BlockSpec((tokens, wide * unit), lambda i: (0, chunk * steps + i))],
        out_specs=pl.BlockSpec((wide, tokens, unit), lambda i: (i, 0, 0)),
        compiler_params=pltpu.CompilerParams(vmem_limit_bytes=VMEM),
        cost_estimate=pl.CostEstimate(
            flops=0, bytes_accessed=4 * tokens * cycle * unit, transcendentals=0
        ),
        name="pack_signal",
    )(keyval)


def pack_filter_kernel(unit, f_ref, out_ref):
    for d in range(out_ref.shape[0]):
        out_ref[d, 0] = f_ref[:, 0, d * unit : (d + 1) * unit].astype(BF16)


def pack_filters(filter_values, cycle, chunks, unit):
    channels = filter_values.shape[-1]
    rows = filter_values.size // channels
    flat = filter_values.reshape(rows, 1, channels)
    wide = max(1, min(cycle, 512 // unit))
    steps = cycle // wide
    return pl.pallas_call(
        functools.partial(pack_filter_kernel, unit),
        grid=(chunks, steps),
        out_shape=jax.ShapeDtypeStruct((cycle, chunks, rows, unit), BF16),
        in_specs=[pl.BlockSpec((rows, 1, wide * unit), lambda g, i: (0, 0, g * steps + i))],
        out_specs=pl.BlockSpec((wide, 1, rows, unit), lambda g, i: (i, g, 0, 0)),
        compiler_params=pltpu.CompilerParams(vmem_limit_bytes=VMEM),
        cost_estimate=pl.CostEstimate(
            flops=0, bytes_accessed=6 * filter_values.size, transcendentals=0
        ),
        name="pack_filters",
    )(flat)


def gate_kernel(unit, c_ref, x_ref, g_ref, s_ref, out_ref):
    for d in range(c_ref.shape[0]):
        lanes = slice(d * unit, (d + 1) * unit)
        direct = s_ref[0:1, lanes] * x_ref[:, lanes].astype(F32)
        value = g_ref[:, lanes].astype(F32) * (c_ref[d].astype(F32) + direct)
        out_ref[:, lanes] = value.astype(BF16)


def gate(convolved, keyval, gating, skip_gain, chunk):
    cycle, tokens, unit = convolved.shape
    wide = max(1, min(cycle, 512 // unit))
    steps = cycle // wide
    lanes = wide * unit
    return pl.pallas_call(
        functools.partial(gate_kernel, unit),
        grid=(steps,),
        out_shape=jax.ShapeDtypeStruct((tokens, cycle * unit), BF16),
        in_specs=[
            pl.BlockSpec((wide, tokens, unit), lambda i: (i, 0, 0)),
            pl.BlockSpec((tokens, lanes), lambda i: (0, chunk * steps + i)),
            pl.BlockSpec((tokens, lanes), lambda i: (0, chunk * steps + i)),
            pl.BlockSpec((1, lanes), lambda i: (0, chunk * steps + i)),
        ],
        out_specs=pl.BlockSpec((tokens, lanes), lambda i: (0, i)),
        compiler_params=pltpu.CompilerParams(vmem_limit_bytes=VMEM),
        cost_estimate=pl.CostEstimate(
            flops=0, bytes_accessed=8 * convolved.size, transcendentals=0
        ),
        name="gate",
    )(convolved, keyval, gating, skip_gain.reshape(1, -1))


def mix_kernel(pieces, start_ref, *refs):
    w_ref, out_ref = refs[pieces], refs[pieces + 1]
    total = None
    for k in range(pieces):
        depth = refs[k].shape[1]
        start = pl.multiple_of(start_ref[k], depth)
        part = jnp.dot(
            refs[k][...], w_ref[pl.ds(start, depth), :], preferred_element_type=F32
        )
        total = part if total is None else total + part
    out_ref[...] = total.astype(BF16)


def mix(hidden, starts, weight):
    tokens = hidden[0].shape[0]
    depth, columns = weight.shape
    tile = min(256, columns)
    pieces = len(hidden)
    return pl.pallas_call(
        functools.partial(mix_kernel, pieces),
        grid=(columns // tile,),
        out_shape=jax.ShapeDtypeStruct((tokens, columns), BF16),
        in_specs=[pl.BlockSpec(memory_space=pltpu.SMEM)]
        + [pl.BlockSpec(h.shape, lambda i: (0, 0)) for h in hidden]
        + [pl.BlockSpec((depth, tile), lambda i: (0, i))],
        out_specs=pl.BlockSpec((tokens, tile), lambda i: (0, i)),
        compiler_params=pltpu.CompilerParams(vmem_limit_bytes=VMEM),
        cost_estimate=pl.CostEstimate(
            flops=2 * tokens * depth * columns,
            bytes_accessed=2 * depth * columns,
            transcendentals=0,
        ),
        name="mix",
    )(starts, *hidden, weight)


def body(keyval, gating, skip_gain, filter_values, blocks, out_weight):
    cycle = lax.axis_size("seq")
    place = lax.axis_index("seq")
    peers = lax.axis_size("tensor")
    side = lax.axis_index("tensor")
    tokens, channels = keyval.shape
    repeat = BLOCK // cycle
    groups_local = blocks.shape[0]
    group_width = channels // groups_local
    narrow = channels // cycle
    unit = min(narrow, group_width)
    chunks = narrow // unit

    weight = lax.all_gather(out_weight, "seq", axis=0, tiled=True)

    exchange = functools.partial(
        lax.all_to_all, axis_name="seq", split_axis=0, concat_axis=0, tiled=True
    )
    signals = [exchange(pack_signal(keyval, g, cycle, unit)) for g in range(chunks)]
    filters = exchange(pack_filters(filter_values, cycle, chunks, unit))

    group = (jnp.arange(chunks, dtype=jnp.int32) * cycle + place) * unit // group_width
    kept_blocks = jnp.take(blocks, group, axis=0)
    kept_rows = (
        kept_blocks[:, :, None] * repeat + jnp.arange(repeat, dtype=jnp.int32)
    ).reshape(chunks, -1)
    local_index = jnp.arange(tokens, dtype=jnp.int32)
    cosine, sine = tables(kept_rows[:, :, None], local_index[None, None, :], tokens)
    ahead = jnp.concatenate(
        [jnp.concatenate([cosine, sine], axis=2), jnp.concatenate([-sine, cosine], axis=2)],
        axis=1,
    ).astype(BF16)
    cosine, sine = tables(kept_rows[:, None, :], local_index[None, :, None], tokens)
    back = jnp.concatenate(
        [jnp.concatenate([cosine, -sine], axis=2), jnp.concatenate([sine, cosine], axis=2)],
        axis=1,
    ).astype(BF16)
    cycle_index = jnp.arange(cycle, dtype=jnp.int32)
    twist = jnp.concatenate(
        tables(local_index[:, None], cycle_index[None, :], cycle * tokens), axis=1
    )

    hidden, starts = [], []
    for g in range(chunks):
        done = exchange(convolve(g, twist, ahead, back, signals[g], filters))
        own = gate(done, keyval, gating, skip_gain, g)
        for shift in range(peers):
            if shift == 0:
                piece = own
            else:
                piece = lax.ppermute(
                    own, "tensor", [(t, (t + shift) % peers) for t in range(peers)]
                )
            hidden.append(piece)
            source = lax.rem(side + peers - shift, peers)
            starts.append(source * channels + g * cycle * unit)
    return mix(hidden, jnp.stack(starts).astype(jnp.int32), weight)


def solution(mesh):
    placed = (
        P("seq", "tensor"),
        P("seq", "tensor"),
        P("tensor"),
        P(None, None, None, "seq", "tensor"),
        P("tensor", None),
        P("seq", "tensor"),
    )
    return jax.shard_map(
        body, mesh=mesh, in_specs=placed, out_specs=P("seq", "tensor"), check_vma=False
    )
```

time: 1080 us -> 612 us (0.57); the launches traced: 1060 us -> 611 us
  waiting for transfers between devices: 649 us -> 438 us
  local copies, waits for them, and re-layouts: 183 us -> 3.64 us
  matrix products: 170 us -> 0 us
  Pallas kernels: 0 us -> 110 us
  starting transfers between devices: 20.8 us -> 40.7 us
  other arithmetic: 21.2 us -> 5.34 us
    all_gather x2 -> x1, waiting for transfers between devices: 433 us -> 107 us  [body(): weight = lax.all_gather(out_weight, 'seq', axis=0, tiled=True)]
    dot_general x25 -> x0, matrix products: 170 us -> none  [the longest x1 44.7 us: body(): jnp.dot(full_hidden, lax.all_gather(out_weight, 'seq', axis=0, tiled=True...]
    pallas_call x0 -> x8, Pallas kernels: none -> 110 us  [the longest x1 42.9 us: mix(): pl.pallas_call(functools.partial(mix_kernel, pieces), grid=(columns // ti...]
    all_to_all x3 -> x5, waiting for transfers between devices: 215 us -> 285 us  [the longest x2 111 us: body(): done = exchange(convolve(g, twist, ahead, back, signals[g], filters))]
    unnamed x10, local copies, waits for them, and re-layouts: 70.7 us -> 2.67 us
    ppermute x0 -> x2, waiting for transfers between devices: none -> 45.2 us  [body(): lax.ppermute(own, 'tensor', [(t, (t + shift) % peers) for t in range(peer...]
    optimization_barrier x8 -> x0, local copies, waits for them, and re-layouts: 26.1 us -> none  [rounded(): lax.optimization_barrier(value.astype(jnp.bfloat16)).astype(jnp.float32)]
    reshape x2 -> x0, local copies, waits for them, and re-layouts: 22.4 us -> none  [the longest x1 15 us: body(): filter_cols.reshape(2, filter_cols.shape[1], repeat, cycle_size, subgroup...]
  transfers between devices with their start and end apart: 5 -> 8, of which waited for: 5 -> 7; matrix products, arithmetic and copies ran while one was open for 5% -> 1% of each run, Pallas kernels for 0% -> 11%
where the time goes in v1:
time: 612 us; the launch traced here: 611 us
  waiting for transfers between devices  438 us (72%)
  Pallas kernels  110 us (18%)
  starting transfers between devices  40.7 us (7%)
  between operations  13.5 us (2%)
    all_to_all x2, waiting for transfers between devices, body(): done = exchange(convolve(g, twist, ahead, back, signals[g], filters))  111 us
    all_to_all x2, waiting for transfers between devices, body(): exchange(pack_signal(keyval, g, cycle, unit))  108 us
    all_gather x1, waiting for transfers between devices, body(): weight = lax.all_gather(out_weight, 'seq', axis=0, tiled=True)  107 us
    all_to_all x1, waiting for transfers between devices, body(): filters = exchange(pack_filters(filter_values, cycle, chunks, unit))  65.9 us
    ppermute x2, waiting for transfers between devices, body(): lax.ppermute(own, 'tensor', [(t, (t + shift) % peers) for t in range(peer...  45.2 us
    pallas_call x1, Pallas kernels, mix(): pl.pallas_call(functools.partial(mix_kernel, pieces), grid=(columns // ti...  42.9 us
    pallas_call x2, Pallas kernels, convolve(): pl.pallas_call(conv_kernel, grid=(1,), out_shape=jax.ShapeDtypeStruct(sig...  41.2 us
    all_to_all x2, starting transfers between devices, body(): exchange(pack_signal(keyval, g, cycle, unit))  16.1 us
  transfers between devices with their start and end apart: 8, of which 7 were waited for; matrix products, arithmetic and copies ran while one was open for 1% of the time, Pallas kernels for 11%

profile of v1, /device:TPU:9, one launch (start us, length us, event | category | flops | bytes accessed | tf_op | source)
XLA Modules:
  0.0 611.2 jit_solution(8398017755897132644)
XLA Ops:
  6.5 0.0 copy-start
  6.5 0.0 all-gather.2.cloned.1.call-start
  6.5 0.7 all-gather.2.cloned.1.call-update
  7.3 8.0 %pack_filters.1 = bf16[16,2,256,128]{3,2,1,0:T(8,128)(2,1)} custom-call(f32[256,1,4096]{2,1,0:T(1,128)} %bitcast.10), custom_call_target="tpu_custom_call" | custom-call | bytes 6291456 | tf_op jit(solution)/shard_map/pack_filters/pallas_call | solution.py:205
  15.3 6.6 %all-to-all-start.1 = ((bf16[16,2,256,128]{3,2,1,0:T(8,128)(2,1)}), bf16[16,2,256,128]{3,2,1,0:T(8,128)(2,1)S(1)}, u32[]{:S(2)}, u32[]{:S(2)}) async-start(bf16[16,2,256,128]{3,2,1,0:T(8,128)(2,1)} %pack_filters.1), calls=%async_computation.1 | async-start | bytes 4194304 | tf_op jit(solution)/shard_map/all_to_all | solution.py:306
  21.9 4.0 pack_signal.3
  25.8 65.9 %all-to-all-done.1.filter_ref = bf16[16,2,256,128]{3,2,1,0:T(8,128)(2,1)S(1)} async-done(((bf16[16,2,256,128]{3,2,1,0:T(8,128)(2,1)}), bf16[16,2,256,128]{3,2,1,0:T(8,128)(2,1)S(1)}, u32[]{:S(2)}, u32[]{:S(2)}) %all-to-all-start.1) | async-done | bytes 2097184 | tf_op jit(solution)/shard_map/all_to_all | solution.py:306
  91.7 0.0 copy-start.4
  91.7 8.0 %all-to-all-start.3 = ((bf16[16,512,128]{2,1,0:T(8,128)(2,1)}), bf16[16,512,128]{2,1,0:T(8,128)(2,1)}, u32[]{:S(2)}, u32[]{:S(2)}) async-start(bf16[16,512,128]{2,1,0:T(8,128)(2,1)} %pack_signal.3), calls=%async_computation.3 | async-start | bytes 4194304 | tf_op jit(solution)/shard_map/all_to_all | solution.py:305
  99.7 3.9 pack_signal.2
  103.6 0.0 copy-done.4
  103.6 66.0 %all-to-all-done.3.x_ref = bf16[16,512,128]{2,1,0:T(8,128)(2,1)} async-done(((bf16[16,512,128]{2,1,0:T(8,128)(2,1)}), bf16[16,512,128]{2,1,0:T(8,128)(2,1)}, u32[]{:S(2)}, u32[]{:S(2)}) %all-to-all-start.3) | async-done | bytes 2097184 | tf_op jit(solution)/shard_map/all_to_all | solution.py:305
  169.7 8.1 %all-to-all-start = ((bf16[16,512,128]{2,1,0:T(8,128)(2,1)}), bf16[16,512,128]{2,1,0:T(8,128)(2,1)}, u32[]{:S(2)}, u32[]{:S(2)}) async-start(bf16[16,512,128]{2,1,0:T(8,128)(2,1)} %pack_signal.2), calls=%async_computation | async-start | bytes 4194304 | tf_op jit(solution)/shard_map/all_to_all | solution.py:305
  177.8 0.1 add.119
  177.9 0.0 copy-done
  177.9 0.6 gather_fusion
  178.5 0.1 select_multiply_fusion
  178.6 0.1 add.116
  178.6 0.1 add.117
  178.8 0.1 fusion.22
  178.9 0.1 copy.7.twist_ref
  179.1 2.5 fusion.15
  181.6 0.1 maximum_maximum_fusion.ahead_ref
  181.7 2.3 negate_convert_fusion
  184.0 0.1 maximum_maximum_fusion.1.back_ref
  184.1 20.5 %convolve.3 = bf16[16,512,128]{2,1,0:T(8,128)(2,1)S(1)} custom-call(f32[512,32]{1,0:T(8,128)S(1)} %copy.7.twist_ref, bf16[2,256,1024]{2,1,0:T(8,128)(2,1)S(1)} %maximum_maximum_fusion.ahead_ref, bf16[2,1024,256]{2,1,0:T(8,128)(2,1)S(1)} %maximum_maximum_fusion.1.back_ref, bf16[16,512,128]{2,1,0:T(8,128)(2,1)} %all-to-all-done.3.x_ref, ...), custom_call_target="tpu_custom_call" | custom-call | flops 2147483648 | bytes 16777216 | tf_op jit(solution)/shard_map/convolve/pallas_call | solution.py:147
  204.6 0.0 copy-start.2
  204.7 1.3 copy-done.2
  206.0 41.7 %all-to-all-done.x_ref = bf16[16,512,128]{2,1,0:T(8,128)(2,1)} async-done(((bf16[16,512,128]{2,1,0:T(8,128)(2,1)}), bf16[16,512,128]{2,1,0:T(8,128)(2,1)}, u32[]{:S(2)}, u32[]{:S(2)}) %all-to-all-start) | async-done | bytes 2097184 | tf_op jit(solution)/shard_map/all_to_all | solution.py:305
  247.7 8.1 %all-to-all-start.4 = ((bf16[16,512,128]{2,1,0:T(8,128)(2,1)}), bf16[16,512,128]{2,1,0:T(8,128)(2,1)}, u32[]{:S(2)}, u32[]{:S(2)}) async-start(bf16[16,512,128]{2,1,0:T(8,128)(2,1)} %copy-done.2), calls=%async_computation.4 | async-start | bytes 4194304 | tf_op jit(solution)/shard_map/all_to_all | solution.py:331
  255.8 20.6 %convolve.2 = bf16[16,512,128]{2,1,0:T(8,128)(2,1)S(1)} custom-call(f32[512,32]{1,0:T(8,128)S(1)} %copy.7.twist_ref, bf16[2,256,1024]{2,1,0:T(8,128)(2,1)S(1)} %maximum_maximum_fusion.ahead_ref, bf16[2,1024,256]{2,1,0:T(8,128)(2,1)S(1)} %maximum_maximum_fusion.1.back_ref, bf16[16,512,128]{2,1,0:T(8,128)(2,1)} %all-to-all-done.x_ref, ...), custom_call_target="tpu_custom_call" | custom-call | flops 2147483648 | bytes 16777216 | tf_op jit(solution)/shard_map/convolve/pallas_call | solution.py:147
  276.4 0.0 copy-start.1
  276.4 1.3 copy-done.1
  277.8 0.0 copy-start.3
  277.8 47.9 %all-to-all-done.4.c_ref = bf16[16,512,128]{2,1,0:T(8,128)(2,1)} async-done(((bf16[16,512,128]{2,1,0:T(8,128)(2,1)}), bf16[16,512,128]{2,1,0:T(8,128)(2,1)}, u32[]{:S(2)}, u32[]{:S(2)}) %all-to-all-start.4) | async-done | bytes 2097184 | tf_op jit(solution)/shard_map/all_to_all | solution.py:331
  325.7 7.4 %all-to-all-start.2 = ((bf16[16,512,128]{2,1,0:T(8,128)(2,1)}), bf16[16,512,128]{2,1,0:T(8,128)(2,1)S(1)}, u32[]{:S(2)}, u32[]{:S(2)}) async-start(bf16[16,512,128]{2,1,0:T(8,128)(2,1)} %copy-done.1), calls=%async_computation.2 | async-start | bytes 4194304 | tf_op jit(solution)/shard_map/all_to_all | solution.py:331
  333.2 0.0 copy-done.3
  333.2 5.3 gate.3.refs_2_
  338.5 1.2 collective-permute-start.1
  339.7 63.3 %all-to-all-done.2.c_ref = bf16[16,512,128]{2,1,0:T(8,128)(2,1)S(1)} async-done(((bf16[16,512,128]{2,1,0:T(8,128)(2,1)}), bf16[16,512,128]{2,1,0:T(8,128)(2,1)S(1)}, u32[]{:S(2)}, u32[]{:S(2)}) %all-to-all-start.2) | async-done | bytes 2097184 | tf_op jit(solution)/shard_map/all_to_all | solution.py:331
  403.0 4.7 gate.2.refs_0_
  407.6 1.2 collective-permute-start
  408.9 0.1 pad_add_fusion.start_ref
  408.9 0.0 collective-permute-done.1.refs_3_
  408.9 45.2 %collective-permute-done.refs_1_ = bf16[512,2048]{1,0:T(8,128)(2,1)S(1)} collective-permute-done((bf16[512,2048]{1,0:T(8,128)(2,1)}, bf16[512,2048]{1,0:T(8,128)(2,1)S(1)}, u32[]{:S(2)}, u32[]{:S(2)}) %collective-permute-start) | collective-permute-done | bytes 2097184 | tf_op jit(solution)/shard_map/ppermute | solution.py:337
  454.2 107.3 %all-gather.2.cloned.1.call-done.refs_4_ = bf16[8192,4096]{1,0:T(8,128)(2,1)} async-done(((bf16[512,4096]{1,0:T(8,128)(2,1)}), bf16[8192,4096]{1,0:T(8,128)(2,1)}) %all-gather.2.cloned.1.call-update) | async-done | bytes 67108880 | tf_op jit(solution)/shard_map/all_gather | solution.py:300
  561.4 42.9 %mix.1 = bf16[512,4096]{1,0:T(8,128)(2,1)} custom-call(s32[4]{0:T(128)S(1)} %pad_add_fusion.start_ref, bf16[512,2048]{1,0:T(8,128)(2,1)} %gate.2.refs_0_, bf16[512,2048]{1,0:T(8,128)(2,1)S(1)} %collective-permute-done.refs_1_, bf16[512,2048]{1,0:T(8,128)(2,1)} %gate.3.refs_2_, bf16[512,2048]{1,0:T(8,128)(2,1)} %collective-permute-done.1.refs_3_, ...), custom_call_target="tpu_custom_call" | custom-call | flops 34359738368 | bytes 67108864 | tf_op jit(solution)/shard_map/mix/pallas_call | solution.py:269
  (6 shorter events, 0.1 us)
Async XLA Ops:
  6.5 171.4 %copy-start = (s32[32,32]{1,0:T(8,128)S(1)}, s32[32,32]{1,0:T(8,128)}, u32[]{:S(2)}) copy-start(s32[32,32]{1,0:T(8,128)} %param.10) | copy-start | bytes 12292
  6.5 554.9 %all-gather.2.cloned.1.call-start = ((), (), s32[]{:S(2)}) async-start(), calls=%async_computation.5 | async-start | bytes 71303168 | tf_op jit(solution)/shard_map/all_gather | solution.py:300
  15.3 76.4 %all-to-all-start.1 = ((bf16[16,2,256,128]{3,2,1,0:T(8,128)(2,1)}), bf16[16,2,256,128]{3,2,1,0:T(8,128)(2,1)S(1)}, u32[]{:S(2)}, u32[]{:S(2)}) async-start(bf16[16,2,256,128]{3,2,1,0:T(8,128)(2,1)} %pack_filters.1), calls=%async_computation.1 | async-start | bytes 4194304 | tf_op jit(solution)/shard_map/all_to_all | solution.py:306
  91.7 11.9 %copy-start.4 = (bf16[16,2,256,128]{3,2,1,0:T(8,128)(2,1)}, bf16[16,2,256,128]{3,2,1,0:T(8,128)(2,1)S(1)}, u32[]{:S(2)}) copy-start(bf16[16,2,256,128]{3,2,1,0:T(8,128)(2,1)S(1)} %all-to-all-done.1.filter_ref) | copy-start | bytes 6291460
  91.7 77.9 %all-to-all-start.3 = ((bf16[16,512,128]{2,1,0:T(8,128)(2,1)}), bf16[16,512,128]{2,1,0:T(8,128)(2,1)}, u32[]{:S(2)}, u32[]{:S(2)}) async-start(bf16[16,512,128]{2,1,0:T(8,128)(2,1)} %pack_signal.3), calls=%async_computation.3 | async-start | bytes 4194304 | tf_op jit(solution)/shard_map/all_to_all | solution.py:305
  169.7 78.0 %all-to-all-start = ((bf16[16,512,128]{2,1,0:T(8,128)(2,1)}), bf16[16,512,128]{2,1,0:T(8,128)(2,1)}, u32[]{:S(2)}, u32[]{:S(2)}) async-start(bf16[16,512,128]{2,1,0:T(8,128)(2,1)} %pack_signal.2), calls=%async_computation | async-start | bytes 4194304 | tf_op jit(solution)/shard_map/all_to_all | solution.py:305
  204.6 1.3 copy-start.2
  247.7 78.0 %all-to-all-start.4 = ((bf16[16,512,128]{2,1,0:T(8,128)(2,1)}), bf16[16,512,128]{2,1,0:T(8,128)(2,1)}, u32[]{:S(2)}, u32[]{:S(2)}) async-start(bf16[16,512,128]{2,1,0:T(8,128)(2,1)} %copy-done.2), calls=%async_computation.4 | async-start | bytes 4194304 | tf_op jit(solution)/shard_map/all_to_all | solution.py:331
  276.4 1.3 copy-start.1
  277.8 55.4 %copy-start.3 = (f32[4096]{0:T(1024)S(1)}, f32[4096]{0:T(1024)}, u32[]{:S(2)}) copy-start(f32[4096]{0:T(1024)} %param.8) | copy-start | bytes 49156
  325.7 77.3 %all-to-all-start.2 = ((bf16[16,512,128]{2,1,0:T(8,128)(2,1)}), bf16[16,512,128]{2,1,0:T(8,128)(2,1)S(1)}, u32[]{:S(2)}, u32[]{:S(2)}) async-start(bf16[16,512,128]{2,1,0:T(8,128)(2,1)} %copy-done.1), calls=%async_computation.2 | async-start | bytes 4194304 | tf_op jit(solution)/shard_map/all_to_all | solution.py:331
  338.5 70.5 %collective-permute-start.1 = (bf16[512,2048]{1,0:T(8,128)(2,1)}, bf16[512,2048]{1,0:T(8,128)(2,1)}, u32[]{:S(2)}, u32[]{:S(2)}) collective-permute-start(bf16[512,2048]{1,0:T(8,128)(2,1)} %gate.3.refs_2_), channel_id=1, source_target_pairs={{0,1},{1,0},{2,3},{3,2},{4,5},{5,4},{6,7},{7,6},{8,9},{9,8},{10,11... | collective-permute-start | bytes 6291464 | tf_op jit(solution)/shard_map/ppermute | solution.py:337
  407.6 46.5 %collective-permute-start = (bf16[512,2048]{1,0:T(8,128)(2,1)}, bf16[512,2048]{1,0:T(8,128)(2,1)S(1)}, u32[]{:S(2)}, u32[]{:S(2)}) collective-permute-start(bf16[512,2048]{1,0:T(8,128)(2,1)} %gate.2.refs_0_), channel_id=1, source_target_pairs={{0,1},{1,0},{2,3},{3,2},{4,5},{5,4},{6,7},{7,6},{8,9},{9,8},{10,11... | collective-permute-start | bytes 6291464 | tf_op jit(solution)/shard_map/ppermute | solution.py:337
Sparse Core Ops, SparseCore 0:
  9.0 552.4 all-gather.1

commit v2 on v1

--- a/solution.py
+++ b/solution.py
@@ -248,40 +248,52 @@
     )(convolved, keyval, gating, skip_gain.reshape(1, -1))
 
 
-def mix_kernel(pieces, start_ref, *refs):
-    w_ref, out_ref = refs[pieces], refs[pieces + 1]
-    total = None
+def mix_kernel(shape, *refs):
+    pieces, peers, halves = shape
+    place_ref, refs = refs[0], refs[1:]
+    h_refs, w_refs, out_refs = refs[: pieces * peers], refs[pieces * peers :][:halves], refs[-peers:]
+    depth = w_refs[0].shape[2]
+    per = h_refs[0].shape[1] // (halves * depth)
+    totals = [None] * peers
     for k in range(pieces):
-        depth = refs[k].shape[1]
-        start = pl.multiple_of(start_ref[k], depth)
-        part = jnp.dot(
-            refs[k][...], w_ref[pl.ds(start, depth), :], preferred_element_type=F32
-        )
-        total = part if total is None else total + part
-    out_ref[...] = total.astype(BF16)
-
-
-def mix(hidden, starts, weight):
-    tokens = hidden[0].shape[0]
-    depth, columns = weight.shape
+        for j in range(per):
+            line = place_ref[2 + 2 * (k * per + j)]
+            turn = place_ref[3 + 2 * (k * per + j)]
+            for core in range(halves):
+                at = j * halves + lax.rem(place_ref[0] + core, halves)
+                lanes = pl.ds(pl.multiple_of(at * depth, depth), depth)
+                w = w_refs[core][line, turn]
+                for m in range(peers):
+                    part = jnp.dot(
+                        h_refs[k * peers + m][:, lanes], w, preferred_element_type=F32
+                    )
+                    totals[m] = part if totals[m] is None else totals[m] + part
+    for m in range(peers):
+        out_refs[m][...] = totals[m].astype(BF16)
+
+
+def mix(hidden, weights, places):
+    pieces, peers, halves = len(hidden), len(hidden[0]), len(weights)
+    tokens = hidden[0][0].shape[0]
+    line, turns, depth, columns = weights[0].shape
     tile = min(256, columns)
-    pieces = len(hidden)
+    flat = [h for piece in hidden for h in piece]
     return pl.pallas_call(
-        functools.partial(mix_kernel, pieces),
+        functools.partial(mix_kernel, (pieces, peers, halves)),
         grid=(columns // tile,),
-        out_shape=jax.ShapeDtypeStruct((tokens, columns), BF16),
+        out_shape=[jax.ShapeDtypeStruct((tokens, columns), BF16)] * peers,
         in_specs=[pl.BlockSpec(memory_space=pltpu.SMEM)]
-        + [pl.BlockSpec(h.shape, lambda i: (0, 0)) for h in hidden]
-        + [pl.BlockSpec((depth, tile), lambda i: (0, i))],
-        out_specs=pl.BlockSpec((tokens, tile), lambda i: (0, i)),
+        + [pl.BlockSpec(h.shape, lambda i: (0, 0)) for h in flat]
+        + [pl.BlockSpec((line, turns, depth, tile), lambda i: (0, 0, 0, i))] * halves,
+        out_specs=[pl.BlockSpec((tokens, tile), lambda i: (0, i))] * peers,
         compiler_params=pltpu.CompilerParams(vmem_limit_bytes=VMEM),
         cost_estimate=pl.CostEstimate(
-            flops=2 * tokens * depth * columns,
-            bytes_accessed=2 * depth * columns,
+            flops=2 * tokens * peers * halves * line * turns * depth * columns,
+            bytes_accessed=2 * halves * line * turns * depth * columns,
             transcendentals=0,
         ),
         name="mix",
-    )(starts, *hidden, weight)
+    )(places, *flat, *weights)
 
 
 def body(keyval, gating, skip_gain, filter_values, blocks, out_weight):
@@ -297,7 +309,45 @@
     unit = min(narrow, group_width)
     chunks = narrow // unit
 
-    weight = lax.all_gather(out_weight, "seq", axis=0, tiled=True)
+    cores = 2 if cycle % 2 == 0 else 1
+    line = math.gcd(cycle // cores, 4)
+    turns = cycle // (cores * line)
+    core, turn = place % cores, place // cores % turns
+
+    def index(i, m, c):
+        return (i % line * turns + m % turns) * cores + c % cores
+
+    def move(value, by_turn, by_core):
+        pairs = [
+            (index(i, m, c), index(i, m + by_turn, c + by_core))
+            for i in range(line)
+            for m in range(turns)
+            for c in range(cores)
+        ]
+        return lax.ppermute(value, "seq", pairs)
+
+    rows, columns = out_weight.shape[0], out_weight.shape[1] // turns
+    shares = []
+    for m in range(turns):
+        target = (turn + m) % turns
+        share = lax.dynamic_slice_in_dim(out_weight, target * columns, columns, axis=1)
+        shares.append(move(share, m, 0) if m else share)
+    stacked = jnp.concatenate(shares, axis=0)
+    lines = [
+        [index(i, m, c) for i in range(line)] for m in range(turns) for c in range(cores)
+    ]
+    bounds = [0, columns * 3 // 4, columns] if columns % 1024 == 0 else [0, columns]
+    weights = []
+    for low, high in zip(bounds[:-1], bounds[1:]):
+        lined = lax.all_gather(
+            stacked[:, low:high], "seq", axis=0, tiled=True, axis_index_groups=lines
+        )
+        weights.append(
+            [
+                (move(lined, 0, c) if c else lined).reshape(line, turns, rows, high - low)
+                for c in range(cores)
+            ]
+        )
 
     exchange = functools.partial(
         lax.all_to_all, axis_name="seq", split_axis=0, concat_axis=0, tiled=True
@@ -326,21 +376,31 @@
         tables(local_index[:, None], cycle_index[None, :], cycle * tokens), axis=1
     )
 
-    hidden, starts = [], []
+    hidden, places = [], [core, jnp.zeros_like(core)]
+    width = cycle * unit
     for g in range(chunks):
         done = exchange(convolve(g, twist, ahead, back, signals[g], filters))
         own = gate(done, keyval, gating, skip_gain, g)
         for shift in range(peers):
-            if shift == 0:
-                piece = own
-            else:
+            piece = own
+            if shift:
                 piece = lax.ppermute(
                     own, "tensor", [(t, (t + shift) % peers) for t in range(peers)]
                 )
-            hidden.append(piece)
-            source = lax.rem(side + peers - shift, peers)
-            starts.append(source * channels + g * cycle * unit)
-    return mix(hidden, jnp.stack(starts).astype(jnp.int32), weight)
+            hidden.append([move(piece, m, 0) if m else piece for m in range(turns)])
+            start = (side + peers - shift) % peers * channels + g * width
+            for j in range(width // (cores * rows)):
+                at = start // rows + j * cores
+                places += [at // (cores * turns), (turn + turns - at // cores % turns) % turns]
+    places = jnp.stack(places).astype(jnp.int32)
+
+    result = jnp.zeros((tokens, columns * turns), BF16)
+    for low, weight in zip(bounds[:-1], weights):
+        for m, part in enumerate(mix(hidden, weight, places)):
+            part = move(part, -m, 0) if m else part
+            source = (turn + m) % turns
+            result = lax.dynamic_update_slice(result, part, (0, source * columns + low))
+    return result
 
 
 def solution(mesh):

time: 612 us -> 871 us (1.42)
  waiting for transfers between devices: 438 us -> 656 us
  starting transfers between devices: 40.7 us -> 57.9 us
  local copies, waits for them, and re-layouts: 3.64 us -> 13.9 us
    ppermute x0 -> x9, waiting for transfers between devices: none -> 205 us  [move(): return lax.ppermute(value, 'seq', pairs)]
    all_to_all x1, waiting for transfers between devices: 65.9 us -> 95.3 us  [body(): filters = exchange(pack_filters(filter_values, cycle, chunks, unit))]
    ppermute x0 -> x9, starting transfers between devices: none -> 17.8 us  [move(): return lax.ppermute(value, 'seq', pairs)]
    all_to_all x2, waiting for transfers between devices: 108 us -> 97.4 us  [body(): exchange(pack_signal(keyval, g, cycle, unit))]
    pallas_call x1 -> x2, Pallas kernels: 42.9 us -> 50.1 us  [mix(): pl.pallas_call(functools.partial(mix_kernel, (pieces, peers, halves)), gr...]
    all_gather x1 -> x2, waiting for transfers between devices: 107 us -> 112 us  [body(): lax.all_gather(stacked[:, low:high], 'seq', axis=0, tiled=True, axis_inde...]
  transfers between devices with their start and end apart: 8 -> 18, of which waited for: 7 -> 13; matrix products, arithmetic and copies ran while one was open for 1% -> 1% of each run, Pallas kernels for 11% -> 13%
where the time goes in v2:
time: 871 us; the launch traced here: 870 us
  waiting for transfers between devices  656 us (75%)
  Pallas kernels  117 us (13%)
  starting transfers between devices  57.9 us (7%)
  between operations  14 us (2%)
  local copies, waits for them, and re-layouts  13.9 us (2%)
  other arithmetic  10.7 us (1%)
    ppermute x9, waiting for transfers between devices, move(): return lax.ppermute(value, 'seq', pairs)  205 us
    all_gather x2, waiting for transfers between devices, body(): lax.all_gather(stacked[:, low:high], 'seq', axis=0, tiled=True, axis_inde...  112 us
    all_to_all x2, waiting for transfers between devices, body(): done = exchange(convolve(g, twist, ahead, back, signals[g], filters))  107 us
    all_to_all x2, waiting for transfers between devices, body(): exchange(pack_signal(keyval, g, cycle, unit))  97.4 us
    all_to_all x1, waiting for transfers between devices, body(): filters = exchange(pack_filters(filter_values, cycle, chunks, unit))  95.3 us
    pallas_call x2, Pallas kernels, mix(): pl.pallas_call(functools.partial(mix_kernel, (pieces, peers, halves)), gr...  50.1 us
    pallas_call x2, Pallas kernels, convolve(): pl.pallas_call(conv_kernel, grid=(1,), out_shape=jax.ShapeDtypeStruct(sig...  41.1 us
    ppermute x2, waiting for transfers between devices, body(): lax.ppermute(own, 'tensor', [(t, (t + shift) % peers) for t in range(peer...  38.5 us
  transfers between devices with their start and end apart: 18, of which 13 were waited for; matrix products, arithmetic and copies ran while one was open for 1% of the time, Pallas kernels for 13%

profile of v2, /device:TPU:9, one launch (start us, length us, event | category | flops | bytes accessed | tf_op | source)
XLA Modules:
  0.0 869.8 jit_solution(18434322910711271855)
XLA Ops:
  6.5 4.1 constant_dynamic-slice_fusion
  10.7 1.2 collective-permute-start.6
  11.9 45.4 %collective-permute-done.6 = bf16[512,2048]{1,0:T(8,128)(2,1)} collective-permute-done((bf16[512,2048]{1,0:T(8,128)(2,1)S(1)}, bf16[512,2048]{1,0:T(8,128)(2,1)}, u32[]{:S(2)}, u32[]{:S(2)}) %collective-permute-start.6) | collective-permute-done | bytes 2097184 | tf_op jit(solution)/shard_map/ppermute | solution.py:327
  57.3 3.1 fusion
  60.5 8.0 pack_filters.1
  68.5 7.5 all-to-all-start.1
  75.9 4.0 pack_signal.2
  80.0 95.3 %all-to-all-done.1.filter_ref = bf16[16,2,256,128]{3,2,1,0:T(8,128)(2,1)S(1)} async-done(((bf16[16,2,256,128]{3,2,1,0:T(8,128)(2,1)}), bf16[16,2,256,128]{3,2,1,0:T(8,128)(2,1)S(1)}, u32[]{:S(2)}, u32[]{:S(2)}) %all-to-all-start.1) | async-done | bytes 2097184 | tf_op jit(solution)/shard_map/all_to_all | solution.py:356
  175.3 1.3 copy-done.7
  176.6 7.4 all-to-all-start
  184.0 3.9 pack_signal.3
  187.9 97.4 %all-to-all-done.x_ref = bf16[16,512,128]{2,1,0:T(8,128)(2,1)} async-done(((bf16[16,512,128]{2,1,0:T(8,128)(2,1)}), bf16[16,512,128]{2,1,0:T(8,128)(2,1)}, u32[]{:S(2)}, u32[]{:S(2)}) %all-to-all-start) | async-done | bytes 2097184 | tf_op jit(solution)/shard_map/all_to_all | solution.py:355
  285.3 7.7 all-to-all-start.3
  293.0 0.6 gather_fusion
  294.1 2.5 fusion.16
  296.6 2.3 negate_convert_fusion
  298.9 112.5 %all-gather.3.cloned.1.call-done = bf16[4096,1536]{1,0:T(8,128)(2,1)} async-done(((bf16[1024,1536]{1,0:T(8,128)(2,1)}), bf16[4096,1536]{1,0:T(8,128)(2,1)}) %all-gather.3.cloned.1.call-update) | async-done | bytes 12582928 | tf_op jit(solution)/shard_map/all_gather | solution.py:342
  411.3 0.4 collective-permute-start.7
  412.2 20.5 %convolve.2 = bf16[16,512,128]{2,1,0:T(8,128)(2,1)S(1)} custom-call(f32[512,32]{1,0:T(8,128)S(1)} %copy.7.twist_ref, bf16[2,256,1024]{2,1,0:T(8,128)(2,1)S(1)} %maximum_maximum_fusion.ahead_ref, bf16[2,1024,256]{2,1,0:T(8,128)(2,1)S(1)} %maximum_maximum_fusion.1.back_ref, bf16[16,512,128]{2,1,0:T(8,128)(2,1)} %all-to-all-done.x_ref, ...), custom_call_target="tpu_custom_call" | custom-call | flops 2147483648 | bytes 16777216 | tf_op jit(solution)/shard_map/convolve/pallas_call | solution.py:147
  432.8 1.3 copy-done.3
  434.1 8.6 all-to-all-start.2
  442.7 20.5 %convolve.3 = bf16[16,512,128]{2,1,0:T(8,128)(2,1)S(1)} custom-call(f32[512,32]{1,0:T(8,128)S(1)} %copy.7.twist_ref, bf16[2,256,1024]{2,1,0:T(8,128)(2,1)S(1)} %maximum_maximum_fusion.ahead_ref, bf16[2,1024,256]{2,1,0:T(8,128)(2,1)S(1)} %maximum_maximum_fusion.1.back_ref, bf16[16,512,128]{2,1,0:T(8,128)(2,1)} %all-to-all-done.3.x_ref, ...), custom_call_target="tpu_custom_call" | custom-call | flops 2147483648 | bytes 16777216 | tf_op jit(solution)/shard_map/convolve/pallas_call | solution.py:147
  463.3 1.3 copy-done.2
  464.6 24.3 %all-to-all-done.2.c_ref = bf16[16,512,128]{2,1,0:T(8,128)(2,1)} async-done(((bf16[16,512,128]{2,1,0:T(8,128)(2,1)}), bf16[16,512,128]{2,1,0:T(8,128)(2,1)}, u32[]{:S(2)}, u32[]{:S(2)}) %all-to-all-start.2) | async-done | bytes 2097184 | tf_op jit(solution)/shard_map/all_to_all | solution.py:382
  488.8 6.3 all-to-all-start.4
  495.4 2.3 pad_maximum_fusion
  497.7 5.0 gate.2.refs_1_
  502.7 1.2 collective-permute-start.1
  503.9 83.2 %all-to-all-done.4.c_ref = bf16[16,512,128]{2,1,0:T(8,128)(2,1)S(1)} async-done(((bf16[16,512,128]{2,1,0:T(8,128)(2,1)}), bf16[16,512,128]{2,1,0:T(8,128)(2,1)S(1)}, u32[]{:S(2)}, u32[]{:S(2)}) %all-to-all-start.4) | async-done | bytes 2097184 | tf_op jit(solution)/shard_map/all_to_all | solution.py:382
  587.1 4.7 gate.3.refs_5_
  591.8 1.2 collective-permute-start.4
  593.0 6.5 collective-permute-start
  599.5 1.4 collective-permute-start.2
  601.0 38.5 %collective-permute-done.4.refs_7_ = bf16[512,2048]{1,0:T(8,128)(2,1)} collective-permute-done((bf16[512,2048]{1,0:T(8,128)(2,1)}, bf16[512,2048]{1,0:T(8,128)(2,1)}, u32[]{:S(2)}, u32[]{:S(2)}) %collective-permute-start.4) | collective-permute-done | bytes 2097184 | tf_op jit(solution)/shard_map/ppermute | solution.py:387
  639.5 6.2 collective-permute-start.5
  645.6 0.3 collective-permute-done.refs_2_
  646.4 44.4 %collective-permute-done.3.refs_6_ = bf16[512,2048]{1,0:T(8,128)(2,1)} collective-permute-done((bf16[512,2048]{1,0:T(8,128)(2,1)}, bf16[512,2048]{1,0:T(8,128)(2,1)}, u32[]{:S(2)}, u32[]{:S(2)}) %collective-permute-start.3) | collective-permute-done | bytes 2097184 | tf_op jit(solution)/shard_map/ppermute | solution.py:327
  690.9 44.9 %collective-permute-done.2.refs_4_ = bf16[512,2048]{1,0:T(8,128)(2,1)} collective-permute-done((bf16[512,2048]{1,0:T(8,128)(2,1)}, bf16[512,2048]{1,0:T(8,128)(2,1)}, u32[]{:S(2)}, u32[]{:S(2)}) %collective-permute-start.2) | collective-permute-done | bytes 2097184 | tf_op jit(solution)/shard_map/ppermute | solution.py:327
  735.8 44.2 %collective-permute-done.5.refs_8_ = bf16[512,2048]{1,0:T(8,128)(2,1)} collective-permute-done((bf16[512,2048]{1,0:T(8,128)(2,1)}, bf16[512,2048]{1,0:T(8,128)(2,1)}, u32[]{:S(2)}, u32[]{:S(2)}) %collective-permute-start.5) | collective-permute-done | bytes 2097184 | tf_op jit(solution)/shard_map/ppermute | solution.py:327
  780.0 34.5 %mix.2 = (bf16[512,1536]{1,0:T(8,128)(2,1)S(1)}, bf16[512,1536]{1,0:T(8,128)(2,1)S(1)}) custom-call(s32[18]{0:T(128)S(1)} %stack.71.refs_0_, bf16[512,2048]{1,0:T(8,128)(2,1)} %gate.2.refs_1_, bf16[512,2048]{1,0:T(8,128)(2,1)} %copy-done.5, bf16[512,2048]{1,0:T(8,128)(2,1)} %collective-permute-done.1.refs_3_, ...), custom_call_target="tpu_custom_call" | custom-call | flops 25769803776 | bytes 25165824 | tf_op jit(solution)/shard_map/mix/pallas_call | solution.py:281
  814.5 1.9 collective-permute-start.8
  816.4 1.6 copy-done.6
  818.0 15.6 %mix.3 = (bf16[512,512]{1,0:T(8,128)(2,1)S(1)}, bf16[512,512]{1,0:T(8,128)(2,1)S(1)}) custom-call(s32[18]{0:T(128)S(1)} %stack.71.refs_0_, bf16[512,2048]{1,0:T(8,128)(2,1)} %gate.2.refs_1_, bf16[512,2048]{1,0:T(8,128)(2,1)S(1)} %copy-done.6, bf16[512,2048]{1,0:T(8,128)(2,1)} %collective-permute-done.1.refs_3_, ...), custom_call_target="tpu_custom_call" | custom-call | flops 8589934592 | bytes 8388608 | tf_op jit(solution)/shard_map/mix/pallas_call | solution.py:281
  833.7 0.5 broadcast_in_dim.12
  834.4 16.6 %collective-permute-done.8 = bf16[512,1536]{1,0:T(8,128)(2,1)} collective-permute-done((bf16[512,1536]{1,0:T(8,128)(2,1)S(1)}, bf16[512,1536]{1,0:T(8,128)(2,1)}, u32[]{:S(2)}, u32[]{:S(2)}) %collective-permute-start.8) | collective-permute-done | bytes 1572896 | tf_op jit(solution)/shard_map/ppermute | solution.py:327
  851.0 1.6 constant_dynamic-update-slice_fusion.2
  852.6 9.4 %collective-permute-done.10 = bf16[512,512]{1,0:T(8,128)(2,1)S(1)} collective-permute-done((bf16[512,512]{1,0:T(8,128)(2,1)S(1)}, bf16[512,512]{1,0:T(8,128)(2,1)S(1)}, u32[]{:S(2)}, u32[]{:S(2)}) %collective-permute-start.10) | collective-permute-done | bytes 524320 | tf_op jit(solution)/shard_map/ppermute | solution.py:327
  862.1 0.8 constant_dynamic-update-slice_fusion
  (43 shorter events, 1.8 us)
Async XLA Ops:
  6.5 286.5 %copy-start = (s32[32,32]{1,0:T(8,128)S(1)}, s32[32,32]{1,0:T(8,128)}, u32[]{:S(2)}) copy-start(s32[32,32]{1,0:T(8,128)} %param.10) | copy-start | bytes 12292
  6.5 404.8 %all-gather.3.cloned.1.call-start = ((), (), s32[]{:S(2)}) async-start(), calls=%async_computation.5 | async-start | bytes 15728640 | tf_op jit(solution)/shard_map/all_gather | solution.py:342
  10.7 46.6 %collective-permute-start.6 = (bf16[512,2048]{1,0:T(8,128)(2,1)S(1)}, bf16[512,2048]{1,0:T(8,128)(2,1)}, u32[]{:S(2)}, u32[]{:S(2)}) collective-permute-start(bf16[512,2048]{1,0:T(8,128)(2,1)S(1)} %get-tuple-element.13), channel_id=1, source_target_pairs={{0,4},{2,6},{4,0},{6,2},{8,12},{10,14},{12,8},{14,10},{16,20},{18,... | collective-permute-start | bytes 6291464 | tf_op jit(solution)/shard_map/ppermute | solution.py:327
  68.5 106.8 %all-to-all-start.1 = ((bf16[16,2,256,128]{3,2,1,0:T(8,128)(2,1)}), bf16[16,2,256,128]{3,2,1,0:T(8,128)(2,1)S(1)}, u32[]{:S(2)}, u32[]{:S(2)}) async-start(bf16[16,2,256,128]{3,2,1,0:T(8,128)(2,1)} %pack_filters.1), calls=%async_computation.1 | async-start | bytes 4194304 | tf_op jit(solution)/shard_map/all_to_all | solution.py:356
  175.3 1.3 copy-start.7
  176.6 108.7 %all-to-all-start = ((bf16[16,512,128]{2,1,0:T(8,128)(2,1)}), bf16[16,512,128]{2,1,0:T(8,128)(2,1)}, u32[]{:S(2)}, u32[]{:S(2)}) async-start(bf16[16,512,128]{2,1,0:T(8,128)(2,1)} %pack_signal.2), calls=%async_computation | async-start | bytes 4194304 | tf_op jit(solution)/shard_map/all_to_all | solution.py:355
  285.3 148.8 %all-to-all-start.3 = ((bf16[16,512,128]{2,1,0:T(8,128)(2,1)}), bf16[16,512,128]{2,1,0:T(8,128)(2,1)}, u32[]{:S(2)}, u32[]{:S(2)}) async-start(bf16[16,512,128]{2,1,0:T(8,128)(2,1)} %pack_signal.3), calls=%async_computation.3 | async-start | bytes 4194304 | tf_op jit(solution)/shard_map/all_to_all | solution.py:355
  411.3 368.7 %collective-permute-start.7 = (bf16[4096,1536]{1,0:T(8,128)(2,1)}, bf16[4096,1536]{1,0:T(8,128)(2,1)}, u32[]{:S(2)}, u32[]{:S(2)}) collective-permute-start(bf16[4096,1536]{1,0:T(8,128)(2,1)} %all-gather.3.cloned.1.call-done), channel_id=1, source_target_pairs={{0,2},{2,0},{4,6},{6,4},{8,10},{10,8},{12,14},{14,12},{16,18},{18,... | collective-permute-start | bytes 37748744 | tf_op jit(solution)/shard_map/ppermute | solution.py:327
  432.7 1.3 copy-start.3
  434.1 54.8 %all-to-all-start.2 = ((bf16[16,512,128]{2,1,0:T(8,128)(2,1)}), bf16[16,512,128]{2,1,0:T(8,128)(2,1)}, u32[]{:S(2)}, u32[]{:S(2)}) async-start(bf16[16,512,128]{2,1,0:T(8,128)(2,1)} %copy-done.3), calls=%async_computation.2 | async-start | bytes 4194304 | tf_op jit(solution)/shard_map/all_to_all | solution.py:382
  463.3 1.3 copy-start.2
  488.8 98.3 %all-to-all-start.4 = ((bf16[16,512,128]{2,1,0:T(8,128)(2,1)}), bf16[16,512,128]{2,1,0:T(8,128)(2,1)S(1)}, u32[]{:S(2)}, u32[]{:S(2)}) async-start(bf16[16,512,128]{2,1,0:T(8,128)(2,1)} %copy-done.2), calls=%async_computation.4 | async-start | bytes 4194304 | tf_op jit(solution)/shard_map/all_to_all | solution.py:382
  495.2 2.6 copy-start.4
  495.2 150.5 %all-gather.5.cloned.1.call-start = ((), (), s32[]{:S(2)}) async-start(), calls=%async_computation.6 | async-start | bytes 5242880 | tf_op jit(solution)/shard_map/all_gather | solution.py:342
  502.7 96.8 %collective-permute-start.1 = (bf16[512,2048]{1,0:T(8,128)(2,1)}, bf16[512,2048]{1,0:T(8,128)(2,1)}, u32[]{:S(2)}, u32[]{:S(2)}) collective-permute-start(bf16[512,2048]{1,0:T(8,128)(2,1)} %gate.2.refs_1_), channel_id=1, source_target_pairs={{0,1},{1,0},{2,3},{3,2},{4,5},{5,4},{6,7},{7,6},{8,9},{9,8},{10,11... | collective-permute-start | bytes 6291464 | tf_op jit(solution)/shard_map/ppermute | solution.py:387
  591.8 47.7 %collective-permute-start.4 = (bf16[512,2048]{1,0:T(8,128)(2,1)}, bf16[512,2048]{1,0:T(8,128)(2,1)}, u32[]{:S(2)}, u32[]{:S(2)}) collective-permute-start(bf16[512,2048]{1,0:T(8,128)(2,1)} %gate.3.refs_5_), channel_id=1, source_target_pairs={{0,1},{1,0},{2,3},{3,2},{4,5},{5,4},{6,7},{7,6},{8,9},{9,8},{10,11... | collective-permute-start | bytes 6291464 | tf_op jit(solution)/shard_map/ppermute | solution.py:387
  593.0 52.9 %collective-permute-start = (bf16[512,2048]{1,0:T(8,128)(2,1)}, bf16[512,2048]{1,0:T(8,128)(2,1)S(1)}, u32[]{:S(2)}, u32[]{:S(2)}) collective-permute-start(bf16[512,2048]{1,0:T(8,128)(2,1)} %gate.2.refs_1_), channel_id=1, source_target_pairs={{0,4},{2,6},{4,0},{6,2},{8,12},{10,14},{12,8},{14,10},{16,20},{18,... | collective-permute-start | bytes 6291464 | tf_op jit(solution)/shard_map/ppermute | solution.py:327
  599.5 91.4 %collective-permute-start.3 = (bf16[512,2048]{1,0:T(8,128)(2,1)}, bf16[512,2048]{1,0:T(8,128)(2,1)}, u32[]{:S(2)}, u32[]{:S(2)}) collective-permute-start(bf16[512,2048]{1,0:T(8,128)(2,1)} %gate.3.refs_5_), channel_id=1, source_target_pairs={{0,4},{2,6},{4,0},{6,2},{8,12},{10,14},{12,8},{14,10},{16,20},{18,... | collective-permute-start | bytes 6291464 | tf_op jit(solution)/shard_map/ppermute | solution.py:327
  599.5 136.3 %collective-permute-start.2 = (bf16[512,2048]{1,0:T(8,128)(2,1)}, bf16[512,2048]{1,0:T(8,128)(2,1)}, u32[]{:S(2)}, u32[]{:S(2)}) collective-permute-start(bf16[512,2048]{1,0:T(8,128)(2,1)} %collective-permute-done.1.refs_3_), channel_id=1, source_target_pairs={{0,4},{2,6},{4,0},{6,2},{8,12},{10,14},{12,8},{14,10},{16,20},{18,... | collective-permute-start | bytes 6291464 | tf_op jit(solution)/shard_map/ppermute | solution.py:327
  639.5 140.5 %collective-permute-start.5 = (bf16[512,2048]{1,0:T(8,128)(2,1)}, bf16[512,2048]{1,0:T(8,128)(2,1)}, u32[]{:S(2)}, u32[]{:S(2)}) collective-permute-start(bf16[512,2048]{1,0:T(8,128)(2,1)} %collective-permute-done.4.refs_7_), channel_id=1, source_target_pairs={{0,4},{2,6},{4,0},{6,2},{8,12},{10,14},{12,8},{14,10},{16,20},{18,... | collective-permute-start | bytes 6291464 | tf_op jit(solution)/shard_map/ppermute | solution.py:327
  645.9 134.1 %copy-start.5 = (bf16[512,2048]{1,0:T(8,128)(2,1)}, bf16[512,2048]{1,0:T(8,128)(2,1)S(1)}, u32[]{:S(2)}) copy-start(bf16[512,2048]{1,0:T(8,128)(2,1)S(1)} %collective-permute-done.refs_2_) | copy-start | bytes 6291460
  645.9 170.5 %collective-permute-start.9 = (bf16[4096,512]{1,0:T(8,128)(2,1)}, bf16[4096,512]{1,0:T(8,128)(2,1)}, u32[]{:S(2)}, u32[]{:S(2)}) collective-permute-start(bf16[4096,512]{1,0:T(8,128)(2,1)} %all-gather.5.cloned.1.call-done), channel_id=1, source_target_pairs={{0,2},{2,0},{4,6},{6,4},{8,10},{10,8},{12,14},{14,12},{16,18},{18,... | collective-permute-start | bytes 12582920 | tf_op jit(solution)/shard_map/ppermute | solution.py:327
  814.5 36.4 %collective-permute-start.8 = (bf16[512,1536]{1,0:T(8,128)(2,1)S(1)}, bf16[512,1536]{1,0:T(8,128)(2,1)}, u32[]{:S(2)}, u32[]{:S(2)}) collective-permute-start(bf16[512,1536]{1,0:T(8,128)(2,1)S(1)} %get-tuple-element.10), channel_id=1, source_target_pairs={{0,4},{2,6},{4,0},{6,2},{8,12},{10,14},{12,8},{14,10},{16,20},{18,... | collective-permute-start | bytes 4718600 | tf_op jit(solution)/shard_map/ppermute | solution.py:327
  816.4 1.6 copy-start.6
  833.6 28.5 %collective-permute-start.10 = (bf16[512,512]{1,0:T(8,128)(2,1)S(1)}, bf16[512,512]{1,0:T(8,128)(2,1)S(1)}, u32[]{:S(2)}, u32[]{:S(2)}) collective-permute-start(bf16[512,512]{1,0:T(8,128)(2,1)S(1)} %get-tuple-element.12), channel_id=1, source_target_pairs={{0,4},{2,6},{4,0},{6,2},{8,12},{10,14},{12,8},{14,10},{16,20},{18,... | collective-permute-start | bytes 1572872 | tf_op jit(solution)/shard_map/ppermute | solution.py:327
  834.2 28.7 %copy-start.1 = (s32[32,32]{1,0:T(8,128)S(1)}, s32[32,32]{1,0:T(8,128)}, u32[]{:S(2)}) copy-start(s32[32,32]{1,0:T(8,128)} %param.10) | copy-start | bytes 12292
  852.6 9.5 %copy-start.8 = (bf16[512,4096]{1,0:T(8,128)(2,1)}, bf16[512,4096]{1,0:T(8,128)(2,1)S(1)}, u32[]{:S(2)}) copy-start(bf16[512,4096]{1,0:T(8,128)(2,1)S(1)} %constant_dynamic-update-slice_fusion.1) | copy-start | bytes 12582916
Sparse Core Ops, SparseCore 0:
  60.6 350.7 all-gather.2
  497.8 110.4 all-gather.4

commit v3 on v1

--- a/solution.py
+++ b/solution.py
@@ -249,7 +249,7 @@
 
 
 def mix_kernel(pieces, start_ref, *refs):
-    w_ref, out_ref = refs[pieces], refs[pieces + 1]
+    w_ref, out_ref = refs[pieces], refs[-1]
     total = None
     for k in range(pieces):
         depth = refs[k].shape[1]
@@ -261,27 +261,29 @@
     out_ref[...] = total.astype(BF16)
 
 
-def mix(hidden, starts, weight):
+def mix(hidden, starts, weight, low, columns, result):
     tokens = hidden[0].shape[0]
-    depth, columns = weight.shape
-    tile = min(256, columns)
+    depth, part = weight.shape
+    tile = min(256, part)
+    first = low // tile
     pieces = len(hidden)
+    before = [] if result is None else [result]
     return pl.pallas_call(
         functools.partial(mix_kernel, pieces),
-        grid=(columns // tile,),
+        grid=(part // tile,),
         out_shape=jax.ShapeDtypeStruct((tokens, columns), BF16),
         in_specs=[pl.BlockSpec(memory_space=pltpu.SMEM)]
         + [pl.BlockSpec(h.shape, lambda i: (0, 0)) for h in hidden]
-        + [pl.BlockSpec((depth, tile), lambda i: (0, i))],
-        out_specs=pl.BlockSpec((tokens, tile), lambda i: (0, i)),
-        compiler_params=pltpu.CompilerParams(vmem_limit_bytes=VMEM),
-        cost_estimate=pl.CostEstimate(
-            flops=2 * tokens * depth * columns,
-            bytes_accessed=2 * depth * columns,
-            transcendentals=0,
+        + [pl.BlockSpec((depth, tile), lambda i: (0, i))]
+        + [pl.BlockSpec(memory_space=pl.ANY) for _ in before],
+        out_specs=pl.BlockSpec((tokens, tile), lambda i: (0, first + i)),
+        input_output_aliases={pieces + 2: 0} if before else {},
+        compiler_params=pltpu.CompilerParams(vmem_limit_bytes=VMEM),
+        cost_estimate=pl.CostEstimate(
+            flops=2 * tokens * depth * part, bytes_accessed=2 * depth * part, transcendentals=0
         ),
         name="mix",
-    )(starts, *hidden, weight)
+    )(starts, *hidden, weight, *before)
 
 
 def body(keyval, gating, skip_gain, filter_values, blocks, out_weight):
@@ -297,7 +299,13 @@
     unit = min(narrow, group_width)
     chunks = narrow // unit
 
-    weight = lax.all_gather(out_weight, "seq", axis=0, tiled=True)
+    columns = out_weight.shape[1]
+    eighth = columns // 8
+    bounds = [0, 4 * eighth, 7 * eighth, columns] if eighth % 256 == 0 else [0, columns]
+    weights = [
+        lax.all_gather(out_weight[:, low:high], "seq", axis=0, tiled=True)
+        for low, high in zip(bounds[:-1], bounds[1:])
+    ]
 
     exchange = functools.partial(
         lax.all_to_all, axis_name="seq", split_axis=0, concat_axis=0, tiled=True
@@ -340,7 +348,11 @@
             hidden.append(piece)
             source = lax.rem(side + peers - shift, peers)
             starts.append(source * channels + g * cycle * unit)
-    return mix(hidden, jnp.stack(starts).astype(jnp.int32), weight)
+    starts = jnp.stack(starts).astype(jnp.int32)
+    result = None
+    for low, weight in zip(bounds[:-1], weights):
+        result = mix(hidden, starts, weight, low, columns, result)
+    return result
 
 
 def solution(mesh):

time: 612 us -> 623 us (1.018)
  Pallas kernels: 110 us -> 120 us
  local copies, waits for them, and re-layouts: 3.64 us -> 12.8 us
  waiting for transfers between devices: 438 us -> 429 us
    pallas_call x1 -> x3, Pallas kernels: 42.9 us -> 52.8 us  [mix(): pl.pallas_call(functools.partial(mix_kernel, pieces), grid=(part // tile,...]
    all_to_all x2, waiting for transfers between devices: 111 us -> 102 us  [body(): done = exchange(convolve(g, twist, ahead, back, signals[g], filters))]
    slice x0 -> x3, local copies, waits for them, and re-layouts: none -> 7.85 us  [body(): out_weight[:, low:high]]
    all_gather x1 -> x3, waiting for transfers between devices: 107 us -> 110 us  [body(): lax.all_gather(out_weight[:, low:high], 'seq', axis=0, tiled=True)]
  transfers between devices with their start and end apart: 8 -> 10, of which waited for: 7 -> 8; matrix products, arithmetic and copies ran while one was open for 1% -> 2% of each run, Pallas kernels for 11% -> 18%
where the time goes in v3:
time: 623 us; the launch traced here: 620 us
  waiting for transfers between devices  429 us (69%)
  Pallas kernels  120 us (19%)
  starting transfers between devices  40.3 us (6%)
  between operations  13.3 us (2%)
  local copies, waits for them, and re-layouts  12.8 us (2%)
    all_gather x3, waiting for transfers between devices, body(): lax.all_gather(out_weight[:, low:high], 'seq', axis=0, tiled=True)  110 us
    all_to_all x2, waiting for transfers between devices, body(): exchange(pack_signal(keyval, g, cycle, unit))  106 us
    all_to_all x2, waiting for transfers between devices, body(): done = exchange(convolve(g, twist, ahead, back, signals[g], filters))  102 us
    all_to_all x1, waiting for transfers between devices, body(): filters = exchange(pack_filters(filter_values, cycle, chunks, unit))  65.9 us
    pallas_call x3, Pallas kernels, mix(): pl.pallas_call(functools.partial(mix_kernel, pieces), grid=(part // tile,...  52.8 us
    ppermute x2, waiting for transfers between devices, body(): lax.ppermute(own, 'tensor', [(t, (t + shift) % peers) for t in range(peer...  45.7 us
    pallas_call x2, Pallas kernels, convolve(): pl.pallas_call(conv_kernel, grid=(1,), out_shape=jax.ShapeDtypeStruct(sig...  41.2 us
    all_to_all x2, starting transfers between devices, body(): exchange(pack_signal(keyval, g, cycle, unit))  16.1 us
  transfers between devices with their start and end apart: 10, of which 8 were waited for; matrix products, arithmetic and copies ran while one was open for 2% of the time, Pallas kernels for 18%

profile of v3, /device:TPU:9, one launch (start us, length us, event | category | flops | bytes accessed | tf_op | source)
XLA Modules:
  0.0 620.5 jit_solution(15134300237930665420)
XLA Ops:
  6.5 3.2 slice.11
  9.8 0.0 all-gather.8.cloned.1.call-update
  9.8 0.0 all-gather.6.cloned.1.call-start
  9.8 2.7 slice.10
  12.5 0.0 all-gather.6.cloned.1.call-update
  12.5 8.2 %pack_filters.1 = bf16[16,2,256,128]{3,2,1,0:T(8,128)(2,1)} custom-call(f32[256,1,4096]{2,1,0:T(1,128)} %bitcast.10), custom_call_target="tpu_custom_call" | custom-call | bytes 6291456 | tf_op jit(solution)/shard_map/pack_filters/pallas_call | solution.py:205
  20.8 6.5 %all-to-all-start.1 = ((bf16[16,2,256,128]{3,2,1,0:T(8,128)(2,1)}), bf16[16,2,256,128]{3,2,1,0:T(8,128)(2,1)S(1)}, u32[]{:S(2)}, u32[]{:S(2)}) async-start(bf16[16,2,256,128]{3,2,1,0:T(8,128)(2,1)} %pack_filters.1), calls=%async_computation.1 | async-start | bytes 4194304 | tf_op jit(solution)/shard_map/all_to_all | solution.py:314
  27.2 3.9 pack_signal.3
  31.2 65.9 %all-to-all-done.1.filter_ref = bf16[16,2,256,128]{3,2,1,0:T(8,128)(2,1)S(1)} async-done(((bf16[16,2,256,128]{3,2,1,0:T(8,128)(2,1)}), bf16[16,2,256,128]{3,2,1,0:T(8,128)(2,1)S(1)}, u32[]{:S(2)}, u32[]{:S(2)}) %all-to-all-start.1) | async-done | bytes 2097184 | tf_op jit(solution)/shard_map/all_to_all | solution.py:314
  97.1 1.3 copy-done.5
  98.4 8.0 %all-to-all-start.3 = ((bf16[16,512,128]{2,1,0:T(8,128)(2,1)}), bf16[16,512,128]{2,1,0:T(8,128)(2,1)}, u32[]{:S(2)}, u32[]{:S(2)}) async-start(bf16[16,512,128]{2,1,0:T(8,128)(2,1)} %pack_signal.3), calls=%async_computation.3 | async-start | bytes 4194304 | tf_op jit(solution)/shard_map/all_to_all | solution.py:313
  106.4 3.9 pack_signal.2
  110.3 66.0 %all-to-all-done.3.x_ref = bf16[16,512,128]{2,1,0:T(8,128)(2,1)} async-done(((bf16[16,512,128]{2,1,0:T(8,128)(2,1)}), bf16[16,512,128]{2,1,0:T(8,128)(2,1)}, u32[]{:S(2)}, u32[]{:S(2)}) %all-to-all-start.3) | async-done | bytes 2097184 | tf_op jit(solution)/shard_map/all_to_all | solution.py:313
  176.3 8.1 %all-to-all-start = ((bf16[16,512,128]{2,1,0:T(8,128)(2,1)}), bf16[16,512,128]{2,1,0:T(8,128)(2,1)}, u32[]{:S(2)}, u32[]{:S(2)}) async-start(bf16[16,512,128]{2,1,0:T(8,128)(2,1)} %pack_signal.2), calls=%async_computation | async-start | bytes 4194304 | tf_op jit(solution)/shard_map/all_to_all | solution.py:313
  184.4 0.0 all-gather.4.cloned.1.call-start
  184.5 1.9 slice.9
  186.4 0.0 all-gather.4.cloned.1.call-update
  186.5 0.6 gather_fusion
  187.1 0.1 select_multiply_fusion
  187.1 0.1 add.116
  187.2 0.1 add.117
  187.3 0.1 add.119
  187.4 0.1 fusion.22
  187.6 0.1 copy.9.twist_ref
  187.7 2.3 negate_convert_fusion
  190.0 0.1 maximum_maximum_fusion.1.back_ref
  190.1 2.5 fusion.15
  192.6 0.1 maximum_maximum_fusion.ahead_ref
  192.7 20.6 %convolve.3 = bf16[16,512,128]{2,1,0:T(8,128)(2,1)S(1)} custom-call(f32[512,32]{1,0:T(8,128)S(1)} %copy.9.twist_ref, bf16[2,256,1024]{2,1,0:T(8,128)(2,1)S(1)} %maximum_maximum_fusion.ahead_ref, bf16[2,1024,256]{2,1,0:T(8,128)(2,1)S(1)} %maximum_maximum_fusion.1.back_ref, bf16[16,512,128]{2,1,0:T(8,128)(2,1)} %all-to-all-done.3.x_ref, ...), custom_call_target="tpu_custom_call" | custom-call | flops 2147483648 | bytes 16777216 | tf_op jit(solution)/shard_map/convolve/pallas_call | solution.py:147
  213.3 1.3 copy-done.3
  214.6 39.7 %all-to-all-done.x_ref = bf16[16,512,128]{2,1,0:T(8,128)(2,1)} async-done(((bf16[16,512,128]{2,1,0:T(8,128)(2,1)}), bf16[16,512,128]{2,1,0:T(8,128)(2,1)}, u32[]{:S(2)}, u32[]{:S(2)}) %all-to-all-start) | async-done | bytes 2097184 | tf_op jit(solution)/shard_map/all_to_all | solution.py:313
  254.3 8.1 %all-to-all-start.4 = ((bf16[16,512,128]{2,1,0:T(8,128)(2,1)}), bf16[16,512,128]{2,1,0:T(8,128)(2,1)}, u32[]{:S(2)}, u32[]{:S(2)}) async-start(bf16[16,512,128]{2,1,0:T(8,128)(2,1)} %copy-done.3), calls=%async_computation.4 | async-start | bytes 4194304 | tf_op jit(solution)/shard_map/all_to_all | solution.py:339
  262.4 20.6 %convolve.2 = bf16[16,512,128]{2,1,0:T(8,128)(2,1)S(1)} custom-call(f32[512,32]{1,0:T(8,128)S(1)} %copy.9.twist_ref, bf16[2,256,1024]{2,1,0:T(8,128)(2,1)S(1)} %maximum_maximum_fusion.ahead_ref, bf16[2,1024,256]{2,1,0:T(8,128)(2,1)S(1)} %maximum_maximum_fusion.1.back_ref, bf16[16,512,128]{2,1,0:T(8,128)(2,1)} %all-to-all-done.x_ref, ...), custom_call_target="tpu_custom_call" | custom-call | flops 2147483648 | bytes 16777216 | tf_op jit(solution)/shard_map/convolve/pallas_call | solution.py:147
  283.1 1.3 copy-done.2
  284.4 46.1 %all-to-all-done.4.c_ref = bf16[16,512,128]{2,1,0:T(8,128)(2,1)} async-done(((bf16[16,512,128]{2,1,0:T(8,128)(2,1)}), bf16[16,512,128]{2,1,0:T(8,128)(2,1)}, u32[]{:S(2)}, u32[]{:S(2)}) %all-to-all-start.4) | async-done | bytes 2097184 | tf_op jit(solution)/shard_map/all_to_all | solution.py:339
  330.5 7.1 %all-to-all-start.2 = ((bf16[16,512,128]{2,1,0:T(8,128)(2,1)}), bf16[16,512,128]{2,1,0:T(8,128)(2,1)S(1)}, u32[]{:S(2)}, u32[]{:S(2)}) async-start(bf16[16,512,128]{2,1,0:T(8,128)(2,1)} %copy-done.2), calls=%async_computation.2 | async-start | bytes 4194304 | tf_op jit(solution)/shard_map/all_to_all | solution.py:339
  337.5 5.2 gate.3.refs_2_
  342.7 1.2 collective-permute-start.1
  344.0 56.0 %all-to-all-done.2.c_ref = bf16[16,512,128]{2,1,0:T(8,128)(2,1)S(1)} async-done(((bf16[16,512,128]{2,1,0:T(8,128)(2,1)}), bf16[16,512,128]{2,1,0:T(8,128)(2,1)S(1)}, u32[]{:S(2)}, u32[]{:S(2)}) %all-to-all-start.2) | async-done | bytes 2097184 | tf_op jit(solution)/shard_map/all_to_all | solution.py:339
  399.9 4.7 gate.2.refs_0_
  404.6 1.2 collective-permute-start
  405.8 0.1 pad_add_fusion.start_ref
  405.9 45.7 %collective-permute-done.refs_1_ = bf16[512,2048]{1,0:T(8,128)(2,1)S(1)} collective-permute-done((bf16[512,2048]{1,0:T(8,128)(2,1)}, bf16[512,2048]{1,0:T(8,128)(2,1)S(1)}, u32[]{:S(2)}, u32[]{:S(2)}) %collective-permute-start) | collective-permute-done | bytes 2097184 | tf_op jit(solution)/shard_map/ppermute | solution.py:345
  451.6 24.1 %mix.3.refs_5_ = bf16[512,4096]{1,0:T(8,128)(2,1)} custom-call(s32[4]{0:T(128)S(1)} %pad_add_fusion.start_ref, bf16[512,2048]{1,0:T(8,128)(2,1)} %gate.2.refs_0_, bf16[512,2048]{1,0:T(8,128)(2,1)S(1)} %collective-permute-done.refs_1_, bf16[512,2048]{1,0:T(8,128)(2,1)} %gate.3.refs_2_, bf16[512,2048]{1,0:T(8,128)(2,1)} %collective-permute-done.1.refs_3_, ...), custom_call_target="tpu_custom_call" | custom-call | flops 17179869184 | bytes 33554432 | tf_op jit(solution)/shard_map/mix/pallas_call | solution.py:271
  475.7 52.3 %all-gather.6.cloned.1.call-done.refs_4_ = bf16[8192,1536]{1,0:T(8,128)(2,1)} async-done(((bf16[512,1536]{1,0:T(8,128)(2,1)}), bf16[8192,1536]{1,0:T(8,128)(2,1)}) %all-gather.6.cloned.1.call-update) | async-done | bytes 25165840 | tf_op jit(solution)/shard_map/all_gather | solution.py:306
  527.9 19.2 %mix.4.refs_5_ = bf16[512,4096]{1,0:T(8,128)(2,1)} custom-call(s32[4]{0:T(128)S(1)} %pad_add_fusion.start_ref, bf16[512,2048]{1,0:T(8,128)(2,1)} %gate.2.refs_0_, bf16[512,2048]{1,0:T(8,128)(2,1)S(1)} %collective-permute-done.refs_1_, bf16[512,2048]{1,0:T(8,128)(2,1)} %gate.3.refs_2_, ...), custom_call_target="tpu_custom_call", output_to_operand_aliasing={{}: (6, {})} | custom-call | flops 12884901888 | bytes 25165824 | tf_op jit(solution)/shard_map/mix/pallas_call | solution.py:271
  547.1 57.3 %all-gather.4.cloned.1.call-done.refs_4_ = bf16[8192,512]{1,0:T(8,128)(2,1)} async-done(((bf16[512,512]{1,0:T(8,128)(2,1)}), bf16[8192,512]{1,0:T(8,128)(2,1)}) %all-gather.4.cloned.1.call-update) | async-done | bytes 8388624 | tf_op jit(solution)/shard_map/all_gather | solution.py:306
  604.4 9.5 %mix.5 = bf16[512,4096]{1,0:T(8,128)(2,1)} custom-call(s32[4]{0:T(128)S(1)} %pad_add_fusion.start_ref, bf16[512,2048]{1,0:T(8,128)(2,1)} %gate.2.refs_0_, bf16[512,2048]{1,0:T(8,128)(2,1)S(1)} %collective-permute-done.refs_1_, bf16[512,2048]{1,0:T(8,128)(2,1)} %gate.3.refs_2_, ...), custom_call_target="tpu_custom_call", output_to_operand_aliasing={{}: (6, {})} | custom-call | flops 4294967296 | bytes 8388608 | tf_op jit(solution)/shard_map/mix/pallas_call | solution.py:271
  (18 shorter events, 0.1 us)
Async XLA Ops:
  6.5 179.9 %copy-start = (s32[32,32]{1,0:T(8,128)S(1)}, s32[32,32]{1,0:T(8,128)}, u32[]{:S(2)}) copy-start(s32[32,32]{1,0:T(8,128)} %param.10) | copy-start | bytes 12292
  6.5 445.0 %all-gather.8.cloned.1.call-start = ((), (), s32[]{:S(2)}) async-start(), calls=%async_computation.7 | async-start | bytes 35651584 | tf_op jit(solution)/shard_map/all_gather | solution.py:306
  9.8 518.2 %all-gather.6.cloned.1.call-start = ((), (), s32[]{:S(2)}) async-start(), calls=%async_computation.6 | async-start | bytes 26738688 | tf_op jit(solution)/shard_map/all_gather | solution.py:306
  20.8 76.3 %all-to-all-start.1 = ((bf16[16,2,256,128]{3,2,1,0:T(8,128)(2,1)}), bf16[16,2,256,128]{3,2,1,0:T(8,128)(2,1)S(1)}, u32[]{:S(2)}, u32[]{:S(2)}) async-start(bf16[16,2,256,128]{3,2,1,0:T(8,128)(2,1)} %pack_filters.1), calls=%async_computation.1 | async-start | bytes 4194304 | tf_op jit(solution)/shard_map/all_to_all | solution.py:314
  97.1 1.3 copy-start.5
  98.4 77.9 %all-to-all-start.3 = ((bf16[16,512,128]{2,1,0:T(8,128)(2,1)}), bf16[16,512,128]{2,1,0:T(8,128)(2,1)}, u32[]{:S(2)}, u32[]{:S(2)}) async-start(bf16[16,512,128]{2,1,0:T(8,128)(2,1)} %pack_signal.3), calls=%async_computation.3 | async-start | bytes 4194304 | tf_op jit(solution)/shard_map/all_to_all | solution.py:313
  176.3 78.0 %all-to-all-start = ((bf16[16,512,128]{2,1,0:T(8,128)(2,1)}), bf16[16,512,128]{2,1,0:T(8,128)(2,1)}, u32[]{:S(2)}, u32[]{:S(2)}) async-start(bf16[16,512,128]{2,1,0:T(8,128)(2,1)} %pack_signal.2), calls=%async_computation | async-start | bytes 4194304 | tf_op jit(solution)/shard_map/all_to_all | solution.py:313
  184.4 420.0 %all-gather.4.cloned.1.call-start = ((), (), s32[]{:S(2)}) async-start(), calls=%async_computation.5 | async-start | bytes 8912896 | tf_op jit(solution)/shard_map/all_gather | solution.py:306
  213.3 1.3 copy-start.3
  254.3 76.1 %all-to-all-start.4 = ((bf16[16,512,128]{2,1,0:T(8,128)(2,1)}), bf16[16,512,128]{2,1,0:T(8,128)(2,1)}, u32[]{:S(2)}, u32[]{:S(2)}) async-start(bf16[16,512,128]{2,1,0:T(8,128)(2,1)} %copy-done.3), calls=%async_computation.4 | async-start | bytes 4194304 | tf_op jit(solution)/shard_map/all_to_all | solution.py:339
  283.0 1.3 copy-start.2
  284.4 53.2 %copy-start.4 = (f32[4096]{0:T(1024)S(1)}, f32[4096]{0:T(1024)}, u32[]{:S(2)}) copy-start(f32[4096]{0:T(1024)} %param.8) | copy-start | bytes 49156
  330.5 69.5 %all-to-all-start.2 = ((bf16[16,512,128]{2,1,0:T(8,128)(2,1)}), bf16[16,512,128]{2,1,0:T(8,128)(2,1)S(1)}, u32[]{:S(2)}, u32[]{:S(2)}) async-start(bf16[16,512,128]{2,1,0:T(8,128)(2,1)} %copy-done.2), calls=%async_computation.2 | async-start | bytes 4194304 | tf_op jit(solution)/shard_map/all_to_all | solution.py:339
  342.7 63.2 %collective-permute-start.1 = (bf16[512,2048]{1,0:T(8,128)(2,1)}, bf16[512,2048]{1,0:T(8,128)(2,1)}, u32[]{:S(2)}, u32[]{:S(2)}) collective-permute-start(bf16[512,2048]{1,0:T(8,128)(2,1)} %gate.3.refs_2_), channel_id=1, source_target_pairs={{0,1},{1,0},{2,3},{3,2},{4,5},{5,4},{6,7},{7,6},{8,9},{9,8},{10,11... | collective-permute-start | bytes 6291464 | tf_op jit(solution)/shard_map/ppermute | solution.py:345
  404.6 46.9 %collective-permute-start = (bf16[512,2048]{1,0:T(8,128)(2,1)}, bf16[512,2048]{1,0:T(8,128)(2,1)S(1)}, u32[]{:S(2)}, u32[]{:S(2)}) collective-permute-start(bf16[512,2048]{1,0:T(8,128)(2,1)} %gate.2.refs_0_), channel_id=1, source_target_pairs={{0,1},{1,0},{2,3},{3,2},{4,5},{5,4},{6,7},{7,6},{8,9},{9,8},{10,11... | collective-permute-start | bytes 6291464 | tf_op jit(solution)/shard_map/ppermute | solution.py:345
  604.4 9.5 %copy-start.1 = (s32[32,32]{1,0:T(8,128)S(1)}, s32[32,32]{1,0:T(8,128)}, u32[]{:S(2)}) copy-start(s32[32,32]{1,0:T(8,128)} %param.10) | copy-start | bytes 12292
Sparse Core Ops, SparseCore 0:
  9.9 388.7 all-gather.7
  400.3 127.5 all-gather.5
  530.1 74.2 all-gather.3

commit v4 on v3

--- a/solution.py
+++ b/solution.py
@@ -249,34 +249,44 @@
 
 
 def mix_kernel(pieces, start_ref, *refs):
-    w_ref, out_ref = refs[pieces], refs[-1]
-    total = None
+    w_ref, out_ref, total_ref = refs[pieces], refs[-2], refs[-1]
+    step = pl.program_id(1)
+    columns = w_ref.shape[1]
+    tile = min(256, columns)
     for k in range(pieces):
-        depth = refs[k].shape[1]
-        start = pl.multiple_of(start_ref[k], depth)
-        part = jnp.dot(
-            refs[k][...], w_ref[pl.ds(start, depth), :], preferred_element_type=F32
-        )
-        total = part if total is None else total + part
-    out_ref[...] = total.astype(BF16)
+
+        @pl.when(step == k)
+        def _(k=k):
+            for low in range(0, columns, tile):
+                lanes = slice(low, low + tile)
+                part = jnp.dot(refs[k][...], w_ref[:, lanes], preferred_element_type=F32)
+                if k:
+                    part = total_ref[:, lanes] + part
+                if k < pieces - 1:
+                    total_ref[:, lanes] = part
+                else:
+                    out_ref[:, lanes] = part.astype(BF16)
 
 
 def mix(hidden, starts, weight, low, columns, result):
-    tokens = hidden[0].shape[0]
+    tokens, width = hidden[0].shape
     depth, part = weight.shape
-    tile = min(256, part)
+    tile = min(1024, part)
     first = low // tile
     pieces = len(hidden)
     before = [] if result is None else [result]
     return pl.pallas_call(
         functools.partial(mix_kernel, pieces),
-        grid=(part // tile,),
+        grid_spec=pltpu.PrefetchScalarGridSpec(
+            num_scalar_prefetch=1,
+            grid=(part // tile, pieces),
+            in_specs=[pl.BlockSpec(h.shape, lambda i, k, s: (0, 0)) for h in hidden]
+            + [pl.BlockSpec((width, tile), lambda i, k, s: (s[k], i))]
+            + [pl.BlockSpec(memory_space=pl.ANY) for _ in before],
+            out_specs=pl.BlockSpec((tokens, tile), lambda i, k, s: (0, first + i)),
+            scratch_shapes=[pltpu.VMEM((tokens, tile), F32)],
+        ),
         out_shape=jax.ShapeDtypeStruct((tokens, columns), BF16),
-        in_specs=[pl.BlockSpec(memory_space=pltpu.SMEM)]
-        + [pl.BlockSpec(h.shape, lambda i: (0, 0)) for h in hidden]
-        + [pl.BlockSpec((depth, tile), lambda i: (0, i))]
-        + [pl.BlockSpec(memory_space=pl.ANY) for _ in before],
-        out_specs=pl.BlockSpec((tokens, tile), lambda i: (0, first + i)),
         input_output_aliases={pieces + 2: 0} if before else {},
         compiler_params=pltpu.CompilerParams(vmem_limit_bytes=VMEM),
         cost_estimate=pl.CostEstimate(
@@ -301,7 +311,7 @@
 
     columns = out_weight.shape[1]
     eighth = columns // 8
-    bounds = [0, 4 * eighth, 7 * eighth, columns] if eighth % 256 == 0 else [0, columns]
+    bounds = [0, 4 * eighth, columns] if eighth % 256 == 0 else [0, columns]
     weights = [
         lax.all_gather(out_weight[:, low:high], "seq", axis=0, tiled=True)
         for low, high in zip(bounds[:-1], bounds[1:])
@@ -347,7 +357,7 @@
                 )
             hidden.append(piece)
             source = lax.rem(side + peers - shift, peers)
-            starts.append(source * channels + g * cycle * unit)
+            starts.append(source * chunks + g)
     starts = jnp.stack(starts).astype(jnp.int32)
     result = None
     for low, weight in zip(bounds[:-1], weights):

time: 623 us -> 605 us (0.971)
  waiting for transfers between devices: 429 us -> 417 us
    all_gather x3 -> x2, waiting for transfers between devices: 110 us -> 92.8 us  [body(): lax.all_gather(out_weight[:, low:high], 'seq', axis=0, tiled=True)]
    pallas_call x3 -> x2, Pallas kernels: 52.8 us -> 50 us  [mix(): pl.pallas_call(functools.partial(mix_kernel, pieces), grid_spec=pltpu.Pre...]
  transfers between devices with their start and end apart: 10 -> 9, of which waited for: 8 -> 7; matrix products, arithmetic and copies ran while one was open for 2% -> 1% of each run, Pallas kernels for 18% -> 15%
where the time goes in v4:
time: 605 us; the launch traced here: 603 us
  waiting for transfers between devices  417 us (69%)
  Pallas kernels  117 us (19%)
  starting transfers between devices  40.4 us (7%)
  between operations  13.5 us (2%)
  local copies, waits for them, and re-layouts  9.81 us (2%)
    all_to_all x2, waiting for transfers between devices, body(): exchange(pack_signal(keyval, g, cycle, unit))  108 us
    all_to_all x2, waiting for transfers between devices, body(): done = exchange(convolve(g, twist, ahead, back, signals[g], filters))  104 us
    all_gather x2, waiting for transfers between devices, body(): lax.all_gather(out_weight[:, low:high], 'seq', axis=0, tiled=True)  92.8 us
    all_to_all x1, waiting for transfers between devices, body(): filters = exchange(pack_filters(filter_values, cycle, chunks, unit))  65.9 us
    pallas_call x2, Pallas kernels, mix(): pl.pallas_call(functools.partial(mix_kernel, pieces), grid_spec=pltpu.Pre...  50 us
    ppermute x2, waiting for transfers between devices, body(): lax.ppermute(own, 'tensor', [(t, (t + shift) % peers) for t in range(peer...  45.7 us
    pallas_call x2, Pallas kernels, convolve(): pl.pallas_call(conv_kernel, grid=(1,), out_shape=jax.ShapeDtypeStruct(sig...  41.1 us
    all_to_all x2, starting transfers between devices, body(): exchange(pack_signal(keyval, g, cycle, unit))  16.1 us
  transfers between devices with their start and end apart: 9, of which 7 were waited for; matrix products, arithmetic and copies ran while one was open for 1% of the time, Pallas kernels for 15%

profile of v4, /device:TPU:9, one launch (start us, length us, event | category | flops | bytes accessed | tf_op | source)
XLA Modules:
  0.0 602.8 jit_solution(9214498412602595775)
XLA Ops:
  6.5 0.0 copy-start
  6.5 0.0 all-gather.5.cloned.1.call-start
  6.5 4.8 fusion.25
  11.4 0.0 all-gather.5.cloned.1.call-update
  11.4 0.0 all-gather.3.cloned.1.call-start
  11.4 0.7 all-gather.3.cloned.1.call-update
  12.2 8.0 %pack_filters.1 = bf16[16,2,256,128]{3,2,1,0:T(8,128)(2,1)} custom-call(f32[256,1,4096]{2,1,0:T(1,128)} %bitcast.10), custom_call_target="tpu_custom_call" | custom-call | bytes 6291456 | tf_op jit(solution)/shard_map/pack_filters/pallas_call | solution.py:205
  20.2 6.6 %all-to-all-start.1 = ((bf16[16,2,256,128]{3,2,1,0:T(8,128)(2,1)}), bf16[16,2,256,128]{3,2,1,0:T(8,128)(2,1)S(1)}, u32[]{:S(2)}, u32[]{:S(2)}) async-start(bf16[16,2,256,128]{3,2,1,0:T(8,128)(2,1)} %pack_filters.1), calls=%async_computation.1 | async-start | bytes 4194304 | tf_op jit(solution)/shard_map/all_to_all | solution.py:324
  26.8 4.0 pack_signal.3
  30.7 65.9 %all-to-all-done.1.filter_ref = bf16[16,2,256,128]{3,2,1,0:T(8,128)(2,1)S(1)} async-done(((bf16[16,2,256,128]{3,2,1,0:T(8,128)(2,1)}), bf16[16,2,256,128]{3,2,1,0:T(8,128)(2,1)S(1)}, u32[]{:S(2)}, u32[]{:S(2)}) %all-to-all-start.1) | async-done | bytes 2097184 | tf_op jit(solution)/shard_map/all_to_all | solution.py:324
  96.6 1.3 copy-done.5
  97.9 8.0 %all-to-all-start.3 = ((bf16[16,512,128]{2,1,0:T(8,128)(2,1)}), bf16[16,512,128]{2,1,0:T(8,128)(2,1)}, u32[]{:S(2)}, u32[]{:S(2)}) async-start(bf16[16,512,128]{2,1,0:T(8,128)(2,1)} %pack_signal.3), calls=%async_computation.3 | async-start | bytes 4194304 | tf_op jit(solution)/shard_map/all_to_all | solution.py:323
  106.0 4.1 pack_signal.2
  110.0 65.9 %all-to-all-done.3.x_ref = bf16[16,512,128]{2,1,0:T(8,128)(2,1)} async-done(((bf16[16,512,128]{2,1,0:T(8,128)(2,1)}), bf16[16,512,128]{2,1,0:T(8,128)(2,1)}, u32[]{:S(2)}, u32[]{:S(2)}) %all-to-all-start.3) | async-done | bytes 2097184 | tf_op jit(solution)/shard_map/all_to_all | solution.py:323
  175.9 8.1 %all-to-all-start = ((bf16[16,512,128]{2,1,0:T(8,128)(2,1)}), bf16[16,512,128]{2,1,0:T(8,128)(2,1)}, u32[]{:S(2)}, u32[]{:S(2)}) async-start(bf16[16,512,128]{2,1,0:T(8,128)(2,1)} %pack_signal.2), calls=%async_computation | async-start | bytes 4194304 | tf_op jit(solution)/shard_map/all_to_all | solution.py:323
  184.0 0.1 add.119
  184.1 0.0 copy-done
  184.1 0.6 gather_fusion
  184.7 0.1 select_multiply_fusion
  184.8 0.1 add.116
  184.9 0.1 add.117
  185.0 0.1 fusion.22
  185.1 0.1 copy.8.twist_ref
  185.3 2.5 fusion.15
  187.8 0.1 maximum_maximum_fusion.ahead_ref
  187.9 2.3 negate_convert_fusion
  190.2 0.1 maximum_maximum_fusion.1.back_ref
  190.3 20.5 %convolve.3 = bf16[16,512,128]{2,1,0:T(8,128)(2,1)S(1)} custom-call(f32[512,32]{1,0:T(8,128)S(1)} %copy.8.twist_ref, bf16[2,256,1024]{2,1,0:T(8,128)(2,1)S(1)} %maximum_maximum_fusion.ahead_ref, bf16[2,1024,256]{2,1,0:T(8,128)(2,1)S(1)} %maximum_maximum_fusion.1.back_ref, bf16[16,512,128]{2,1,0:T(8,128)(2,1)} %all-to-all-done.3.x_ref, ...), custom_call_target="tpu_custom_call" | custom-call | flops 2147483648 | bytes 16777216 | tf_op jit(solution)/shard_map/convolve/pallas_call | solution.py:147
  210.8 0.0 copy-start.3
  210.8 1.3 copy-done.3
  212.2 41.7 %all-to-all-done.x_ref = bf16[16,512,128]{2,1,0:T(8,128)(2,1)} async-done(((bf16[16,512,128]{2,1,0:T(8,128)(2,1)}), bf16[16,512,128]{2,1,0:T(8,128)(2,1)}, u32[]{:S(2)}, u32[]{:S(2)}) %all-to-all-start) | async-done | bytes 2097184 | tf_op jit(solution)/shard_map/all_to_all | solution.py:323
  253.9 8.1 %all-to-all-start.4 = ((bf16[16,512,128]{2,1,0:T(8,128)(2,1)}), bf16[16,512,128]{2,1,0:T(8,128)(2,1)}, u32[]{:S(2)}, u32[]{:S(2)}) async-start(bf16[16,512,128]{2,1,0:T(8,128)(2,1)} %copy-done.3), calls=%async_computation.4 | async-start | bytes 4194304 | tf_op jit(solution)/shard_map/all_to_all | solution.py:349
  262.0 20.5 %convolve.2 = bf16[16,512,128]{2,1,0:T(8,128)(2,1)S(1)} custom-call(f32[512,32]{1,0:T(8,128)S(1)} %copy.8.twist_ref, bf16[2,256,1024]{2,1,0:T(8,128)(2,1)S(1)} %maximum_maximum_fusion.ahead_ref, bf16[2,1024,256]{2,1,0:T(8,128)(2,1)S(1)} %maximum_maximum_fusion.1.back_ref, bf16[16,512,128]{2,1,0:T(8,128)(2,1)} %all-to-all-done.x_ref, ...), custom_call_target="tpu_custom_call" | custom-call | flops 2147483648 | bytes 16777216 | tf_op jit(solution)/shard_map/convolve/pallas_call | solution.py:147
  282.6 0.0 copy-start.2
  282.6 1.3 copy-done.2
  283.9 46.1 %all-to-all-done.4.c_ref = bf16[16,512,128]{2,1,0:T(8,128)(2,1)} async-done(((bf16[16,512,128]{2,1,0:T(8,128)(2,1)}), bf16[16,512,128]{2,1,0:T(8,128)(2,1)}, u32[]{:S(2)}, u32[]{:S(2)}) %all-to-all-start.4) | async-done | bytes 2097184 | tf_op jit(solution)/shard_map/all_to_all | solution.py:349
  330.0 7.1 %all-to-all-start.2 = ((bf16[16,512,128]{2,1,0:T(8,128)(2,1)}), bf16[16,512,128]{2,1,0:T(8,128)(2,1)S(1)}, u32[]{:S(2)}, u32[]{:S(2)}) async-start(bf16[16,512,128]{2,1,0:T(8,128)(2,1)} %copy-done.2), calls=%async_computation.2 | async-start | bytes 4194304 | tf_op jit(solution)/shard_map/all_to_all | solution.py:349
  337.1 5.1 gate.3.refs_2_
  342.2 1.2 collective-permute-start.1
  343.4 58.1 %all-to-all-done.2.c_ref = bf16[16,512,128]{2,1,0:T(8,128)(2,1)S(1)} async-done(((bf16[16,512,128]{2,1,0:T(8,128)(2,1)}), bf16[16,512,128]{2,1,0:T(8,128)(2,1)S(1)}, u32[]{:S(2)}, u32[]{:S(2)}) %all-to-all-start.2) | async-done | bytes 2097184 | tf_op jit(solution)/shard_map/all_to_all | solution.py:349
  401.5 4.7 gate.2.refs_0_
  406.2 1.2 collective-permute-start
  407.4 0.1 pad_add_fusion.start_ref
  407.5 0.0 collective-permute-done.1.refs_3_
  407.5 45.7 %collective-permute-done.refs_1_ = bf16[512,2048]{1,0:T(8,128)(2,1)S(1)} collective-permute-done((bf16[512,2048]{1,0:T(8,128)(2,1)}, bf16[512,2048]{1,0:T(8,128)(2,1)S(1)}, u32[]{:S(2)}, u32[]{:S(2)}) %collective-permute-start) | collective-permute-done | bytes 2097184 | tf_op jit(solution)/shard_map/ppermute | solution.py:355
  453.2 25.2 %mix.2.refs_5_ = bf16[512,4096]{1,0:T(8,128)(2,1)} custom-call(s32[4]{0:T(128)S(1)} %pad_add_fusion.start_ref, bf16[512,2048]{1,0:T(8,128)(2,1)} %gate.2.refs_0_, bf16[512,2048]{1,0:T(8,128)(2,1)S(1)} %collective-permute-done.refs_1_, bf16[512,2048]{1,0:T(8,128)(2,1)} %gate.3.refs_2_, bf16[512,2048]{1,0:T(8,128)(2,1)} %collective-permute-done.1.refs_3_, ...), custom_call_target="tpu_custom_call" | custom-call | flops 17179869184 | bytes 33554432 | tf_op jit(solution)/shard_map/mix/pallas_call | solution.py:278
  478.3 92.8 %all-gather.3.cloned.1.call-done.refs_4_ = bf16[8192,2048]{1,0:T(8,128)(2,1)} async-done(((bf16[512,2048]{1,0:T(8,128)(2,1)}), bf16[8192,2048]{1,0:T(8,128)(2,1)}) %all-gather.3.cloned.1.call-update) | async-done | bytes 33554448 | tf_op jit(solution)/shard_map/all_gather | solution.py:316
  571.1 24.8 %mix.3 = bf16[512,4096]{1,0:T(8,128)(2,1)} custom-call(s32[4]{0:T(128)S(1)} %pad_add_fusion.start_ref, bf16[512,2048]{1,0:T(8,128)(2,1)} %gate.2.refs_0_, bf16[512,2048]{1,0:T(8,128)(2,1)S(1)} %collective-permute-done.refs_1_, bf16[512,2048]{1,0:T(8,128)(2,1)} %gate.3.refs_2_, ...), custom_call_target="tpu_custom_call", output_to_operand_aliasing={{}: (6, {})} | custom-call | flops 17179869184 | bytes 33554432 | tf_op jit(solution)/shard_map/mix/pallas_call | solution.py:278
  (12 shorter events, 0.1 us)
Async XLA Ops:
  6.5 177.6 %copy-start = (s32[32,32]{1,0:T(8,128)S(1)}, s32[32,32]{1,0:T(8,128)}, u32[]{:S(2)}) copy-start(s32[32,32]{1,0:T(8,128)} %param.10) | copy-start | bytes 12292
  6.5 446.6 %all-gather.5.cloned.1.call-start = ((), (), s32[]{:S(2)}) async-start(), calls=%async_computation.6 | async-start | bytes 35651584 | tf_op jit(solution)/shard_map/all_gather | solution.py:316
  11.4 559.7 %all-gather.3.cloned.1.call-start = ((), (), s32[]{:S(2)}) async-start(), calls=%async_computation.5 | async-start | bytes 35651584 | tf_op jit(solution)/shard_map/all_gather | solution.py:316
  20.2 76.4 %all-to-all-start.1 = ((bf16[16,2,256,128]{3,2,1,0:T(8,128)(2,1)}), bf16[16,2,256,128]{3,2,1,0:T(8,128)(2,1)S(1)}, u32[]{:S(2)}, u32[]{:S(2)}) async-start(bf16[16,2,256,128]{3,2,1,0:T(8,128)(2,1)} %pack_filters.1), calls=%async_computation.1 | async-start | bytes 4194304 | tf_op jit(solution)/shard_map/all_to_all | solution.py:324
  96.6 1.3 copy-start.5
  97.9 78.0 %all-to-all-start.3 = ((bf16[16,512,128]{2,1,0:T(8,128)(2,1)}), bf16[16,512,128]{2,1,0:T(8,128)(2,1)}, u32[]{:S(2)}, u32[]{:S(2)}) async-start(bf16[16,512,128]{2,1,0:T(8,128)(2,1)} %pack_signal.3), calls=%async_computation.3 | async-start | bytes 4194304 | tf_op jit(solution)/shard_map/all_to_all | solution.py:323
  175.9 78.0 %all-to-all-start = ((bf16[16,512,128]{2,1,0:T(8,128)(2,1)}), bf16[16,512,128]{2,1,0:T(8,128)(2,1)}, u32[]{:S(2)}, u32[]{:S(2)}) async-start(bf16[16,512,128]{2,1,0:T(8,128)(2,1)} %pack_signal.2), calls=%async_computation | async-start | bytes 4194304 | tf_op jit(solution)/shard_map/all_to_all | solution.py:323
  210.8 1.4 copy-start.3
  253.9 76.1 %all-to-all-start.4 = ((bf16[16,512,128]{2,1,0:T(8,128)(2,1)}), bf16[16,512,128]{2,1,0:T(8,128)(2,1)}, u32[]{:S(2)}, u32[]{:S(2)}) async-start(bf16[16,512,128]{2,1,0:T(8,128)(2,1)} %copy-done.3), calls=%async_computation.4 | async-start | bytes 4194304 | tf_op jit(solution)/shard_map/all_to_all | solution.py:349
  282.6 1.3 copy-start.2
  283.9 53.2 %copy-start.4 = (f32[4096]{0:T(1024)S(1)}, f32[4096]{0:T(1024)}, u32[]{:S(2)}) copy-start(f32[4096]{0:T(1024)} %param.8) | copy-start | bytes 49156
  330.0 71.5 %all-to-all-start.2 = ((bf16[16,512,128]{2,1,0:T(8,128)(2,1)}), bf16[16,512,128]{2,1,0:T(8,128)(2,1)S(1)}, u32[]{:S(2)}, u32[]{:S(2)}) async-start(bf16[16,512,128]{2,1,0:T(8,128)(2,1)} %copy-done.2), calls=%async_computation.2 | async-start | bytes 4194304 | tf_op jit(solution)/shard_map/all_to_all | solution.py:349
  342.2 65.3 %collective-permute-start.1 = (bf16[512,2048]{1,0:T(8,128)(2,1)}, bf16[512,2048]{1,0:T(8,128)(2,1)}, u32[]{:S(2)}, u32[]{:S(2)}) collective-permute-start(bf16[512,2048]{1,0:T(8,128)(2,1)} %gate.3.refs_2_), channel_id=1, source_target_pairs={{0,1},{1,0},{2,3},{3,2},{4,5},{5,4},{6,7},{7,6},{8,9},{9,8},{10,11... | collective-permute-start | bytes 6291464 | tf_op jit(solution)/shard_map/ppermute | solution.py:355
  406.2 46.9 %collective-permute-start = (bf16[512,2048]{1,0:T(8,128)(2,1)}, bf16[512,2048]{1,0:T(8,128)(2,1)S(1)}, u32[]{:S(2)}, u32[]{:S(2)}) collective-permute-start(bf16[512,2048]{1,0:T(8,128)(2,1)} %gate.2.refs_0_), channel_id=1, source_target_pairs={{0,1},{1,0},{2,3},{3,2},{4,5},{5,4},{6,7},{7,6},{8,9},{9,8},{10,11... | collective-permute-start | bytes 6291464 | tf_op jit(solution)/shard_map/ppermute | solution.py:355
  571.1 24.8 %copy-start.1 = (s32[32,32]{1,0:T(8,128)S(1)}, s32[32,32]{1,0:T(8,128)}, u32[]{:S(2)}) copy-start(s32[32,32]{1,0:T(8,128)} %param.10) | copy-start | bytes 12292
Sparse Core Ops, SparseCore 0:
  11.5 390.8 all-gather.4
  404.0 167.0 all-gather.2

commit v5 on v4

--- a/solution.py
+++ b/solution.py
@@ -296,6 +296,54 @@
     )(starts, *hidden, weight, *before)
 
 
+def pair_kernel(pieces, place_ref, *refs):
+    a_ref, b_ref, out_ref, total_ref = refs[pieces : pieces + 4]
+    step = pl.program_id(1)
+    columns = a_ref.shape[1]
+    tile = min(256, columns)
+    for k in range(pieces):
+        for place, w_ref in enumerate((a_ref, b_ref)):
+
+            @pl.when(jnp.logical_and(step == k, place_ref[2 * pieces + k] == place))
+            def _(k=k, w_ref=w_ref):
+                for low in range(0, columns, tile):
+                    lanes = slice(low, low + tile)
+                    part = jnp.dot(refs[k][...], w_ref[:, lanes], preferred_element_type=F32)
+                    if k:
+                        part = total_ref[:, lanes] + part
+                    if k < pieces - 1:
+                        total_ref[:, lanes] = part
+                    else:
+                        out_ref[:, lanes] = part.astype(BF16)
+
+
+def mix_pair(hidden, places, weights, columns):
+    tokens, width = hidden[0].shape
+    depth, part = weights[0].shape
+    tile = min(512, part)
+    pieces = len(hidden)
+    return pl.pallas_call(
+        functools.partial(pair_kernel, pieces),
+        grid_spec=pltpu.PrefetchScalarGridSpec(
+            num_scalar_prefetch=1,
+            grid=(part // tile, pieces),
+            in_specs=[pl.BlockSpec(h.shape, lambda i, k, s: (0, 0)) for h in hidden]
+            + [
+                pl.BlockSpec((width, tile), lambda i, k, s: (s[k], i)),
+                pl.BlockSpec((width, tile), lambda i, k, s: (s[pieces + k], i)),
+            ],
+            out_specs=pl.BlockSpec((tokens, tile), lambda i, k, s: (0, i)),
+            scratch_shapes=[pltpu.VMEM((tokens, tile), F32)],
+        ),
+        out_shape=jax.ShapeDtypeStruct((tokens, columns), BF16),
+        compiler_params=pltpu.CompilerParams(vmem_limit_bytes=VMEM),
+        cost_estimate=pl.CostEstimate(
+            flops=4 * tokens * depth * part, bytes_accessed=4 * depth * part, transcendentals=0
+        ),
+        name="mix_pair",
+    )(places, *hidden, *weights)
+
+
 def body(keyval, gating, skip_gain, filter_values, blocks, out_weight):
     cycle = lax.axis_size("seq")
     place = lax.axis_index("seq")
@@ -310,12 +358,19 @@
     chunks = narrow // unit
 
     columns = out_weight.shape[1]
-    eighth = columns // 8
-    bounds = [0, 4 * eighth, columns] if eighth % 256 == 0 else [0, columns]
-    weights = [
-        lax.all_gather(out_weight[:, low:high], "seq", axis=0, tiled=True)
-        for low, high in zip(bounds[:-1], bounds[1:])
-    ]
+    half = cycle // 2
+    width = cycle * unit
+    paired = columns % 2048 == 0 and peers == 2 and half * out_weight.shape[0] == channels
+    cut = columns // 2 if paired else 0
+    if paired:
+        sides = [list(range(half)), list(range(half, cycle))]
+        gather = functools.partial(
+            lax.all_gather, axis_name="seq", axis=0, tiled=True, axis_index_groups=sides
+        )
+        own = out_weight[:, :cut]
+        other = lax.ppermute(own, "seq", [(i, (i + half) % cycle) for i in range(cycle)])
+        pair = [gather(own), gather(other)]
+    weight = lax.all_gather(out_weight[:, cut:], "seq", axis=0, tiled=True)
 
     exchange = functools.partial(
         lax.all_to_all, axis_name="seq", split_axis=0, concat_axis=0, tiled=True
@@ -358,11 +413,14 @@
             hidden.append(piece)
             source = lax.rem(side + peers - shift, peers)
             starts.append(source * chunks + g)
+    result = None
+    if paired:
+        which = [(place // half + side + shift) % 2 for g in range(chunks) for shift in range(2)]
+        rows = [jnp.full((), g, jnp.int32) for g in range(chunks) for shift in range(2)]
+        places = jnp.stack(rows + rows + which).astype(jnp.int32)
+        result = mix_pair(hidden, places, pair, columns)
     starts = jnp.stack(starts).astype(jnp.int32)
-    result = None
-    for low, weight in zip(bounds[:-1], weights):
-        result = mix(hidden, starts, weight, low, columns, result)
-    return result
+    return mix(hidden, starts, weight, cut, columns, result)
 
 
 def solution(mesh):

time: 605 us -> 606 us (level)
  waiting for transfers between devices: 417 us -> 405 us
  Pallas kernels: 117 us -> 126 us
    ppermute x0 -> x1, waiting for transfers between devices: none -> 90.2 us  [body(): lax.ppermute(own, 'seq', [(i, (i + half) % cycle) for i in range(cycle)])]
    all_gather x2 -> x3, waiting for transfers between devices: 92.8 us -> 21.4 us  [the longest x1 21.4 us: body(): weight = lax.all_gather(out_weight[:, cut:], 'seq', axis=0, tiled=True)]
    pallas_call x0 -> x1, Pallas kernels: none -> 34.2 us  [mix_pair(): pl.pallas_call(functools.partial(pair_kernel, pieces), grid_spec=pltpu.Pr...]
    pallas_call x2 -> x1, Pallas kernels: 50 us -> 24.8 us  [mix(): pl.pallas_call(functools.partial(mix_kernel, pieces), grid_spec=pltpu.Pre...]
    all_to_all x1, waiting for transfers between devices: 65.9 us -> 42 us  [body(): filters = exchange(pack_filters(filter_values, cycle, chunks, unit))]
    all_to_all x2, waiting for transfers between devices: 108 us -> 97.4 us  [body(): exchange(pack_signal(keyval, g, cycle, unit))]
  transfers between devices with their start and end apart: 9 -> 11, of which waited for: 7 -> 8; matrix products, arithmetic and copies ran while one was open for 1% -> 1% of each run, Pallas kernels for 15% -> 17%
where the time goes in v5:
time: 606 us; the launch traced here: 605 us
  waiting for transfers between devices  405 us (67%)
  Pallas kernels  126 us (21%)
  starting transfers between devices  43.8 us (7%)
  between operations  13.2 us (2%)
  local copies, waits for them, and re-layouts  11.5 us (2%)
    all_to_all x2, waiting for transfers between devices, body(): done = exchange(convolve(g, twist, ahead, back, signals[g], filters))  109 us
    all_to_all x2, waiting for transfers between devices, body(): exchange(pack_signal(keyval, g, cycle, unit))  97.4 us
    ppermute x1, waiting for transfers between devices, body(): lax.ppermute(own, 'seq', [(i, (i + half) % cycle) for i in range(cycle)])  90.2 us
    ppermute x2, waiting for transfers between devices, body(): lax.ppermute(own, 'tensor', [(t, (t + shift) % peers) for t in range(peer...  45.1 us
    all_to_all x1, waiting for transfers between devices, body(): filters = exchange(pack_filters(filter_values, cycle, chunks, unit))  42 us
    pallas_call x2, Pallas kernels, convolve(): pl.pallas_call(conv_kernel, grid=(1,), out_shape=jax.ShapeDtypeStruct(sig...  41.1 us
    pallas_call x1, Pallas kernels, mix_pair(): pl.pallas_call(functools.partial(pair_kernel, pieces), grid_spec=pltpu.Pr...  34.2 us
    pallas_call x1, Pallas kernels, mix(): pl.pallas_call(functools.partial(mix_kernel, pieces), grid_spec=pltpu.Pre...  24.8 us
  transfers between devices with their start and end apart: 11, of which 8 were waited for; matrix products, arithmetic and copies ran while one was open for 1% of the time, Pallas kernels for 17%

profile of v5, /device:TPU:9, one launch (start us, length us, event | category | flops | bytes accessed | tf_op | source)
XLA Modules:
  0.0 605.0 jit_solution(3271837026509763294)
XLA Ops:
  6.5 4.8 fusion.25
  11.4 0.0 all-gather.6.cloned.1.call-update
  11.4 0.0 all-gather.8.cloned.1.call-start
  11.4 1.5 copy-done.6
  13.0 2.3 collective-permute-start.2
  15.3 90.2 %collective-permute-done.2 = bf16[512,2048]{1,0:T(8,128)(2,1)} collective-permute-done((bf16[512,2048]{1,0:T(8,128)(2,1)S(1)}, bf16[512,2048]{1,0:T(8,128)(2,1)}, u32[]{:S(2)}, u32[]{:S(2)}) %collective-permute-start.2) | collective-permute-done | bytes 2097184 | tf_op jit(solution)/shard_map/ppermute | solution.py:371
  105.4 0.0 all-gather.8.cloned.1.call-update
  105.5 0.0 all-gather.4.cloned.1.call-start
  105.5 0.7 all-gather.4.cloned.1.call-update
  106.2 8.0 %pack_filters.1 = bf16[16,2,256,128]{3,2,1,0:T(8,128)(2,1)} custom-call(f32[256,1,4096]{2,1,0:T(1,128)} %bitcast.12), custom_call_target="tpu_custom_call" | custom-call | bytes 6291456 | tf_op jit(solution)/shard_map/pack_filters/pallas_call | solution.py:205
  114.2 7.4 %all-to-all-start.1 = ((bf16[16,2,256,128]{3,2,1,0:T(8,128)(2,1)}), bf16[16,2,256,128]{3,2,1,0:T(8,128)(2,1)S(1)}, u32[]{:S(2)}, u32[]{:S(2)}) async-start(bf16[16,2,256,128]{3,2,1,0:T(8,128)(2,1)} %pack_filters.1), calls=%async_computation.1 | async-start | bytes 4194304 | tf_op jit(solution)/shard_map/all_to_all | solution.py:379
  121.7 4.0 pack_signal.3
  125.6 42.0 %all-to-all-done.1.filter_ref = bf16[16,2,256,128]{3,2,1,0:T(8,128)(2,1)S(1)} async-done(((bf16[16,2,256,128]{3,2,1,0:T(8,128)(2,1)}), bf16[16,2,256,128]{3,2,1,0:T(8,128)(2,1)S(1)}, u32[]{:S(2)}, u32[]{:S(2)}) %all-to-all-start.1) | async-done | bytes 2097184 | tf_op jit(solution)/shard_map/all_to_all | solution.py:379
  167.6 1.4 copy-done.5
  169.0 7.1 %all-to-all-start.3 = ((bf16[16,512,128]{2,1,0:T(8,128)(2,1)}), bf16[16,512,128]{2,1,0:T(8,128)(2,1)}, u32[]{:S(2)}, u32[]{:S(2)}) async-start(bf16[16,512,128]{2,1,0:T(8,128)(2,1)} %pack_signal.3), calls=%async_computation.3 | async-start | bytes 4194304 | tf_op jit(solution)/shard_map/all_to_all | solution.py:378
  176.1 3.9 pack_signal.2
  180.0 57.0 %all-to-all-done.3.x_ref = bf16[16,512,128]{2,1,0:T(8,128)(2,1)} async-done(((bf16[16,512,128]{2,1,0:T(8,128)(2,1)}), bf16[16,512,128]{2,1,0:T(8,128)(2,1)}, u32[]{:S(2)}, u32[]{:S(2)}) %all-to-all-start.3) | async-done | bytes 2097184 | tf_op jit(solution)/shard_map/all_to_all | solution.py:378
  236.9 7.9 %all-to-all-start = ((bf16[16,512,128]{2,1,0:T(8,128)(2,1)}), bf16[16,512,128]{2,1,0:T(8,128)(2,1)}, u32[]{:S(2)}, u32[]{:S(2)}) async-start(bf16[16,512,128]{2,1,0:T(8,128)(2,1)} %pack_signal.2), calls=%async_computation | async-start | bytes 4194304 | tf_op jit(solution)/shard_map/all_to_all | solution.py:378
  244.9 0.6 gather_fusion
  245.5 0.1 select_multiply_fusion
  245.5 0.1 add.136
  245.6 0.1 add.137
  245.7 0.1 add.139
  245.8 0.1 fusion.22
  246.0 0.1 copy.8.twist_ref
  246.1 2.3 negate_convert_fusion
  248.4 0.1 maximum_maximum_fusion.1.back_ref
  248.5 2.5 fusion.15
  251.0 0.1 maximum_maximum_fusion.ahead_ref
  251.1 20.6 %convolve.3 = bf16[16,512,128]{2,1,0:T(8,128)(2,1)S(1)} custom-call(f32[512,32]{1,0:T(8,128)S(1)} %copy.8.twist_ref, bf16[2,256,1024]{2,1,0:T(8,128)(2,1)S(1)} %maximum_maximum_fusion.ahead_ref, bf16[2,1024,256]{2,1,0:T(8,128)(2,1)S(1)} %maximum_maximum_fusion.1.back_ref, bf16[16,512,128]{2,1,0:T(8,128)(2,1)} %all-to-all-done.3.x_ref, ...), custom_call_target="tpu_custom_call" | custom-call | flops 2147483648 | bytes 16777216 | tf_op jit(solution)/shard_map/convolve/pallas_call | solution.py:147
  271.7 1.4 copy-done.3
  273.1 40.4 %all-to-all-done.x_ref = bf16[16,512,128]{2,1,0:T(8,128)(2,1)} async-done(((bf16[16,512,128]{2,1,0:T(8,128)(2,1)}), bf16[16,512,128]{2,1,0:T(8,128)(2,1)}, u32[]{:S(2)}, u32[]{:S(2)}) %all-to-all-start) | async-done | bytes 2097184 | tf_op jit(solution)/shard_map/all_to_all | solution.py:378
  313.5 7.8 %all-to-all-start.4 = ((bf16[16,512,128]{2,1,0:T(8,128)(2,1)}), bf16[16,512,128]{2,1,0:T(8,128)(2,1)}, u32[]{:S(2)}, u32[]{:S(2)}) async-start(bf16[16,512,128]{2,1,0:T(8,128)(2,1)} %copy-done.3), calls=%async_computation.4 | async-start | bytes 4194304 | tf_op jit(solution)/shard_map/all_to_all | solution.py:404
  321.3 20.5 %convolve.2 = bf16[16,512,128]{2,1,0:T(8,128)(2,1)S(1)} custom-call(f32[512,32]{1,0:T(8,128)S(1)} %copy.8.twist_ref, bf16[2,256,1024]{2,1,0:T(8,128)(2,1)S(1)} %maximum_maximum_fusion.ahead_ref, bf16[2,1024,256]{2,1,0:T(8,128)(2,1)S(1)} %maximum_maximum_fusion.1.back_ref, bf16[16,512,128]{2,1,0:T(8,128)(2,1)} %all-to-all-done.x_ref, ...), custom_call_target="tpu_custom_call" | custom-call | flops 2147483648 | bytes 16777216 | tf_op jit(solution)/shard_map/convolve/pallas_call | solution.py:147
  341.9 1.3 copy-done.2
  343.2 45.3 %all-to-all-done.4.c_ref = bf16[16,512,128]{2,1,0:T(8,128)(2,1)} async-done(((bf16[16,512,128]{2,1,0:T(8,128)(2,1)}), bf16[16,512,128]{2,1,0:T(8,128)(2,1)}, u32[]{:S(2)}, u32[]{:S(2)}) %all-to-all-start.4) | async-done | bytes 2097184 | tf_op jit(solution)/shard_map/all_to_all | solution.py:404
  388.5 8.6 %all-to-all-start.2 = ((bf16[16,512,128]{2,1,0:T(8,128)(2,1)}), bf16[16,512,128]{2,1,0:T(8,128)(2,1)S(1)}, u32[]{:S(2)}, u32[]{:S(2)}) async-start(bf16[16,512,128]{2,1,0:T(8,128)(2,1)} %copy-done.2), calls=%async_computation.2 | async-start | bytes 4194304 | tf_op jit(solution)/shard_map/all_to_all | solution.py:404
  397.1 5.2 gate.3.refs_2_
  402.3 1.3 collective-permute-start.1
  403.6 63.3 %all-to-all-done.2.c_ref = bf16[16,512,128]{2,1,0:T(8,128)(2,1)S(1)} async-done(((bf16[16,512,128]{2,1,0:T(8,128)(2,1)}), bf16[16,512,128]{2,1,0:T(8,128)(2,1)S(1)}, u32[]{:S(2)}, u32[]{:S(2)}) %all-to-all-start.2) | async-done | bytes 2097184 | tf_op jit(solution)/shard_map/all_to_all | solution.py:404
  466.9 4.6 gate.2.refs_0_
  471.5 1.2 collective-permute-start
  472.8 0.1 stack.33.place_ref
  472.9 0.1 pad_add_fusion.start_ref
  472.9 45.1 %collective-permute-done.refs_1_ = bf16[512,2048]{1,0:T(8,128)(2,1)S(1)} collective-permute-done((bf16[512,2048]{1,0:T(8,128)(2,1)}, bf16[512,2048]{1,0:T(8,128)(2,1)S(1)}, u32[]{:S(2)}, u32[]{:S(2)}) %collective-permute-start) | collective-permute-done | bytes 2097184 | tf_op jit(solution)/shard_map/ppermute | solution.py:410
  518.1 34.2 %mix_pair.1.refs_5_ = bf16[512,4096]{1,0:T(8,128)(2,1)} custom-call(s32[12]{0:T(128)S(1)} %stack.33.place_ref, bf16[512,2048]{1,0:T(8,128)(2,1)} %gate.2.refs_0_, bf16[512,2048]{1,0:T(8,128)(2,1)S(1)} %collective-permute-done.refs_1_, bf16[512,2048]{1,0:T(8,128)(2,1)} %gate.3.refs_2_, bf16[512,2048]{1,0:T(8,128)(2,1)} %collective-permute-done.1.refs_3_, ...), custom_call_target="tpu_custom_call" | custom-call | flops 17179869184 | bytes 33554432 | tf_op jit(solution)/shard_map/mix_pair/pallas_call | solution.py:325
  552.2 21.4 %all-gather.4.cloned.1.call-done.refs_4_ = bf16[8192,2048]{1,0:T(8,128)(2,1)} async-done(((bf16[512,2048]{1,0:T(8,128)(2,1)}), bf16[8192,2048]{1,0:T(8,128)(2,1)}) %all-gather.4.cloned.1.call-update) | async-done | bytes 33554448 | tf_op jit(solution)/shard_map/all_gather | solution.py:373
  573.6 24.8 %mix.1 = bf16[512,4096]{1,0:T(8,128)(2,1)} custom-call(s32[4]{0:T(128)S(1)} %pad_add_fusion.start_ref, bf16[512,2048]{1,0:T(8,128)(2,1)} %gate.2.refs_0_, bf16[512,2048]{1,0:T(8,128)(2,1)S(1)} %collective-permute-done.refs_1_, bf16[512,2048]{1,0:T(8,128)(2,1)} %gate.3.refs_2_, ...), custom_call_target="tpu_custom_call", output_to_operand_aliasing={{}: (6, {})} | custom-call | flops 17179869184 | bytes 33554432 | tf_op jit(solution)/shard_map/mix/pallas_call | solution.py:278
  (22 shorter events, 0.1 us)
Async XLA Ops:
  6.5 238.3 %copy-start = (s32[32,32]{1,0:T(8,128)S(1)}, s32[32,32]{1,0:T(8,128)}, u32[]{:S(2)}) copy-start(s32[32,32]{1,0:T(8,128)} %param.10) | copy-start | bytes 12292
  6.5 511.5 %all-gather.6.cloned.1.call-start = ((), (), s32[]{:S(2)}) async-start(), calls=%async_computation.6 | async-start | bytes 18874368 | tf_op jit(solution)/shard_map/all_gather | solution.py:372
  11.4 1.6 copy-start.6
  11.4 506.7 %all-gather.8.cloned.1.call-start = ((), (), s32[]{:S(2)}) async-start(), calls=%async_computation.7 | async-start | bytes 18874368 | tf_op jit(solution)/shard_map/all_gather | solution.py:372
  13.0 92.5 %collective-permute-start.2 = (bf16[512,2048]{1,0:T(8,128)(2,1)S(1)}, bf16[512,2048]{1,0:T(8,128)(2,1)}, u32[]{:S(2)}, u32[]{:S(2)}) collective-permute-start(bf16[512,2048]{1,0:T(8,128)(2,1)S(1)} %copy-done.6), channel_id=1, source_target_pairs={{0,16},{2,18},{4,20},{6,22},{8,24},{10,26},{12,28},{14,30},{16,0},... | collective-permute-start | bytes 6291464 | tf_op jit(solution)/shard_map/ppermute | solution.py:371
  105.5 468.1 %all-gather.4.cloned.1.call-start = ((), (), s32[]{:S(2)}) async-start(), calls=%async_computation.5 | async-start | bytes 35651584 | tf_op jit(solution)/shard_map/all_gather | solution.py:373
  114.2 53.4 %all-to-all-start.1 = ((bf16[16,2,256,128]{3,2,1,0:T(8,128)(2,1)}), bf16[16,2,256,128]{3,2,1,0:T(8,128)(2,1)S(1)}, u32[]{:S(2)}, u32[]{:S(2)}) async-start(bf16[16,2,256,128]{3,2,1,0:T(8,128)(2,1)} %pack_filters.1), calls=%async_computation.1 | async-start | bytes 4194304 | tf_op jit(solution)/shard_map/all_to_all | solution.py:379
  167.6 1.4 copy-start.5
  169.0 68.0 %all-to-all-start.3 = ((bf16[16,512,128]{2,1,0:T(8,128)(2,1)}), bf16[16,512,128]{2,1,0:T(8,128)(2,1)}, u32[]{:S(2)}, u32[]{:S(2)}) async-start(bf16[16,512,128]{2,1,0:T(8,128)(2,1)} %pack_signal.3), calls=%async_computation.3 | async-start | bytes 4194304 | tf_op jit(solution)/shard_map/all_to_all | solution.py:378
  236.9 76.6 %all-to-all-start = ((bf16[16,512,128]{2,1,0:T(8,128)(2,1)}), bf16[16,512,128]{2,1,0:T(8,128)(2,1)}, u32[]{:S(2)}, u32[]{:S(2)}) async-start(bf16[16,512,128]{2,1,0:T(8,128)(2,1)} %pack_signal.2), calls=%async_computation | async-start | bytes 4194304 | tf_op jit(solution)/shard_map/all_to_all | solution.py:378
  271.7 1.4 copy-start.3
  313.5 75.0 %all-to-all-start.4 = ((bf16[16,512,128]{2,1,0:T(8,128)(2,1)}), bf16[16,512,128]{2,1,0:T(8,128)(2,1)}, u32[]{:S(2)}, u32[]{:S(2)}) async-start(bf16[16,512,128]{2,1,0:T(8,128)(2,1)} %copy-done.3), calls=%async_computation.4 | async-start | bytes 4194304 | tf_op jit(solution)/shard_map/all_to_all | solution.py:404
  341.9 1.3 copy-start.2
  343.2 53.9 %copy-start.4 = (f32[4096]{0:T(1024)S(1)}, f32[4096]{0:T(1024)}, u32[]{:S(2)}) copy-start(f32[4096]{0:T(1024)} %param.8) | copy-start | bytes 49156
  388.5 78.4 %all-to-all-start.2 = ((bf16[16,512,128]{2,1,0:T(8,128)(2,1)}), bf16[16,512,128]{2,1,0:T(8,128)(2,1)S(1)}, u32[]{:S(2)}, u32[]{:S(2)}) async-start(bf16[16,512,128]{2,1,0:T(8,128)(2,1)} %copy-done.2), calls=%async_computation.2 | async-start | bytes 4194304 | tf_op jit(solution)/shard_map/all_to_all | solution.py:404
  402.3 70.6 %collective-permute-start.1 = (bf16[512,2048]{1,0:T(8,128)(2,1)}, bf16[512,2048]{1,0:T(8,128)(2,1)}, u32[]{:S(2)}, u32[]{:S(2)}) collective-permute-start(bf16[512,2048]{1,0:T(8,128)(2,1)} %gate.3.refs_2_), channel_id=1, source_target_pairs={{0,1},{1,0},{2,3},{3,2},{4,5},{5,4},{6,7},{7,6},{8,9},{9,8},{10,11... | collective-permute-start | bytes 6291464 | tf_op jit(solution)/shard_map/ppermute | solution.py:410
  471.5 46.5 %collective-permute-start = (bf16[512,2048]{1,0:T(8,128)(2,1)}, bf16[512,2048]{1,0:T(8,128)(2,1)S(1)}, u32[]{:S(2)}, u32[]{:S(2)}) collective-permute-start(bf16[512,2048]{1,0:T(8,128)(2,1)} %gate.2.refs_0_), channel_id=1, source_target_pairs={{0,1},{1,0},{2,3},{3,2},{4,5},{5,4},{6,7},{7,6},{8,9},{9,8},{10,11... | collective-permute-start | bytes 6291464 | tf_op jit(solution)/shard_map/ppermute | solution.py:410
  573.6 24.8 %copy-start.1 = (s32[32,32]{1,0:T(8,128)S(1)}, s32[32,32]{1,0:T(8,128)}, u32[]{:S(2)}) copy-start(s32[32,32]{1,0:T(8,128)} %param.10) | copy-start | bytes 12292
Sparse Core Ops, SparseCore 0:
  11.5 156.4 all-gather.5
  169.6 143.5 all-gather.7
  314.8 258.7 all-gather.3

commit v6 on v5

--- a/solution.py
+++ b/solution.py
@@ -320,7 +320,7 @@
 def mix_pair(hidden, places, weights, columns):
     tokens, width = hidden[0].shape
     depth, part = weights[0].shape
-    tile = min(512, part)
+    tile = min(1024, part)
     pieces = len(hidden)
     return pl.pallas_call(
         functools.partial(pair_kernel, pieces),
@@ -357,6 +357,7 @@
     unit = min(narrow, group_width)
     chunks = narrow // unit
 
+    packed_filters = pack_filters(filter_values, cycle, chunks, unit)
     columns = out_weight.shape[1]
     half = cycle // 2
     width = cycle * unit
@@ -368,15 +369,16 @@
             lax.all_gather, axis_name="seq", axis=0, tiled=True, axis_index_groups=sides
         )
         own = out_weight[:, :cut]
-        other = lax.ppermute(own, "seq", [(i, (i + half) % cycle) for i in range(cycle)])
+        sent, packed_filters = lax.optimization_barrier((own, packed_filters))
+        other = lax.ppermute(sent, "seq", [(i, (i + half) % cycle) for i in range(cycle)])
         pair = [gather(own), gather(other)]
     weight = lax.all_gather(out_weight[:, cut:], "seq", axis=0, tiled=True)
 
     exchange = functools.partial(
         lax.all_to_all, axis_name="seq", split_axis=0, concat_axis=0, tiled=True
     )
+    filters = exchange(packed_filters)
     signals = [exchange(pack_signal(keyval, g, cycle, unit)) for g in range(chunks)]
-    filters = exchange(pack_filters(filter_values, cycle, chunks, unit))
 
     group = (jnp.arange(chunks, dtype=jnp.int32) * cycle + place) * unit // group_width
     kept_blocks = jnp.take(blocks, group, axis=0)

time: 606 us -> 607 us (level)
  transfers between devices with their start and end apart: 11 -> 11, of which waited for: 8 -> 8; matrix products, arithmetic and copies ran while one was open for 1% -> 1% of each run, Pallas kernels for 17% -> 16%
where the time goes in v6:
time: 607 us
  waiting for transfers between devices  411 us (68%)
  Pallas kernels  123 us (20%)
  starting transfers between devices  42.7 us (7%)
  between operations  13.3 us (2%)
  local copies, waits for them, and re-layouts  11.3 us (2%)
    all_to_all x2, waiting for transfers between devices, body(): done = exchange(convolve(g, twist, ahead, back, signals[g], filters))  108 us
    all_to_all x2, waiting for transfers between devices, body(): exchange(pack_signal(keyval, g, cycle, unit))  97.3 us
    ppermute x1, waiting for transfers between devices, body(): lax.ppermute(sent, 'seq', [(i, (i + half) % cycle) for i in range(cycle)])  90 us
    ppermute x2, waiting for transfers between devices, body(): lax.ppermute(own, 'tensor', [(t, (t + shift) % peers) for t in range(peer...  45.1 us
    all_to_all x1, waiting for transfers between devices, body(): filters = exchange(packed_filters)  44.8 us
    pallas_call x2, Pallas kernels, convolve(): pl.pallas_call(conv_kernel, grid=(1,), out_shape=jax.ShapeDtypeStruct(sig...  41.1 us
    pallas_call x1, Pallas kernels, mix_pair(): pl.pallas_call(functools.partial(pair_kernel, pieces), grid_spec=pltpu.Pr...  30.5 us
    all_gather x1, waiting for transfers between devices, body(): weight = lax.all_gather(out_weight[:, cut:], 'seq', axis=0, tiled=True)  25.1 us
  transfers between devices with their start and end apart: 11, of which 8 were waited for; matrix products, arithmetic and copies ran while one was open for 1% of the time, Pallas kernels for 16%

profile of v6, /device:TPU:9, one launch (start us, length us, event | category | flops | bytes accessed | tf_op | source)
XLA Modules:
  0.0 606.6 jit_solution(17739097316478546420)
XLA Ops:
  6.5 4.8 fusion.25
  11.3 0.0 all-gather.6.cloned.1.call-update
  11.4 0.0 all-gather.8.cloned.1.call-start
  11.4 8.2 %pack_filters.1 = bf16[16,2,256,128]{3,2,1,0:T(8,128)(2,1)} custom-call(f32[256,1,4096]{2,1,0:T(1,128)} %bitcast.12), custom_call_target="tpu_custom_call" | custom-call | bytes 6291456 | tf_op jit(solution)/shard_map/pack_filters/pallas_call | solution.py:205
  19.6 2.3 collective-permute-start.2
  21.9 90.0 %collective-permute-done.2 = bf16[512,2048]{1,0:T(8,128)(2,1)S(1)} collective-permute-done((bf16[512,2048]{1,0:T(8,128)(2,1)S(1)}, bf16[512,2048]{1,0:T(8,128)(2,1)S(1)}, u32[]{:S(2)}, u32[]{:S(2)}) %collective-permute-start.2) | collective-permute-done | bytes 2097184 | tf_op jit(solution)/shard_map/ppermute | solution.py:373
  112.0 1.4 copy-done.7
  113.3 0.0 all-gather.8.cloned.1.call-update
  113.3 0.0 all-gather.4.cloned.1.call-start
  113.4 0.7 all-gather.4.cloned.1.call-update
  114.1 7.4 %all-to-all-start.1 = ((bf16[16,2,256,128]{3,2,1,0:T(8,128)(2,1)}), bf16[16,2,256,128]{3,2,1,0:T(8,128)(2,1)S(1)}, u32[]{:S(2)}, u32[]{:S(2)}) async-start(bf16[16,2,256,128]{3,2,1,0:T(8,128)(2,1)} %pack_filters.1), calls=%async_computation.1 | async-start | bytes 4194304 | tf_op jit(solution)/shard_map/all_to_all | solution.py:380
  121.4 4.0 pack_signal.3
  125.4 44.8 %all-to-all-done.1.filter_ref = bf16[16,2,256,128]{3,2,1,0:T(8,128)(2,1)S(1)} async-done(((bf16[16,2,256,128]{3,2,1,0:T(8,128)(2,1)}), bf16[16,2,256,128]{3,2,1,0:T(8,128)(2,1)S(1)}, u32[]{:S(2)}, u32[]{:S(2)}) %all-to-all-start.1) | async-done | bytes 2097184 | tf_op jit(solution)/shard_map/all_to_all | solution.py:380
  170.2 1.4 copy-done.5
  171.6 5.9 all-to-all-start.3
  177.5 3.9 pack_signal.2
  181.3 58.3 %all-to-all-done.3.x_ref = bf16[16,512,128]{2,1,0:T(8,128)(2,1)} async-done(((bf16[16,512,128]{2,1,0:T(8,128)(2,1)}), bf16[16,512,128]{2,1,0:T(8,128)(2,1)}, u32[]{:S(2)}, u32[]{:S(2)}) %all-to-all-start.3) | async-done | bytes 2097184 | tf_op jit(solution)/shard_map/all_to_all | solution.py:381
  239.6 8.0 %all-to-all-start = ((bf16[16,512,128]{2,1,0:T(8,128)(2,1)}), bf16[16,512,128]{2,1,0:T(8,128)(2,1)}, u32[]{:S(2)}, u32[]{:S(2)}) async-start(bf16[16,512,128]{2,1,0:T(8,128)(2,1)} %pack_signal.2), calls=%async_computation | async-start | bytes 4194304 | tf_op jit(solution)/shard_map/all_to_all | solution.py:381
  247.7 0.6 gather_fusion
  248.3 0.1 select_multiply_fusion
  248.4 0.1 add.136
  248.4 0.1 add.137
  248.6 0.1 add.139
  248.7 0.1 fusion.22
  248.8 0.1 copy.8.twist_ref
  249.0 2.3 negate_convert_fusion
  251.2 0.1 maximum_maximum_fusion.1.back_ref
  251.4 2.5 fusion.15
  253.8 0.1 maximum_maximum_fusion.ahead_ref
  254.0 20.5 %convolve.3 = bf16[16,512,128]{2,1,0:T(8,128)(2,1)S(1)} custom-call(f32[512,32]{1,0:T(8,128)S(1)} %copy.8.twist_ref, bf16[2,256,1024]{2,1,0:T(8,128)(2,1)S(1)} %maximum_maximum_fusion.ahead_ref, bf16[2,1024,256]{2,1,0:T(8,128)(2,1)S(1)} %maximum_maximum_fusion.1.back_ref, bf16[16,512,128]{2,1,0:T(8,128)(2,1)} %all-to-all-done.3.x_ref, ...), custom_call_target="tpu_custom_call" | custom-call | flops 2147483648 | bytes 16777216 | tf_op jit(solution)/shard_map/convolve/pallas_call | solution.py:147
  274.5 1.3 copy-done.3
  275.9 39.0 %all-to-all-done.x_ref = bf16[16,512,128]{2,1,0:T(8,128)(2,1)} async-done(((bf16[16,512,128]{2,1,0:T(8,128)(2,1)}), bf16[16,512,128]{2,1,0:T(8,128)(2,1)}, u32[]{:S(2)}, u32[]{:S(2)}) %all-to-all-start) | async-done | bytes 2097184 | tf_op jit(solution)/shard_map/all_to_all | solution.py:381
  314.9 7.9 %all-to-all-start.4 = ((bf16[16,512,128]{2,1,0:T(8,128)(2,1)}), bf16[16,512,128]{2,1,0:T(8,128)(2,1)}, u32[]{:S(2)}, u32[]{:S(2)}) async-start(bf16[16,512,128]{2,1,0:T(8,128)(2,1)} %copy-done.3), calls=%async_computation.4 | async-start | bytes 4194304 | tf_op jit(solution)/shard_map/all_to_all | solution.py:406
  322.7 20.5 %convolve.2 = bf16[16,512,128]{2,1,0:T(8,128)(2,1)S(1)} custom-call(f32[512,32]{1,0:T(8,128)S(1)} %copy.8.twist_ref, bf16[2,256,1024]{2,1,0:T(8,128)(2,1)S(1)} %maximum_maximum_fusion.ahead_ref, bf16[2,1024,256]{2,1,0:T(8,128)(2,1)S(1)} %maximum_maximum_fusion.1.back_ref, bf16[16,512,128]{2,1,0:T(8,128)(2,1)} %all-to-all-done.x_ref, ...), custom_call_target="tpu_custom_call" | custom-call | flops 2147483648 | bytes 16777216 | tf_op jit(solution)/shard_map/convolve/pallas_call | solution.py:147
  343.3 1.3 copy-done.2
  344.6 45.3 %all-to-all-done.4.c_ref = bf16[16,512,128]{2,1,0:T(8,128)(2,1)} async-done(((bf16[16,512,128]{2,1,0:T(8,128)(2,1)}), bf16[16,512,128]{2,1,0:T(8,128)(2,1)}, u32[]{:S(2)}, u32[]{:S(2)}) %all-to-all-start.4) | async-done | bytes 2097184 | tf_op jit(solution)/shard_map/all_to_all | solution.py:406
  389.9 8.6 %all-to-all-start.2 = ((bf16[16,512,128]{2,1,0:T(8,128)(2,1)}), bf16[16,512,128]{2,1,0:T(8,128)(2,1)S(1)}, u32[]{:S(2)}, u32[]{:S(2)}) async-start(bf16[16,512,128]{2,1,0:T(8,128)(2,1)} %copy-done.2), calls=%async_computation.2 | async-start | bytes 4194304 | tf_op jit(solution)/shard_map/all_to_all | solution.py:406
  398.5 5.3 gate.3.refs_2_
  403.7 1.3 collective-permute-start.1
  405.1 63.2 %all-to-all-done.2.c_ref = bf16[16,512,128]{2,1,0:T(8,128)(2,1)S(1)} async-done(((bf16[16,512,128]{2,1,0:T(8,128)(2,1)}), bf16[16,512,128]{2,1,0:T(8,128)(2,1)S(1)}, u32[]{:S(2)}, u32[]{:S(2)}) %all-to-all-start.2) | async-done | bytes 2097184 | tf_op jit(solution)/shard_map/all_to_all | solution.py:406
  468.3 4.6 gate.2.refs_0_
  472.9 1.3 collective-permute-start
  474.2 0.1 stack.33.place_ref
  474.3 0.1 pad_add_fusion.start_ref
  474.4 45.1 %collective-permute-done.refs_1_ = bf16[512,2048]{1,0:T(8,128)(2,1)S(1)} collective-permute-done((bf16[512,2048]{1,0:T(8,128)(2,1)}, bf16[512,2048]{1,0:T(8,128)(2,1)S(1)}, u32[]{:S(2)}, u32[]{:S(2)}) %collective-permute-start) | collective-permute-done | bytes 2097184 | tf_op jit(solution)/shard_map/ppermute | solution.py:412
  519.5 30.5 %mix_pair.1.refs_5_ = bf16[512,4096]{1,0:T(8,128)(2,1)} custom-call(s32[12]{0:T(128)S(1)} %stack.33.place_ref, bf16[512,2048]{1,0:T(8,128)(2,1)} %gate.2.refs_0_, bf16[512,2048]{1,0:T(8,128)(2,1)S(1)} %collective-permute-done.refs_1_, bf16[512,2048]{1,0:T(8,128)(2,1)} %gate.3.refs_2_, bf16[512,2048]{1,0:T(8,128)(2,1)} %collective-permute-done.1.refs_3_, ...), custom_call_target="tpu_custom_call" | custom-call | flops 17179869184 | bytes 33554432 | tf_op jit(solution)/shard_map/mix_pair/pallas_call | solution.py:325
  549.9 25.1 %all-gather.4.cloned.1.call-done.refs_4_ = bf16[8192,2048]{1,0:T(8,128)(2,1)} async-done(((bf16[512,2048]{1,0:T(8,128)(2,1)}), bf16[8192,2048]{1,0:T(8,128)(2,1)}) %all-gather.4.cloned.1.call-update) | async-done | bytes 33554448 | tf_op jit(solution)/shard_map/all_gather | solution.py:375
  575.0 25.1 %mix.1 = bf16[512,4096]{1,0:T(8,128)(2,1)} custom-call(s32[4]{0:T(128)S(1)} %pad_add_fusion.start_ref, bf16[512,2048]{1,0:T(8,128)(2,1)} %gate.2.refs_0_, bf16[512,2048]{1,0:T(8,128)(2,1)S(1)} %collective-permute-done.refs_1_, bf16[512,2048]{1,0:T(8,128)(2,1)} %gate.3.refs_2_, ...), custom_call_target="tpu_custom_call", output_to_operand_aliasing={{}: (6, {})} | custom-call | flops 17179869184 | bytes 33554432 | tf_op jit(solution)/shard_map/mix/pallas_call | solution.py:278
  (24 shorter events, 0.1 us)
Async XLA Ops:
  6.5 241.2 %copy-start = (s32[32,32]{1,0:T(8,128)S(1)}, s32[32,32]{1,0:T(8,128)}, u32[]{:S(2)}) copy-start(s32[32,32]{1,0:T(8,128)} %param.10) | copy-start | bytes 12292
  6.5 512.9 %all-gather.6.cloned.1.call-start = ((), (), s32[]{:S(2)}) async-start(), calls=%async_computation.6 | async-start | bytes 18874368 | tf_op jit(solution)/shard_map/all_gather | solution.py:374
  11.4 508.1 %all-gather.8.cloned.1.call-start = ((), (), s32[]{:S(2)}) async-start(), calls=%async_computation.7 | async-start | bytes 18874368 | tf_op jit(solution)/shard_map/all_gather | solution.py:374
  11.4 8.2 %copy-start.6 = (bf16[512,2048]{1,0:T(8,128)(2,1)S(1)}, bf16[512,2048]{1,0:T(8,128)(2,1)}, u32[]{:S(2)}) copy-start(bf16[512,2048]{1,0:T(8,128)(2,1)} %get-tuple-element.8) | copy-start | bytes 6291460
  19.6 92.3 %collective-permute-start.2 = (bf16[512,2048]{1,0:T(8,128)(2,1)S(1)}, bf16[512,2048]{1,0:T(8,128)(2,1)S(1)}, u32[]{:S(2)}, u32[]{:S(2)}) collective-permute-start(bf16[512,2048]{1,0:T(8,128)(2,1)S(1)} %copy-done.6), channel_id=1, source_target_pairs={{0,16},{2,18},{4,20},{6,22},{8,24},{10,26},{12,28},{14,30},{16,0},... | collective-permute-start | bytes 6291464 | tf_op jit(solution)/shard_map/ppermute | solution.py:373
  112.0 1.4 copy-start.7
  113.3 461.7 %all-gather.4.cloned.1.call-start = ((), (), s32[]{:S(2)}) async-start(), calls=%async_computation.5 | async-start | bytes 35651584 | tf_op jit(solution)/shard_map/all_gather | solution.py:375
  114.1 56.2 %all-to-all-start.1 = ((bf16[16,2,256,128]{3,2,1,0:T(8,128)(2,1)}), bf16[16,2,256,128]{3,2,1,0:T(8,128)(2,1)S(1)}, u32[]{:S(2)}, u32[]{:S(2)}) async-start(bf16[16,2,256,128]{3,2,1,0:T(8,128)(2,1)} %pack_filters.1), calls=%async_computation.1 | async-start | bytes 4194304 | tf_op jit(solution)/shard_map/all_to_all | solution.py:380
  170.2 1.4 copy-start.5
  171.6 68.0 %all-to-all-start.3 = ((bf16[16,512,128]{2,1,0:T(8,128)(2,1)}), bf16[16,512,128]{2,1,0:T(8,128)(2,1)}, u32[]{:S(2)}, u32[]{:S(2)}) async-start(bf16[16,512,128]{2,1,0:T(8,128)(2,1)} %pack_signal.3), calls=%async_computation.3 | async-start | bytes 4194304 | tf_op jit(solution)/shard_map/all_to_all | solution.py:381
  239.6 75.2 %all-to-all-start = ((bf16[16,512,128]{2,1,0:T(8,128)(2,1)}), bf16[16,512,128]{2,1,0:T(8,128)(2,1)}, u32[]{:S(2)}, u32[]{:S(2)}) async-start(bf16[16,512,128]{2,1,0:T(8,128)(2,1)} %pack_signal.2), calls=%async_computation | async-start | bytes 4194304 | tf_op jit(solution)/shard_map/all_to_all | solution.py:381
  274.5 1.4 copy-start.3
  314.9 75.0 %all-to-all-start.4 = ((bf16[16,512,128]{2,1,0:T(8,128)(2,1)}), bf16[16,512,128]{2,1,0:T(8,128)(2,1)}, u32[]{:S(2)}, u32[]{:S(2)}) async-start(bf16[16,512,128]{2,1,0:T(8,128)(2,1)} %copy-done.3), calls=%async_computation.4 | async-start | bytes 4194304 | tf_op jit(solution)/shard_map/all_to_all | solution.py:406
  343.3 1.3 copy-start.2
  344.6 53.9 %copy-start.4 = (f32[4096]{0:T(1024)S(1)}, f32[4096]{0:T(1024)}, u32[]{:S(2)}) copy-start(f32[4096]{0:T(1024)} %param.8) | copy-start | bytes 49156
  389.9 78.4 %all-to-all-start.2 = ((bf16[16,512,128]{2,1,0:T(8,128)(2,1)}), bf16[16,512,128]{2,1,0:T(8,128)(2,1)S(1)}, u32[]{:S(2)}, u32[]{:S(2)}) async-start(bf16[16,512,128]{2,1,0:T(8,128)(2,1)} %copy-done.2), calls=%async_computation.2 | async-start | bytes 4194304 | tf_op jit(solution)/shard_map/all_to_all | solution.py:406
  403.7 70.6 %collective-permute-start.1 = (bf16[512,2048]{1,0:T(8,128)(2,1)}, bf16[512,2048]{1,0:T(8,128)(2,1)}, u32[]{:S(2)}, u32[]{:S(2)}) collective-permute-start(bf16[512,2048]{1,0:T(8,128)(2,1)} %gate.3.refs_2_), channel_id=1, source_target_pairs={{0,1},{1,0},{2,3},{3,2},{4,5},{5,4},{6,7},{7,6},{8,9},{9,8},{10,11... | collective-permute-start | bytes 6291464 | tf_op jit(solution)/shard_map/ppermute | solution.py:412
  472.9 46.5 %collective-permute-start = (bf16[512,2048]{1,0:T(8,128)(2,1)}, bf16[512,2048]{1,0:T(8,128)(2,1)S(1)}, u32[]{:S(2)}, u32[]{:S(2)}) collective-permute-start(bf16[512,2048]{1,0:T(8,128)(2,1)} %gate.2.refs_0_), channel_id=1, source_target_pairs={{0,1},{1,0},{2,3},{3,2},{4,5},{5,4},{6,7},{7,6},{8,9},{9,8},{10,11... | collective-permute-start | bytes 6291464 | tf_op jit(solution)/shard_map/ppermute | solution.py:412
  575.0 25.1 %copy-start.1 = (s32[32,32]{1,0:T(8,128)S(1)}, s32[32,32]{1,0:T(8,128)}, u32[]{:S(2)}) copy-start(s32[32,32]{1,0:T(8,128)} %param.10) | copy-start | bytes 12292
Sparse Core Ops, SparseCore 0:
  11.5 156.3 all-gather.5
  169.5 143.5 all-gather.7
  314.7 260.2 all-gather.3

commit v7 on v6

--- a/solution.py
+++ b/solution.py
@@ -371,13 +371,14 @@
         own = out_weight[:, :cut]
         sent, packed_filters = lax.optimization_barrier((own, packed_filters))
         other = lax.ppermute(sent, "seq", [(i, (i + half) % cycle) for i in range(cycle)])
-        pair = [gather(own), gather(other)]
-    weight = lax.all_gather(out_weight[:, cut:], "seq", axis=0, tiled=True)
-
     exchange = functools.partial(
         lax.all_to_all, axis_name="seq", split_axis=0, concat_axis=0, tiled=True
     )
     filters = exchange(packed_filters)
+    if paired:
+        other, filters = lax.optimization_barrier((other, filters))
+        pair = [gather(own), gather(other)]
+    weight = lax.all_gather(out_weight[:, cut:], "seq", axis=0, tiled=True)
     signals = [exchange(pack_signal(keyval, g, cycle, unit)) for g in range(chunks)]
 
     group = (jnp.arange(chunks, dtype=jnp.int32) * cycle + place) * unit // group_width

time: 607 us -> 613 us (level)
  waiting for transfers between devices: 411 us -> 419 us
    ppermute x1, waiting for transfers between devices: 90 us -> 144 us  [body(): lax.ppermute(sent, 'seq', [(i, (i + half) % cycle) for i in range(cycle)])]
    all_to_all x1, waiting for transfers between devices: 44.8 us -> 0.01 us  [body(): filters = exchange(packed_filters)]
  transfers between devices with their start and end apart: 11 -> 11, of which waited for: 8 -> 7; matrix products, arithmetic and copies ran while one was open for 1% -> 1% of each run, Pallas kernels for 16% -> 16%
where the time goes in v7:
time: 613 us; the launch traced here: 612 us
  waiting for transfers between devices  419 us (68%)
  Pallas kernels  123 us (20%)
  starting transfers between devices  41 us (7%)
  between operations  13.2 us (2%)
  local copies, waits for them, and re-layouts  10.5 us (2%)
    ppermute x1, waiting for transfers between devices, body(): lax.ppermute(sent, 'seq', [(i, (i + half) % cycle) for i in range(cycle)])  144 us
    all_to_all x2, waiting for transfers between devices, body(): done = exchange(convolve(g, twist, ahead, back, signals[g], filters))  109 us
    all_to_all x2, waiting for transfers between devices, body(): exchange(pack_signal(keyval, g, cycle, unit))  95.9 us
    ppermute x2, waiting for transfers between devices, body(): lax.ppermute(own, 'tensor', [(t, (t + shift) % peers) for t in range(peer...  45.2 us
    pallas_call x2, Pallas kernels, convolve(): pl.pallas_call(conv_kernel, grid=(1,), out_shape=jax.ShapeDtypeStruct(sig...  41.1 us
    pallas_call x1, Pallas kernels, mix_pair(): pl.pallas_call(functools.partial(pair_kernel, pieces), grid_spec=pltpu.Pr...  30.5 us
    all_gather x1, waiting for transfers between devices, body(): weight = lax.all_gather(out_weight[:, cut:], 'seq', axis=0, tiled=True)  25.1 us
    pallas_call x1, Pallas kernels, mix(): pl.pallas_call(functools.partial(mix_kernel, pieces), grid_spec=pltpu.Pre...  25.1 us
  transfers between devices with their start and end apart: 11, of which 7 were waited for; matrix products, arithmetic and copies ran while one was open for 1% of the time, Pallas kernels for 16%

profile of v7, /device:TPU:9, one launch (start us, length us, event | category | flops | bytes accessed | tf_op | source)
XLA Modules:
  0.0 612.1 jit_solution(10517366096847681559)
XLA Ops:
  6.5 4.8 fusion.25
  11.3 0.0 all-gather.6.cloned.1.call-update
  11.4 8.0 %pack_filters.1 = bf16[16,2,256,128]{3,2,1,0:T(8,128)(2,1)} custom-call(f32[256,1,4096]{2,1,0:T(1,128)} %bitcast.12), custom_call_target="tpu_custom_call" | custom-call | bytes 6291456 | tf_op jit(solution)/shard_map/pack_filters/pallas_call | solution.py:205
  19.4 6.6 %all-to-all-start.1 = ((bf16[16,2,256,128]{3,2,1,0:T(8,128)(2,1)}), bf16[16,2,256,128]{3,2,1,0:T(8,128)(2,1)S(1)}, u32[]{:S(2)}, u32[]{:S(2)}) async-start(bf16[16,2,256,128]{3,2,1,0:T(8,128)(2,1)} %pack_filters.1), calls=%async_computation.1 | async-start | bytes 4194304 | tf_op jit(solution)/shard_map/all_to_all | solution.py:377
  26.0 0.0 all-gather.8.cloned.1.call-start
  26.0 2.2 collective-permute-start
  28.2 143.8 %collective-permute-done = bf16[512,2048]{1,0:T(8,128)(2,1)} collective-permute-done((bf16[512,2048]{1,0:T(8,128)(2,1)}, bf16[512,2048]{1,0:T(8,128)(2,1)}, u32[]{:S(2)}, u32[]{:S(2)}) %collective-permute-start) | collective-permute-done | bytes 2097184 | tf_op jit(solution)/shard_map/ppermute | solution.py:373
  172.0 0.0 all-gather.8.cloned.1.call-update
  172.0 0.0 all-gather.4.cloned.1.call-start
  172.1 0.7 all-gather.4.cloned.1.call-update
  172.8 0.6 copy-done.5
  173.4 4.0 pack_signal.3
  177.3 5.7 all-to-all-start.3
  183.0 4.1 pack_signal.2
  187.1 63.6 %all-to-all-done.3.x_ref = bf16[16,512,128]{2,1,0:T(8,128)(2,1)S(1)} async-done(((bf16[16,512,128]{2,1,0:T(8,128)(2,1)}), bf16[16,512,128]{2,1,0:T(8,128)(2,1)S(1)}, u32[]{:S(2)}, u32[]{:S(2)}) %all-to-all-start.3) | async-done | bytes 2097184 | tf_op jit(solution)/shard_map/all_to_all | solution.py:382
  250.7 1.4 copy-done.6
  252.1 7.7 %all-to-all-start = ((bf16[16,512,128]{2,1,0:T(8,128)(2,1)}), bf16[16,512,128]{2,1,0:T(8,128)(2,1)}, u32[]{:S(2)}, u32[]{:S(2)}) async-start(bf16[16,512,128]{2,1,0:T(8,128)(2,1)} %pack_signal.2), calls=%async_computation | async-start | bytes 4194304 | tf_op jit(solution)/shard_map/all_to_all | solution.py:382
  259.8 0.6 gather_fusion
  260.4 0.1 select_multiply_fusion
  260.5 0.1 add.136
  260.6 0.1 add.137
  260.7 0.1 add.139
  260.8 0.1 fusion.22
  261.0 0.1 copy.8.twist_ref
  261.1 2.3 negate_convert_fusion
  263.4 0.1 maximum_maximum_fusion.1.back_ref
  263.5 2.5 fusion.15
  266.0 0.1 maximum_maximum_fusion.ahead_ref
  266.1 20.6 %convolve.3 = bf16[16,512,128]{2,1,0:T(8,128)(2,1)S(1)} custom-call(f32[512,32]{1,0:T(8,128)S(1)} %copy.8.twist_ref, bf16[2,256,1024]{2,1,0:T(8,128)(2,1)S(1)} %maximum_maximum_fusion.ahead_ref, bf16[2,1024,256]{2,1,0:T(8,128)(2,1)S(1)} %maximum_maximum_fusion.1.back_ref, bf16[16,512,128]{2,1,0:T(8,128)(2,1)} %copy-done.6, bf16[16,2,256,128]{3,2,1,0:T(8,128)(2,1)} %copy-done.5), custom_call_target="tpu_custom_call" | custom-call | flops 2147483648 | bytes 16777216 | tf_op jit(solution)/shard_map/convolve/pallas_call | solution.py:147
  286.7 1.4 copy-done.3
  288.1 32.3 %all-to-all-done.x_ref = bf16[16,512,128]{2,1,0:T(8,128)(2,1)} async-done(((bf16[16,512,128]{2,1,0:T(8,128)(2,1)}), bf16[16,512,128]{2,1,0:T(8,128)(2,1)}, u32[]{:S(2)}, u32[]{:S(2)}) %all-to-all-start) | async-done | bytes 2097184 | tf_op jit(solution)/shard_map/all_to_all | solution.py:382
  320.4 7.8 %all-to-all-start.4 = ((bf16[16,512,128]{2,1,0:T(8,128)(2,1)}), bf16[16,512,128]{2,1,0:T(8,128)(2,1)}, u32[]{:S(2)}, u32[]{:S(2)}) async-start(bf16[16,512,128]{2,1,0:T(8,128)(2,1)} %copy-done.3), calls=%async_computation.4 | async-start | bytes 4194304 | tf_op jit(solution)/shard_map/all_to_all | solution.py:407
  328.2 20.5 %convolve.2 = bf16[16,512,128]{2,1,0:T(8,128)(2,1)S(1)} custom-call(f32[512,32]{1,0:T(8,128)S(1)} %copy.8.twist_ref, bf16[2,256,1024]{2,1,0:T(8,128)(2,1)S(1)} %maximum_maximum_fusion.ahead_ref, bf16[2,1024,256]{2,1,0:T(8,128)(2,1)S(1)} %maximum_maximum_fusion.1.back_ref, bf16[16,512,128]{2,1,0:T(8,128)(2,1)} %all-to-all-done.x_ref, ...), custom_call_target="tpu_custom_call" | custom-call | flops 2147483648 | bytes 16777216 | tf_op jit(solution)/shard_map/convolve/pallas_call | solution.py:147
  348.8 0.0 copy-start.2
  348.8 1.3 copy-done.2
  350.1 45.2 %all-to-all-done.4.c_ref = bf16[16,512,128]{2,1,0:T(8,128)(2,1)} async-done(((bf16[16,512,128]{2,1,0:T(8,128)(2,1)}), bf16[16,512,128]{2,1,0:T(8,128)(2,1)}, u32[]{:S(2)}, u32[]{:S(2)}) %all-to-all-start.4) | async-done | bytes 2097184 | tf_op jit(solution)/shard_map/all_to_all | solution.py:407
  395.3 8.6 %all-to-all-start.2 = ((bf16[16,512,128]{2,1,0:T(8,128)(2,1)}), bf16[16,512,128]{2,1,0:T(8,128)(2,1)S(1)}, u32[]{:S(2)}, u32[]{:S(2)}) async-start(bf16[16,512,128]{2,1,0:T(8,128)(2,1)} %copy-done.2), calls=%async_computation.2 | async-start | bytes 4194304 | tf_op jit(solution)/shard_map/all_to_all | solution.py:407
  403.9 5.2 gate.3.refs_2_
  409.1 1.2 collective-permute-start.2
  410.3 63.4 %all-to-all-done.2.c_ref = bf16[16,512,128]{2,1,0:T(8,128)(2,1)S(1)} async-done(((bf16[16,512,128]{2,1,0:T(8,128)(2,1)}), bf16[16,512,128]{2,1,0:T(8,128)(2,1)S(1)}, u32[]{:S(2)}, u32[]{:S(2)}) %all-to-all-start.2) | async-done | bytes 2097184 | tf_op jit(solution)/shard_map/all_to_all | solution.py:407
  473.7 4.6 gate.2.refs_0_
  478.4 1.2 collective-permute-start.1
  479.6 0.1 stack.33.place_ref
  479.7 0.1 pad_add_fusion.start_ref
  479.7 45.2 %collective-permute-done.1.refs_1_ = bf16[512,2048]{1,0:T(8,128)(2,1)S(1)} collective-permute-done((bf16[512,2048]{1,0:T(8,128)(2,1)}, bf16[512,2048]{1,0:T(8,128)(2,1)S(1)}, u32[]{:S(2)}, u32[]{:S(2)}) %collective-permute-start.1) | collective-permute-done | bytes 2097184 | tf_op jit(solution)/shard_map/ppermute | solution.py:413
  524.9 30.5 %mix_pair.1.refs_5_ = bf16[512,4096]{1,0:T(8,128)(2,1)} custom-call(s32[12]{0:T(128)S(1)} %stack.33.place_ref, bf16[512,2048]{1,0:T(8,128)(2,1)} %gate.2.refs_0_, bf16[512,2048]{1,0:T(8,128)(2,1)S(1)} %collective-permute-done.1.refs_1_, bf16[512,2048]{1,0:T(8,128)(2,1)} %gate.3.refs_2_, bf16[512,2048]{1,0:T(8,128)(2,1)} %collective-permute-done.2.refs_3_, ...), custom_call_target="tpu_custom_call" | custom-call | flops 17179869184 | bytes 33554432 | tf_op jit(solution)/shard_map/mix_pair/pallas_call | solution.py:325
  555.4 25.1 %all-gather.4.cloned.1.call-done.refs_4_ = bf16[8192,2048]{1,0:T(8,128)(2,1)} async-done(((bf16[512,2048]{1,0:T(8,128)(2,1)}), bf16[8192,2048]{1,0:T(8,128)(2,1)}) %all-gather.4.cloned.1.call-update) | async-done | bytes 33554448 | tf_op jit(solution)/shard_map/all_gather | solution.py:381
  580.5 25.1 %mix.1 = bf16[512,4096]{1,0:T(8,128)(2,1)} custom-call(s32[4]{0:T(128)S(1)} %pad_add_fusion.start_ref, bf16[512,2048]{1,0:T(8,128)(2,1)} %gate.2.refs_0_, bf16[512,2048]{1,0:T(8,128)(2,1)S(1)} %collective-permute-done.1.refs_1_, bf16[512,2048]{1,0:T(8,128)(2,1)} %gate.3.refs_2_, ...), custom_call_target="tpu_custom_call", output_to_operand_aliasing={{}: (6, {})} | custom-call | flops 17179869184 | bytes 33554432 | tf_op jit(solution)/shard_map/mix/pallas_call | solution.py:278
  (22 shorter events, 0.1 us)
Async XLA Ops:
  6.5 253.3 %copy-start = (s32[32,32]{1,0:T(8,128)S(1)}, s32[32,32]{1,0:T(8,128)}, u32[]{:S(2)}) copy-start(s32[32,32]{1,0:T(8,128)} %param.10) | copy-start | bytes 12292
  6.5 518.4 %all-gather.6.cloned.1.call-start = ((), (), s32[]{:S(2)}) async-start(), calls=%async_computation.6 | async-start | bytes 18874368 | tf_op jit(solution)/shard_map/all_gather | solution.py:380
  19.4 152.6 %all-to-all-start.1 = ((bf16[16,2,256,128]{3,2,1,0:T(8,128)(2,1)}), bf16[16,2,256,128]{3,2,1,0:T(8,128)(2,1)S(1)}, u32[]{:S(2)}, u32[]{:S(2)}) async-start(bf16[16,2,256,128]{3,2,1,0:T(8,128)(2,1)} %pack_filters.1), calls=%async_computation.1 | async-start | bytes 4194304 | tf_op jit(solution)/shard_map/all_to_all | solution.py:377
  26.0 498.9 %all-gather.8.cloned.1.call-start = ((), (), s32[]{:S(2)}) async-start(), calls=%async_computation.7 | async-start | bytes 18874368 | tf_op jit(solution)/shard_map/all_gather | solution.py:380
  26.0 146.0 %collective-permute-start = (bf16[512,2048]{1,0:T(8,128)(2,1)}, bf16[512,2048]{1,0:T(8,128)(2,1)}, u32[]{:S(2)}, u32[]{:S(2)}) collective-permute-start(bf16[512,2048]{1,0:T(8,128)(2,1)} %get-tuple-element.9), channel_id=1, source_target_pairs={{0,16},{2,18},{4,20},{6,22},{8,24},{10,26},{12,28},{14,30},{16,0},... | collective-permute-start | bytes 6291464 | tf_op jit(solution)/shard_map/ppermute | solution.py:373
  172.0 1.4 copy-start.5
  172.0 408.5 %all-gather.4.cloned.1.call-start = ((), (), s32[]{:S(2)}) async-start(), calls=%async_computation.5 | async-start | bytes 35651584 | tf_op jit(solution)/shard_map/all_gather | solution.py:381
  177.3 73.4 %all-to-all-start.3 = ((bf16[16,512,128]{2,1,0:T(8,128)(2,1)}), bf16[16,512,128]{2,1,0:T(8,128)(2,1)S(1)}, u32[]{:S(2)}, u32[]{:S(2)}) async-start(bf16[16,512,128]{2,1,0:T(8,128)(2,1)} %pack_signal.3), calls=%async_computation.3 | async-start | bytes 4194304 | tf_op jit(solution)/shard_map/all_to_all | solution.py:382
  250.7 1.4 copy-start.6
  252.1 68.3 %all-to-all-start = ((bf16[16,512,128]{2,1,0:T(8,128)(2,1)}), bf16[16,512,128]{2,1,0:T(8,128)(2,1)}, u32[]{:S(2)}, u32[]{:S(2)}) async-start(bf16[16,512,128]{2,1,0:T(8,128)(2,1)} %pack_signal.2), calls=%async_computation | async-start | bytes 4194304 | tf_op jit(solution)/shard_map/all_to_all | solution.py:382
  286.7 1.4 copy-start.3
  320.4 74.9 %all-to-all-start.4 = ((bf16[16,512,128]{2,1,0:T(8,128)(2,1)}), bf16[16,512,128]{2,1,0:T(8,128)(2,1)}, u32[]{:S(2)}, u32[]{:S(2)}) async-start(bf16[16,512,128]{2,1,0:T(8,128)(2,1)} %copy-done.3), calls=%async_computation.4 | async-start | bytes 4194304 | tf_op jit(solution)/shard_map/all_to_all | solution.py:407
  348.8 1.3 copy-start.2
  350.1 53.8 %copy-start.4 = (f32[4096]{0:T(1024)S(1)}, f32[4096]{0:T(1024)}, u32[]{:S(2)}) copy-start(f32[4096]{0:T(1024)} %param.8) | copy-start | bytes 49156
  395.3 78.4 %all-to-all-start.2 = ((bf16[16,512,128]{2,1,0:T(8,128)(2,1)}), bf16[16,512,128]{2,1,0:T(8,128)(2,1)S(1)}, u32[]{:S(2)}, u32[]{:S(2)}) async-start(bf16[16,512,128]{2,1,0:T(8,128)(2,1)} %copy-done.2), calls=%async_computation.2 | async-start | bytes 4194304 | tf_op jit(solution)/shard_map/all_to_all | solution.py:407
  409.1 70.6 %collective-permute-start.2 = (bf16[512,2048]{1,0:T(8,128)(2,1)}, bf16[512,2048]{1,0:T(8,128)(2,1)}, u32[]{:S(2)}, u32[]{:S(2)}) collective-permute-start(bf16[512,2048]{1,0:T(8,128)(2,1)} %gate.3.refs_2_), channel_id=1, source_target_pairs={{0,1},{1,0},{2,3},{3,2},{4,5},{5,4},{6,7},{7,6},{8,9},{9,8},{10,11... | collective-permute-start | bytes 6291464 | tf_op jit(solution)/shard_map/ppermute | solution.py:413
  478.4 46.5 %collective-permute-start.1 = (bf16[512,2048]{1,0:T(8,128)(2,1)}, bf16[512,2048]{1,0:T(8,128)(2,1)S(1)}, u32[]{:S(2)}, u32[]{:S(2)}) collective-permute-start(bf16[512,2048]{1,0:T(8,128)(2,1)} %gate.2.refs_0_), channel_id=1, source_target_pairs={{0,1},{1,0},{2,3},{3,2},{4,5},{5,4},{6,7},{7,6},{8,9},{9,8},{10,11... | collective-permute-start | bytes 6291464 | tf_op jit(solution)/shard_map/ppermute | solution.py:413
  580.5 25.1 %copy-start.1 = (s32[32,32]{1,0:T(8,128)S(1)}, s32[32,32]{1,0:T(8,128)}, u32[]{:S(2)}) copy-start(s32[32,32]{1,0:T(8,128)} %param.10) | copy-start | bytes 12292
Sparse Core Ops, SparseCore 0:
  11.5 160.3 all-gather.5
  173.5 145.1 all-gather.7
  320.3 260.1 all-gather.3

commit v8 on v7

--- a/solution.py
+++ b/solution.py
@@ -271,7 +271,7 @@
 def mix(hidden, starts, weight, low, columns, result):
     tokens, width = hidden[0].shape
     depth, part = weight.shape
-    tile = min(1024, part)
+    tile = min(512, part)
     first = low // tile
     pieces = len(hidden)
     before = [] if result is None else [result]
@@ -362,7 +362,8 @@
     half = cycle // 2
     width = cycle * unit
     paired = columns % 2048 == 0 and peers == 2 and half * out_weight.shape[0] == channels
-    cut = columns // 2 if paired else 0
+    cut = columns // 4 if paired else 0
+    bounds = [cut, cut + (columns - cut) // 2, columns] if paired else [0, columns]
     if paired:
         sides = [list(range(half)), list(range(half, cycle))]
         gather = functools.partial(
@@ -378,7 +379,10 @@
     if paired:
         other, filters = lax.optimization_barrier((other, filters))
         pair = [gather(own), gather(other)]
-    weight = lax.all_gather(out_weight[:, cut:], "seq", axis=0, tiled=True)
+    weights = [
+        lax.all_gather(out_weight[:, low:high], "seq", axis=0, tiled=True)
+        for low, high in zip(bounds[:-1], bounds[1:])
+    ]
     signals = [exchange(pack_signal(keyval, g, cycle, unit)) for g in range(chunks)]
 
     group = (jnp.arange(chunks, dtype=jnp.int32) * cycle + place) * unit // group_width
@@ -423,7 +427,9 @@
         places = jnp.stack(rows + rows + which).astype(jnp.int32)
         result = mix_pair(hidden, places, pair, columns)
     starts = jnp.stack(starts).astype(jnp.int32)
-    return mix(hidden, starts, weight, cut, columns, result)
+    for low, weight in zip(bounds[:-1], weights):
+        result = mix(hidden, starts, weight, low, columns, result)
+    return result
 
 
 def solution(mesh):

time: 613 us -> 623 us (1.016)
  Pallas kernels: 123 us -> 130 us
    ppermute x1, waiting for transfers between devices: 144 us -> 88 us  [body(): lax.ppermute(sent, 'seq', [(i, (i + half) % cycle) for i in range(cycle)])]
    all_gather x1 -> x2, waiting for transfers between devices: 25.1 us -> 71.5 us  [body(): lax.all_gather(out_weight[:, low:high], 'seq', axis=0, tiled=True)]
    pallas_call x1 -> x2, Pallas kernels: 25.1 us -> 45.2 us  [mix(): pl.pallas_call(functools.partial(mix_kernel, pieces), grid_spec=pltpu.Pre...]
    pallas_call x1, Pallas kernels: 30.5 us -> 18 us  [mix_pair(): pl.pallas_call(functools.partial(pair_kernel, pieces), grid_spec=pltpu.Pr...]
  transfers between devices with their start and end apart: 11 -> 12, of which waited for: 7 -> 7; matrix products, arithmetic and copies ran while one was open for 1% -> 2% of each run, Pallas kernels for 16% -> 17%
where the time goes in v8:
time: 623 us; the launch traced here: 620 us
  waiting for transfers between devices  417 us (67%)
  Pallas kernels  130 us (21%)
  starting transfers between devices  42.6 us (7%)
  between operations  13.3 us (2%)
  local copies, waits for them, and re-layouts  11.8 us (2%)
    all_to_all x2, waiting for transfers between devices, body(): done = exchange(convolve(g, twist, ahead, back, signals[g], filters))  110 us
    all_to_all x2, waiting for transfers between devices, body(): exchange(pack_signal(keyval, g, cycle, unit))  102 us
    ppermute x1, waiting for transfers between devices, body(): lax.ppermute(sent, 'seq', [(i, (i + half) % cycle) for i in range(cycle)])  88 us
    all_gather x2, waiting for transfers between devices, body(): lax.all_gather(out_weight[:, low:high], 'seq', axis=0, tiled=True)  71.5 us
    pallas_call x2, Pallas kernels, mix(): pl.pallas_call(functools.partial(mix_kernel, pieces), grid_spec=pltpu.Pre...  45.2 us
    ppermute x2, waiting for transfers between devices, body(): lax.ppermute(own, 'tensor', [(t, (t + shift) % peers) for t in range(peer...  45.2 us
    pallas_call x2, Pallas kernels, convolve(): pl.pallas_call(conv_kernel, grid=(1,), out_shape=jax.ShapeDtypeStruct(sig...  41.2 us
    pallas_call x1, Pallas kernels, mix_pair(): pl.pallas_call(functools.partial(pair_kernel, pieces), grid_spec=pltpu.Pr...  18 us
  transfers between devices with their start and end apart: 12, of which 7 were waited for; matrix products, arithmetic and copies ran while one was open for 2% of the time, Pallas kernels for 17%

profile of v8, /device:TPU:9, one launch (start us, length us, event | category | flops | bytes accessed | tf_op | source)
XLA Modules:
  0.0 620.0 jit_solution(8928390749720744879)
XLA Ops:
  6.5 2.3 slice.9
  8.9 8.0 %pack_filters.1 = bf16[16,2,256,128]{3,2,1,0:T(8,128)(2,1)} custom-call(f32[256,1,4096]{2,1,0:T(1,128)} %bitcast.12), custom_call_target="tpu_custom_call" | custom-call | bytes 6291456 | tf_op jit(solution)/shard_map/pack_filters/pallas_call | solution.py:205
  16.9 6.7 %all-to-all-start.1 = ((bf16[16,2,256,128]{3,2,1,0:T(8,128)(2,1)}), bf16[16,2,256,128]{3,2,1,0:T(8,128)(2,1)S(1)}, u32[]{:S(2)}, u32[]{:S(2)}) async-start(bf16[16,2,256,128]{3,2,1,0:T(8,128)(2,1)} %pack_filters.1), calls=%async_computation.1 | async-start | bytes 4194304 | tf_op jit(solution)/shard_map/all_to_all | solution.py:378
  23.6 0.0 all-gather.11.cloned.1.call-start
  23.7 2.2 collective-permute-start
  25.8 88.0 %collective-permute-done = bf16[512,1024]{1,0:T(8,128)(2,1)} collective-permute-done((bf16[512,1024]{1,0:T(8,128)(2,1)S(1)}, bf16[512,1024]{1,0:T(8,128)(2,1)}, u32[]{:S(2)}, u32[]{:S(2)}) %collective-permute-start) | collective-permute-done | bytes 1048608 | tf_op jit(solution)/shard_map/ppermute | solution.py:374
  113.9 0.0 all-gather.11.cloned.1.call-update
  113.9 0.0 all-gather.7.cloned.1.call-start
  114.0 4.4 fusion.25
  118.4 0.0 all-gather.5.cloned.1.call-start
  118.5 0.5 all-gather.5.cloned.1.call-update
  119.0 3.9 pack_signal.3
  122.9 7.7 %all-to-all-start.3 = ((bf16[16,512,128]{2,1,0:T(8,128)(2,1)}), bf16[16,512,128]{2,1,0:T(8,128)(2,1)S(1)}, u32[]{:S(2)}, u32[]{:S(2)}) async-start(bf16[16,512,128]{2,1,0:T(8,128)(2,1)} %pack_signal.3), calls=%async_computation.3 | async-start | bytes 4194304 | tf_op jit(solution)/shard_map/all_to_all | solution.py:386
  130.6 3.9 pack_signal.2
  134.6 60.2 %all-to-all-done.3.x_ref = bf16[16,512,128]{2,1,0:T(8,128)(2,1)S(1)} async-done(((bf16[16,512,128]{2,1,0:T(8,128)(2,1)}), bf16[16,512,128]{2,1,0:T(8,128)(2,1)S(1)}, u32[]{:S(2)}, u32[]{:S(2)}) %all-to-all-start.3) | async-done | bytes 2097184 | tf_op jit(solution)/shard_map/all_to_all | solution.py:386
  194.8 1.3 copy-done.6
  196.1 8.4 %all-to-all-start = ((bf16[16,512,128]{2,1,0:T(8,128)(2,1)}), bf16[16,512,128]{2,1,0:T(8,128)(2,1)}, u32[]{:S(2)}, u32[]{:S(2)}) async-start(bf16[16,512,128]{2,1,0:T(8,128)(2,1)} %pack_signal.2), calls=%async_computation | async-start | bytes 4194304 | tf_op jit(solution)/shard_map/all_to_all | solution.py:386
  204.5 0.1 add.139
  204.6 0.6 gather_fusion
  205.2 0.1 select_multiply_fusion
  205.3 0.1 add.136
  205.3 0.1 add.137
  205.4 0.1 fusion.22
  205.6 0.1 copy.9.twist_ref
  205.8 2.5 fusion.15
  208.2 0.1 maximum_maximum_fusion.ahead_ref
  208.4 2.3 negate_convert_fusion
  210.6 0.1 maximum_maximum_fusion.1.back_ref
  210.8 20.5 %convolve.3 = bf16[16,512,128]{2,1,0:T(8,128)(2,1)S(1)} custom-call(f32[512,32]{1,0:T(8,128)S(1)} %copy.9.twist_ref, bf16[2,256,1024]{2,1,0:T(8,128)(2,1)S(1)} %maximum_maximum_fusion.ahead_ref, bf16[2,1024,256]{2,1,0:T(8,128)(2,1)S(1)} %maximum_maximum_fusion.1.back_ref, bf16[16,512,128]{2,1,0:T(8,128)(2,1)} %copy-done.6, bf16[16,2,256,128]{3,2,1,0:T(8,128)(2,1)} %copy-done.5), custom_call_target="tpu_custom_call" | custom-call | flops 2147483648 | bytes 16777216 | tf_op jit(solution)/shard_map/convolve/pallas_call | solution.py:147
  231.3 1.3 copy-done.3
  232.7 41.7 %all-to-all-done.x_ref = bf16[16,512,128]{2,1,0:T(8,128)(2,1)} async-done(((bf16[16,512,128]{2,1,0:T(8,128)(2,1)}), bf16[16,512,128]{2,1,0:T(8,128)(2,1)}, u32[]{:S(2)}, u32[]{:S(2)}) %all-to-all-start) | async-done | bytes 2097184 | tf_op jit(solution)/shard_map/all_to_all | solution.py:386
  274.4 7.7 %all-to-all-start.4 = ((bf16[16,512,128]{2,1,0:T(8,128)(2,1)}), bf16[16,512,128]{2,1,0:T(8,128)(2,1)}, u32[]{:S(2)}, u32[]{:S(2)}) async-start(bf16[16,512,128]{2,1,0:T(8,128)(2,1)} %copy-done.3), calls=%async_computation.4 | async-start | bytes 4194304 | tf_op jit(solution)/shard_map/all_to_all | solution.py:411
  282.1 20.6 %convolve.2 = bf16[16,512,128]{2,1,0:T(8,128)(2,1)S(1)} custom-call(f32[512,32]{1,0:T(8,128)S(1)} %copy.9.twist_ref, bf16[2,256,1024]{2,1,0:T(8,128)(2,1)S(1)} %maximum_maximum_fusion.ahead_ref, bf16[2,1024,256]{2,1,0:T(8,128)(2,1)S(1)} %maximum_maximum_fusion.1.back_ref, bf16[16,512,128]{2,1,0:T(8,128)(2,1)} %all-to-all-done.x_ref, ...), custom_call_target="tpu_custom_call" | custom-call | flops 2147483648 | bytes 16777216 | tf_op jit(solution)/shard_map/convolve/pallas_call | solution.py:147
  302.7 1.3 copy-done.2
  304.0 48.0 %all-to-all-done.4.c_ref = bf16[16,512,128]{2,1,0:T(8,128)(2,1)} async-done(((bf16[16,512,128]{2,1,0:T(8,128)(2,1)}), bf16[16,512,128]{2,1,0:T(8,128)(2,1)}, u32[]{:S(2)}, u32[]{:S(2)}) %all-to-all-start.4) | async-done | bytes 2097184 | tf_op jit(solution)/shard_map/all_to_all | solution.py:411
  352.0 7.4 %all-to-all-start.2 = ((bf16[16,512,128]{2,1,0:T(8,128)(2,1)}), bf16[16,512,128]{2,1,0:T(8,128)(2,1)S(1)}, u32[]{:S(2)}, u32[]{:S(2)}) async-start(bf16[16,512,128]{2,1,0:T(8,128)(2,1)} %copy-done.2), calls=%async_computation.2 | async-start | bytes 4194304 | tf_op jit(solution)/shard_map/all_to_all | solution.py:411
  359.5 5.1 gate.3.refs_2_
  364.6 1.2 collective-permute-start.2
  365.8 61.8 %all-to-all-done.2.c_ref = bf16[16,512,128]{2,1,0:T(8,128)(2,1)S(1)} async-done(((bf16[16,512,128]{2,1,0:T(8,128)(2,1)}), bf16[16,512,128]{2,1,0:T(8,128)(2,1)S(1)}, u32[]{:S(2)}, u32[]{:S(2)}) %all-to-all-start.2) | async-done | bytes 2097184 | tf_op jit(solution)/shard_map/all_to_all | solution.py:411
  427.5 4.7 gate.2.refs_0_
  432.2 1.2 collective-permute-start.1
  433.4 0.1 stack.33.place_ref
  433.5 0.1 pad_add_fusion.start_ref
  433.6 45.2 %collective-permute-done.1.refs_1_ = bf16[512,2048]{1,0:T(8,128)(2,1)S(1)} collective-permute-done((bf16[512,2048]{1,0:T(8,128)(2,1)}, bf16[512,2048]{1,0:T(8,128)(2,1)S(1)}, u32[]{:S(2)}, u32[]{:S(2)}) %collective-permute-start.1) | collective-permute-done | bytes 2097184 | tf_op jit(solution)/shard_map/ppermute | solution.py:417
  478.7 18.0 %mix_pair.1.refs_5_ = bf16[512,4096]{1,0:T(8,128)(2,1)} custom-call(s32[12]{0:T(128)S(1)} %stack.33.place_ref, bf16[512,2048]{1,0:T(8,128)(2,1)} %gate.2.refs_0_, bf16[512,2048]{1,0:T(8,128)(2,1)S(1)} %collective-permute-done.1.refs_1_, bf16[512,2048]{1,0:T(8,128)(2,1)} %gate.3.refs_2_, bf16[512,2048]{1,0:T(8,128)(2,1)} %collective-permute-done.2.refs_3_, ...), custom_call_target="tpu_custom_call" | custom-call | flops 8589934592 | bytes 16777216 | tf_op jit(solution)/shard_map/mix_pair/pallas_call | solution.py:325
  496.8 22.9 %mix.2.refs_5_ = bf16[512,4096]{1,0:T(8,128)(2,1)} custom-call(s32[4]{0:T(128)S(1)} %pad_add_fusion.start_ref, bf16[512,2048]{1,0:T(8,128)(2,1)} %gate.2.refs_0_, bf16[512,2048]{1,0:T(8,128)(2,1)S(1)} %collective-permute-done.1.refs_1_, bf16[512,2048]{1,0:T(8,128)(2,1)} %gate.3.refs_2_, ...), custom_call_target="tpu_custom_call", output_to_operand_aliasing={{}: (6, {})} | custom-call | flops 12884901888 | bytes 25165824 | tf_op jit(solution)/shard_map/mix/pallas_call | solution.py:278
  519.6 71.5 %all-gather.5.cloned.1.call-done.refs_4_ = bf16[8192,1536]{1,0:T(8,128)(2,1)} async-done(((bf16[512,1536]{1,0:T(8,128)(2,1)}), bf16[8192,1536]{1,0:T(8,128)(2,1)}) %all-gather.5.cloned.1.call-update) | async-done | bytes 25165840 | tf_op jit(solution)/shard_map/all_gather | solution.py:383
  591.1 22.4 %mix.3 = bf16[512,4096]{1,0:T(8,128)(2,1)} custom-call(s32[4]{0:T(128)S(1)} %pad_add_fusion.start_ref, bf16[512,2048]{1,0:T(8,128)(2,1)} %gate.2.refs_0_, bf16[512,2048]{1,0:T(8,128)(2,1)S(1)} %collective-permute-done.1.refs_1_, bf16[512,2048]{1,0:T(8,128)(2,1)} %gate.3.refs_2_, ...), custom_call_target="tpu_custom_call", output_to_operand_aliasing={{}: (6, {})} | custom-call | flops 12884901888 | bytes 25165824 | tf_op jit(solution)/shard_map/mix/pallas_call | solution.py:278
  (29 shorter events, 0.1 us)
Async XLA Ops:
  6.5 198.1 %copy-start = (s32[32,32]{1,0:T(8,128)S(1)}, s32[32,32]{1,0:T(8,128)}, u32[]{:S(2)}) copy-start(s32[32,32]{1,0:T(8,128)} %param.10) | copy-start | bytes 12292
  6.5 472.2 %all-gather.9.cloned.1.call-start = ((), (), s32[]{:S(2)}) async-start(), calls=%async_computation.7 | async-start | bytes 9437184 | tf_op jit(solution)/shard_map/all_gather | solution.py:381
  16.9 6.8 %copy-start.7 = (bf16[512,1024]{1,0:T(8,128)(2,1)S(1)}, bf16[512,1024]{1,0:T(8,128)(2,1)}, u32[]{:S(2)}) copy-start(bf16[512,1024]{1,0:T(8,128)(2,1)} %slice.9) | copy-start | bytes 3145732
  16.9 97.0 %all-to-all-start.1 = ((bf16[16,2,256,128]{3,2,1,0:T(8,128)(2,1)}), bf16[16,2,256,128]{3,2,1,0:T(8,128)(2,1)S(1)}, u32[]{:S(2)}, u32[]{:S(2)}) async-start(bf16[16,2,256,128]{3,2,1,0:T(8,128)(2,1)} %pack_filters.1), calls=%async_computation.1 | async-start | bytes 4194304 | tf_op jit(solution)/shard_map/all_to_all | solution.py:378
  23.6 455.1 %all-gather.11.cloned.1.call-start = ((), (), s32[]{:S(2)}) async-start(), calls=%async_computation.8 | async-start | bytes 9437184 | tf_op jit(solution)/shard_map/all_gather | solution.py:381
  23.7 90.2 %collective-permute-start = (bf16[512,1024]{1,0:T(8,128)(2,1)S(1)}, bf16[512,1024]{1,0:T(8,128)(2,1)}, u32[]{:S(2)}, u32[]{:S(2)}) collective-permute-start(bf16[512,1024]{1,0:T(8,128)(2,1)S(1)} %copy-done.7), channel_id=1, source_target_pairs={{0,16},{2,18},{4,20},{6,22},{8,24},{10,26},{12,28},{14,30},{16,0},... | collective-permute-start | bytes 3145736 | tf_op jit(solution)/shard_map/ppermute | solution.py:374
  113.9 4.5 copy-start.5
  113.9 382.8 %all-gather.7.cloned.1.call-start = ((), (), s32[]{:S(2)}) async-start(), calls=%async_computation.6 | async-start | bytes 26738688 | tf_op jit(solution)/shard_map/all_gather | solution.py:383
  118.4 472.7 %all-gather.5.cloned.1.call-start = ((), (), s32[]{:S(2)}) async-start(), calls=%async_computation.5 | async-start | bytes 26738688 | tf_op jit(solution)/shard_map/all_gather | solution.py:383
  122.9 71.8 %all-to-all-start.3 = ((bf16[16,512,128]{2,1,0:T(8,128)(2,1)}), bf16[16,512,128]{2,1,0:T(8,128)(2,1)S(1)}, u32[]{:S(2)}, u32[]{:S(2)}) async-start(bf16[16,512,128]{2,1,0:T(8,128)(2,1)} %pack_signal.3), calls=%async_computation.3 | async-start | bytes 4194304 | tf_op jit(solution)/shard_map/all_to_all | solution.py:386
  194.8 1.3 copy-start.6
  196.1 78.3 %all-to-all-start = ((bf16[16,512,128]{2,1,0:T(8,128)(2,1)}), bf16[16,512,128]{2,1,0:T(8,128)(2,1)}, u32[]{:S(2)}, u32[]{:S(2)}) async-start(bf16[16,512,128]{2,1,0:T(8,128)(2,1)} %pack_signal.2), calls=%async_computation | async-start | bytes 4194304 | tf_op jit(solution)/shard_map/all_to_all | solution.py:386
  231.3 1.4 copy-start.3
  274.4 77.6 %all-to-all-start.4 = ((bf16[16,512,128]{2,1,0:T(8,128)(2,1)}), bf16[16,512,128]{2,1,0:T(8,128)(2,1)}, u32[]{:S(2)}, u32[]{:S(2)}) async-start(bf16[16,512,128]{2,1,0:T(8,128)(2,1)} %copy-done.3), calls=%async_computation.4 | async-start | bytes 4194304 | tf_op jit(solution)/shard_map/all_to_all | solution.py:411
  302.7 1.3 copy-start.2
  304.0 55.4 %copy-start.4 = (f32[4096]{0:T(1024)S(1)}, f32[4096]{0:T(1024)}, u32[]{:S(2)}) copy-start(f32[4096]{0:T(1024)} %param.8) | copy-start | bytes 49156
  352.0 75.5 %all-to-all-start.2 = ((bf16[16,512,128]{2,1,0:T(8,128)(2,1)}), bf16[16,512,128]{2,1,0:T(8,128)(2,1)S(1)}, u32[]{:S(2)}, u32[]{:S(2)}) async-start(bf16[16,512,128]{2,1,0:T(8,128)(2,1)} %copy-done.2), calls=%async_computation.2 | async-start | bytes 4194304 | tf_op jit(solution)/shard_map/all_to_all | solution.py:411
  364.6 69.0 %collective-permute-start.2 = (bf16[512,2048]{1,0:T(8,128)(2,1)}, bf16[512,2048]{1,0:T(8,128)(2,1)}, u32[]{:S(2)}, u32[]{:S(2)}) collective-permute-start(bf16[512,2048]{1,0:T(8,128)(2,1)} %gate.3.refs_2_), channel_id=1, source_target_pairs={{0,1},{1,0},{2,3},{3,2},{4,5},{5,4},{6,7},{7,6},{8,9},{9,8},{10,11... | collective-permute-start | bytes 6291464 | tf_op jit(solution)/shard_map/ppermute | solution.py:417
  432.2 46.5 %collective-permute-start.1 = (bf16[512,2048]{1,0:T(8,128)(2,1)}, bf16[512,2048]{1,0:T(8,128)(2,1)S(1)}, u32[]{:S(2)}, u32[]{:S(2)}) collective-permute-start(bf16[512,2048]{1,0:T(8,128)(2,1)} %gate.2.refs_0_), channel_id=1, source_target_pairs={{0,1},{1,0},{2,3},{3,2},{4,5},{5,4},{6,7},{7,6},{8,9},{9,8},{10,11... | collective-permute-start | bytes 6291464 | tf_op jit(solution)/shard_map/ppermute | solution.py:417
  591.1 22.4 %copy-start.1 = (s32[32,32]{1,0:T(8,128)S(1)}, s32[32,32]{1,0:T(8,128)}, u32[]{:S(2)}) copy-start(s32[32,32]{1,0:T(8,128)} %param.10) | copy-start | bytes 12292
Sparse Core Ops, SparseCore 0:
  9.0 96.2 all-gather.8
  114.0 82.1 all-gather.10
  197.8 264.1 all-gather.6
  463.4 127.6 all-gather.4

commit v9 on v3

--- a/solution.py
+++ b/solution.py
@@ -301,7 +301,7 @@
 
     columns = out_weight.shape[1]
     eighth = columns // 8
-    bounds = [0, 4 * eighth, 7 * eighth, columns] if eighth % 256 == 0 else [0, columns]
+    bounds = [0, 5 * eighth, columns] if eighth % 256 == 0 else [0, columns]
     weights = [
         lax.all_gather(out_weight[:, low:high], "seq", axis=0, tiled=True)
         for low, high in zip(bounds[:-1], bounds[1:])

time: 623 us -> 601 us (0.965)
  waiting for transfers between devices: 429 us -> 415 us
    all_gather x3 -> x2, waiting for transfers between devices: 110 us -> 86.5 us  [body(): lax.all_gather(out_weight[:, low:high], 'seq', axis=0, tiled=True)]
    all_to_all x2, waiting for transfers between devices: 102 us -> 110 us  [body(): done = exchange(convolve(g, twist, ahead, back, signals[g], filters))]
    pallas_call x3 -> x2, Pallas kernels: 52.8 us -> 47.8 us  [mix(): pl.pallas_call(functools.partial(mix_kernel, pieces), grid=(part // tile,...]
  transfers between devices with their start and end apart: 10 -> 9, of which waited for: 8 -> 7; matrix products, arithmetic and copies ran while one was open for 2% -> 1% of each run, Pallas kernels for 18% -> 16%
where the time goes in v9:
time: 601 us; the launch traced here: 599 us
  waiting for transfers between devices  415 us (69%)
  Pallas kernels  115 us (19%)
  starting transfers between devices  39.3 us (7%)
  between operations  13.5 us (2%)
  local copies, waits for them, and re-layouts  11.1 us (2%)
    all_to_all x2, waiting for transfers between devices, body(): done = exchange(convolve(g, twist, ahead, back, signals[g], filters))  110 us
    all_to_all x2, waiting for transfers between devices, body(): exchange(pack_signal(keyval, g, cycle, unit))  108 us
    all_gather x2, waiting for transfers between devices, body(): lax.all_gather(out_weight[:, low:high], 'seq', axis=0, tiled=True)  86.5 us
    all_to_all x1, waiting for transfers between devices, body(): filters = exchange(pack_filters(filter_values, cycle, chunks, unit))  65.8 us
    pallas_call x2, Pallas kernels, mix(): pl.pallas_call(functools.partial(mix_kernel, pieces), grid=(part // tile,...  47.8 us
    ppermute x2, waiting for transfers between devices, body(): lax.ppermute(own, 'tensor', [(t, (t + shift) % peers) for t in range(peer...  45.3 us
    pallas_call x2, Pallas kernels, convolve(): pl.pallas_call(conv_kernel, grid=(1,), out_shape=jax.ShapeDtypeStruct(sig...  41.2 us
    all_to_all x2, starting transfers between devices, body(): exchange(pack_signal(keyval, g, cycle, unit))  16.2 us
  transfers between devices with their start and end apart: 9, of which 7 were waited for; matrix products, arithmetic and copies ran while one was open for 1% of the time, Pallas kernels for 16%

profile of v9, /device:TPU:9, one launch (start us, length us, event | category | flops | bytes accessed | tf_op | source)
XLA Modules:
  0.0 599.2 jit_solution(11519081918186484199)
XLA Ops:
  6.5 0.0 copy-start
  6.5 0.0 all-gather.5.cloned.1.call-start
  6.5 3.4 slice.7
  9.9 0.0 all-gather.5.cloned.1.call-update
  10.0 0.0 all-gather.3.cloned.1.call-start
  10.0 2.7 slice.6
  12.7 0.0 all-gather.3.cloned.1.call-update
  12.7 8.3 %pack_filters.1 = bf16[16,2,256,128]{3,2,1,0:T(8,128)(2,1)} custom-call(f32[256,1,4096]{2,1,0:T(1,128)} %bitcast.10), custom_call_target="tpu_custom_call" | custom-call | bytes 6291456 | tf_op jit(solution)/shard_map/pack_filters/pallas_call | solution.py:205
  21.0 6.6 %all-to-all-start.1 = ((bf16[16,2,256,128]{3,2,1,0:T(8,128)(2,1)}), bf16[16,2,256,128]{3,2,1,0:T(8,128)(2,1)S(1)}, u32[]{:S(2)}, u32[]{:S(2)}) async-start(bf16[16,2,256,128]{3,2,1,0:T(8,128)(2,1)} %pack_filters.1), calls=%async_computation.1 | async-start | bytes 4194304 | tf_op jit(solution)/shard_map/all_to_all | solution.py:314
  27.5 4.0 pack_signal.3
  31.6 65.8 %all-to-all-done.1.filter_ref = bf16[16,2,256,128]{3,2,1,0:T(8,128)(2,1)S(1)} async-done(((bf16[16,2,256,128]{3,2,1,0:T(8,128)(2,1)}), bf16[16,2,256,128]{3,2,1,0:T(8,128)(2,1)S(1)}, u32[]{:S(2)}, u32[]{:S(2)}) %all-to-all-start.1) | async-done | bytes 2097184 | tf_op jit(solution)/shard_map/all_to_all | solution.py:314
  97.4 1.4 copy-done.5
  98.7 8.1 %all-to-all-start.3 = ((bf16[16,512,128]{2,1,0:T(8,128)(2,1)}), bf16[16,512,128]{2,1,0:T(8,128)(2,1)}, u32[]{:S(2)}, u32[]{:S(2)}) async-start(bf16[16,512,128]{2,1,0:T(8,128)(2,1)} %pack_signal.3), calls=%async_computation.3 | async-start | bytes 4194304 | tf_op jit(solution)/shard_map/all_to_all | solution.py:313
  106.8 3.9 pack_signal.2
  110.7 66.0 %all-to-all-done.3.x_ref = bf16[16,512,128]{2,1,0:T(8,128)(2,1)} async-done(((bf16[16,512,128]{2,1,0:T(8,128)(2,1)}), bf16[16,512,128]{2,1,0:T(8,128)(2,1)}, u32[]{:S(2)}, u32[]{:S(2)}) %all-to-all-start.3) | async-done | bytes 2097184 | tf_op jit(solution)/shard_map/all_to_all | solution.py:313
  176.7 8.1 %all-to-all-start = ((bf16[16,512,128]{2,1,0:T(8,128)(2,1)}), bf16[16,512,128]{2,1,0:T(8,128)(2,1)}, u32[]{:S(2)}, u32[]{:S(2)}) async-start(bf16[16,512,128]{2,1,0:T(8,128)(2,1)} %pack_signal.2), calls=%async_computation | async-start | bytes 4194304 | tf_op jit(solution)/shard_map/all_to_all | solution.py:313
  184.9 0.0 copy-done
  184.9 0.6 gather_fusion
  185.5 0.1 select_multiply_fusion
  185.5 0.1 add.116
  185.6 0.1 add.117
  185.7 0.1 add.119
  185.8 0.1 fusion.22
  186.0 0.1 copy.8.twist_ref
  186.2 2.3 negate_convert_fusion
  188.4 0.1 maximum_maximum_fusion.1.back_ref
  188.5 2.5 fusion.15
  191.0 0.1 maximum_maximum_fusion.ahead_ref
  191.2 20.6 %convolve.3 = bf16[16,512,128]{2,1,0:T(8,128)(2,1)S(1)} custom-call(f32[512,32]{1,0:T(8,128)S(1)} %copy.8.twist_ref, bf16[2,256,1024]{2,1,0:T(8,128)(2,1)S(1)} %maximum_maximum_fusion.ahead_ref, bf16[2,1024,256]{2,1,0:T(8,128)(2,1)S(1)} %maximum_maximum_fusion.1.back_ref, bf16[16,512,128]{2,1,0:T(8,128)(2,1)} %all-to-all-done.3.x_ref, ...), custom_call_target="tpu_custom_call" | custom-call | flops 2147483648 | bytes 16777216 | tf_op jit(solution)/shard_map/convolve/pallas_call | solution.py:147
  211.7 0.0 copy-start.3
  211.7 1.4 copy-done.3
  213.1 41.7 %all-to-all-done.x_ref = bf16[16,512,128]{2,1,0:T(8,128)(2,1)} async-done(((bf16[16,512,128]{2,1,0:T(8,128)(2,1)}), bf16[16,512,128]{2,1,0:T(8,128)(2,1)}, u32[]{:S(2)}, u32[]{:S(2)}) %all-to-all-start) | async-done | bytes 2097184 | tf_op jit(solution)/shard_map/all_to_all | solution.py:313
  254.8 8.1 %all-to-all-start.4 = ((bf16[16,512,128]{2,1,0:T(8,128)(2,1)}), bf16[16,512,128]{2,1,0:T(8,128)(2,1)}, u32[]{:S(2)}, u32[]{:S(2)}) async-start(bf16[16,512,128]{2,1,0:T(8,128)(2,1)} %copy-done.3), calls=%async_computation.4 | async-start | bytes 4194304 | tf_op jit(solution)/shard_map/all_to_all | solution.py:339
  262.9 20.6 %convolve.2 = bf16[16,512,128]{2,1,0:T(8,128)(2,1)S(1)} custom-call(f32[512,32]{1,0:T(8,128)S(1)} %copy.8.twist_ref, bf16[2,256,1024]{2,1,0:T(8,128)(2,1)S(1)} %maximum_maximum_fusion.ahead_ref, bf16[2,1024,256]{2,1,0:T(8,128)(2,1)S(1)} %maximum_maximum_fusion.1.back_ref, bf16[16,512,128]{2,1,0:T(8,128)(2,1)} %all-to-all-done.x_ref, ...), custom_call_target="tpu_custom_call" | custom-call | flops 2147483648 | bytes 16777216 | tf_op jit(solution)/shard_map/convolve/pallas_call | solution.py:147
  283.5 1.3 copy-done.2
  284.8 48.0 %all-to-all-done.4.c_ref = bf16[16,512,128]{2,1,0:T(8,128)(2,1)} async-done(((bf16[16,512,128]{2,1,0:T(8,128)(2,1)}), bf16[16,512,128]{2,1,0:T(8,128)(2,1)}, u32[]{:S(2)}, u32[]{:S(2)}) %all-to-all-start.4) | async-done | bytes 2097184 | tf_op jit(solution)/shard_map/all_to_all | solution.py:339
  332.8 6.1 %all-to-all-start.2 = ((bf16[16,512,128]{2,1,0:T(8,128)(2,1)}), bf16[16,512,128]{2,1,0:T(8,128)(2,1)S(1)}, u32[]{:S(2)}, u32[]{:S(2)}) async-start(bf16[16,512,128]{2,1,0:T(8,128)(2,1)} %copy-done.2), calls=%async_computation.2 | async-start | bytes 4194304 | tf_op jit(solution)/shard_map/all_to_all | solution.py:339
  338.9 5.2 gate.3.refs_2_
  344.1 1.2 collective-permute-start.1
  345.3 61.6 %all-to-all-done.2.c_ref = bf16[16,512,128]{2,1,0:T(8,128)(2,1)S(1)} async-done(((bf16[16,512,128]{2,1,0:T(8,128)(2,1)}), bf16[16,512,128]{2,1,0:T(8,128)(2,1)S(1)}, u32[]{:S(2)}, u32[]{:S(2)}) %all-to-all-start.2) | async-done | bytes 2097184 | tf_op jit(solution)/shard_map/all_to_all | solution.py:339
  406.9 4.6 gate.2.refs_0_
  411.5 1.2 collective-permute-start
  412.7 0.1 pad_add_fusion.start_ref
  412.8 0.0 collective-permute-done.1.refs_3_
  412.8 45.3 %collective-permute-done.refs_1_ = bf16[512,2048]{1,0:T(8,128)(2,1)S(1)} collective-permute-done((bf16[512,2048]{1,0:T(8,128)(2,1)}, bf16[512,2048]{1,0:T(8,128)(2,1)S(1)}, u32[]{:S(2)}, u32[]{:S(2)}) %collective-permute-start) | collective-permute-done | bytes 2097184 | tf_op jit(solution)/shard_map/ppermute | solution.py:345
  458.0 28.8 %mix.2.refs_5_ = bf16[512,4096]{1,0:T(8,128)(2,1)} custom-call(s32[4]{0:T(128)S(1)} %pad_add_fusion.start_ref, bf16[512,2048]{1,0:T(8,128)(2,1)} %gate.2.refs_0_, bf16[512,2048]{1,0:T(8,128)(2,1)S(1)} %collective-permute-done.refs_1_, bf16[512,2048]{1,0:T(8,128)(2,1)} %gate.3.refs_2_, bf16[512,2048]{1,0:T(8,128)(2,1)} %collective-permute-done.1.refs_3_, ...), custom_call_target="tpu_custom_call" | custom-call | flops 21474836480 | bytes 41943040 | tf_op jit(solution)/shard_map/mix/pallas_call | solution.py:271
  486.8 86.5 %all-gather.3.cloned.1.call-done.refs_4_ = bf16[8192,1536]{1,0:T(8,128)(2,1)} async-done(((bf16[512,1536]{1,0:T(8,128)(2,1)}), bf16[8192,1536]{1,0:T(8,128)(2,1)}) %all-gather.3.cloned.1.call-update) | async-done | bytes 25165840 | tf_op jit(solution)/shard_map/all_gather | solution.py:306
  573.3 19.0 %mix.3 = bf16[512,4096]{1,0:T(8,128)(2,1)} custom-call(s32[4]{0:T(128)S(1)} %pad_add_fusion.start_ref, bf16[512,2048]{1,0:T(8,128)(2,1)} %gate.2.refs_0_, bf16[512,2048]{1,0:T(8,128)(2,1)S(1)} %collective-permute-done.refs_1_, bf16[512,2048]{1,0:T(8,128)(2,1)} %gate.3.refs_2_, ...), custom_call_target="tpu_custom_call", output_to_operand_aliasing={{}: (6, {})} | custom-call | flops 12884901888 | bytes 25165824 | tf_op jit(solution)/shard_map/mix/pallas_call | solution.py:271
  (13 shorter events, 0.1 us)
Async XLA Ops:
  6.5 178.4 %copy-start = (s32[32,32]{1,0:T(8,128)S(1)}, s32[32,32]{1,0:T(8,128)}, u32[]{:S(2)}) copy-start(s32[32,32]{1,0:T(8,128)} %param.10) | copy-start | bytes 12292
  6.5 451.5 %all-gather.5.cloned.1.call-start = ((), (), s32[]{:S(2)}) async-start(), calls=%async_computation.6 | async-start | bytes 44564480 | tf_op jit(solution)/shard_map/all_gather | solution.py:306
  10.0 563.3 %all-gather.3.cloned.1.call-start = ((), (), s32[]{:S(2)}) async-start(), calls=%async_computation.5 | async-start | bytes 26738688 | tf_op jit(solution)/shard_map/all_gather | solution.py:306
  21.0 76.4 %all-to-all-start.1 = ((bf16[16,2,256,128]{3,2,1,0:T(8,128)(2,1)}), bf16[16,2,256,128]{3,2,1,0:T(8,128)(2,1)S(1)}, u32[]{:S(2)}, u32[]{:S(2)}) async-start(bf16[16,2,256,128]{3,2,1,0:T(8,128)(2,1)} %pack_filters.1), calls=%async_computation.1 | async-start | bytes 4194304 | tf_op jit(solution)/shard_map/all_to_all | solution.py:314
  97.4 1.4 copy-start.5
  98.7 78.0 %all-to-all-start.3 = ((bf16[16,512,128]{2,1,0:T(8,128)(2,1)}), bf16[16,512,128]{2,1,0:T(8,128)(2,1)}, u32[]{:S(2)}, u32[]{:S(2)}) async-start(bf16[16,512,128]{2,1,0:T(8,128)(2,1)} %pack_signal.3), calls=%async_computation.3 | async-start | bytes 4194304 | tf_op jit(solution)/shard_map/all_to_all | solution.py:313
  176.7 78.0 %all-to-all-start = ((bf16[16,512,128]{2,1,0:T(8,128)(2,1)}), bf16[16,512,128]{2,1,0:T(8,128)(2,1)}, u32[]{:S(2)}, u32[]{:S(2)}) async-start(bf16[16,512,128]{2,1,0:T(8,128)(2,1)} %pack_signal.2), calls=%async_computation | async-start | bytes 4194304 | tf_op jit(solution)/shard_map/all_to_all | solution.py:313
  211.7 1.4 copy-start.3
  254.8 78.0 %all-to-all-start.4 = ((bf16[16,512,128]{2,1,0:T(8,128)(2,1)}), bf16[16,512,128]{2,1,0:T(8,128)(2,1)}, u32[]{:S(2)}, u32[]{:S(2)}) async-start(bf16[16,512,128]{2,1,0:T(8,128)(2,1)} %copy-done.3), calls=%async_computation.4 | async-start | bytes 4194304 | tf_op jit(solution)/shard_map/all_to_all | solution.py:339
  283.5 1.3 copy-start.2
  284.8 54.1 %copy-start.4 = (f32[4096]{0:T(1024)S(1)}, f32[4096]{0:T(1024)}, u32[]{:S(2)}) copy-start(f32[4096]{0:T(1024)} %param.8) | copy-start | bytes 49156
  332.8 74.1 %all-to-all-start.2 = ((bf16[16,512,128]{2,1,0:T(8,128)(2,1)}), bf16[16,512,128]{2,1,0:T(8,128)(2,1)S(1)}, u32[]{:S(2)}, u32[]{:S(2)}) async-start(bf16[16,512,128]{2,1,0:T(8,128)(2,1)} %copy-done.2), calls=%async_computation.2 | async-start | bytes 4194304 | tf_op jit(solution)/shard_map/all_to_all | solution.py:339
  344.1 68.7 %collective-permute-start.1 = (bf16[512,2048]{1,0:T(8,128)(2,1)}, bf16[512,2048]{1,0:T(8,128)(2,1)}, u32[]{:S(2)}, u32[]{:S(2)}) collective-permute-start(bf16[512,2048]{1,0:T(8,128)(2,1)} %gate.3.refs_2_), channel_id=1, source_target_pairs={{0,1},{1,0},{2,3},{3,2},{4,5},{5,4},{6,7},{7,6},{8,9},{9,8},{10,11... | collective-permute-start | bytes 6291464 | tf_op jit(solution)/shard_map/ppermute | solution.py:345
  411.5 46.5 %collective-permute-start = (bf16[512,2048]{1,0:T(8,128)(2,1)}, bf16[512,2048]{1,0:T(8,128)(2,1)S(1)}, u32[]{:S(2)}, u32[]{:S(2)}) collective-permute-start(bf16[512,2048]{1,0:T(8,128)(2,1)} %gate.2.refs_0_), channel_id=1, source_target_pairs={{0,1},{1,0},{2,3},{3,2},{4,5},{5,4},{6,7},{7,6},{8,9},{9,8},{10,11... | collective-permute-start | bytes 6291464 | tf_op jit(solution)/shard_map/ppermute | solution.py:345
  573.3 19.0 %copy-start.1 = (s32[32,32]{1,0:T(8,128)S(1)}, s32[32,32]{1,0:T(8,128)}, u32[]{:S(2)}) copy-start(s32[32,32]{1,0:T(8,128)} %param.10) | copy-start | bytes 12292
Sparse Core Ops, SparseCore 0:
  10.1 433.8 all-gather.4
  445.6 127.6 all-gather.2

commit v10 on v9

--- a/solution.py
+++ b/solution.py
@@ -273,12 +273,12 @@
         grid=(part // tile,),
         out_shape=jax.ShapeDtypeStruct((tokens, columns), BF16),
         in_specs=[pl.BlockSpec(memory_space=pltpu.SMEM)]
-        + [pl.BlockSpec(h.shape, lambda i: (0, 0)) for h in hidden]
+        + [pl.BlockSpec(memory_space=pltpu.VMEM) for h in hidden]
         + [pl.BlockSpec((depth, tile), lambda i: (0, i))]
         + [pl.BlockSpec(memory_space=pl.ANY) for _ in before],
         out_specs=pl.BlockSpec((tokens, tile), lambda i: (0, first + i)),
         input_output_aliases={pieces + 2: 0} if before else {},
-        compiler_params=pltpu.CompilerParams(vmem_limit_bytes=VMEM),
+        compiler_params=pltpu.CompilerParams(vmem_limit_bytes=32 * 2**20),
         cost_estimate=pl.CostEstimate(
             flops=2 * tokens * depth * part, bytes_accessed=2 * depth * part, transcendentals=0
         ),

time: 601 us -> 601 us (level)
  no operation moved by 1% of the time
where the time goes in v10:
time: 601 us; the launch traced here: 599 us
  waiting for transfers between devices  415 us (69%)
  Pallas kernels  115 us (19%)
  starting transfers between devices  39.3 us (7%)
  between operations  13.5 us (2%)
  local copies, waits for them, and re-layouts  11.1 us (2%)
    all_to_all x2, waiting for transfers between devices, body(): done = exchange(convolve(g, twist, ahead, back, signals[g], filters))  110 us
    all_to_all x2, waiting for transfers between devices, body(): exchange(pack_signal(keyval, g, cycle, unit))  108 us
    all_gather x2, waiting for transfers between devices, body(): lax.all_gather(out_weight[:, low:high], 'seq', axis=0, tiled=True)  86.5 us
    all_to_all x1, waiting for transfers between devices, body(): filters = exchange(pack_filters(filter_values, cycle, chunks, unit))  65.8 us
    pallas_call x2, Pallas kernels, mix(): pl.pallas_call(functools.partial(mix_kernel, pieces), grid=(part // tile,...  47.8 us
    ppermute x2, waiting for transfers between devices, body(): lax.ppermute(own, 'tensor', [(t, (t + shift) % peers) for t in range(peer...  45.3 us
    pallas_call x2, Pallas kernels, convolve(): pl.pallas_call(conv_kernel, grid=(1,), out_shape=jax.ShapeDtypeStruct(sig...  41.2 us
    all_to_all x2, starting transfers between devices, body(): exchange(pack_signal(keyval, g, cycle, unit))  16.2 us
  transfers between devices with their start and end apart: 9, of which 7 were waited for; matrix products, arithmetic and copies ran while one was open for 1% of the time, Pallas kernels for 16%

profile of v10, /device:TPU:9, one launch (start us, length us, event | category | flops | bytes accessed | tf_op | source)
XLA Modules:
  0.0 599.2 jit_solution(11519081918186484199)
XLA Ops:
  6.5 0.0 copy-start
  6.5 0.0 all-gather.5.cloned.1.call-start
  6.5 3.4 slice.7
  9.9 0.0 all-gather.5.cloned.1.call-update
  10.0 0.0 all-gather.3.cloned.1.call-start
  10.0 2.7 slice.6
  12.7 0.0 all-gather.3.cloned.1.call-update
  12.7 8.3 %pack_filters.1 = bf16[16,2,256,128]{3,2,1,0:T(8,128)(2,1)} custom-call(f32[256,1,4096]{2,1,0:T(1,128)} %bitcast.10), custom_call_target="tpu_custom_call" | custom-call | bytes 6291456 | tf_op jit(solution)/shard_map/pack_filters/pallas_call | solution.py:205
  21.0 6.6 %all-to-all-start.1 = ((bf16[16,2,256,128]{3,2,1,0:T(8,128)(2,1)}), bf16[16,2,256,128]{3,2,1,0:T(8,128)(2,1)S(1)}, u32[]{:S(2)}, u32[]{:S(2)}) async-start(bf16[16,2,256,128]{3,2,1,0:T(8,128)(2,1)} %pack_filters.1), calls=%async_computation.1 | async-start | bytes 4194304 | tf_op jit(solution)/shard_map/all_to_all | solution.py:314
  27.5 4.0 pack_signal.3
  31.6 65.8 %all-to-all-done.1.filter_ref = bf16[16,2,256,128]{3,2,1,0:T(8,128)(2,1)S(1)} async-done(((bf16[16,2,256,128]{3,2,1,0:T(8,128)(2,1)}), bf16[16,2,256,128]{3,2,1,0:T(8,128)(2,1)S(1)}, u32[]{:S(2)}, u32[]{:S(2)}) %all-to-all-start.1) | async-done | bytes 2097184 | tf_op jit(solution)/shard_map/all_to_all | solution.py:314
  97.4 1.4 copy-done.5
  98.7 8.1 %all-to-all-start.3 = ((bf16[16,512,128]{2,1,0:T(8,128)(2,1)}), bf16[16,512,128]{2,1,0:T(8,128)(2,1)}, u32[]{:S(2)}, u32[]{:S(2)}) async-start(bf16[16,512,128]{2,1,0:T(8,128)(2,1)} %pack_signal.3), calls=%async_computation.3 | async-start | bytes 4194304 | tf_op jit(solution)/shard_map/all_to_all | solution.py:313
  106.8 3.9 pack_signal.2
  110.7 66.0 %all-to-all-done.3.x_ref = bf16[16,512,128]{2,1,0:T(8,128)(2,1)} async-done(((bf16[16,512,128]{2,1,0:T(8,128)(2,1)}), bf16[16,512,128]{2,1,0:T(8,128)(2,1)}, u32[]{:S(2)}, u32[]{:S(2)}) %all-to-all-start.3) | async-done | bytes 2097184 | tf_op jit(solution)/shard_map/all_to_all | solution.py:313
  176.7 8.1 %all-to-all-start = ((bf16[16,512,128]{2,1,0:T(8,128)(2,1)}), bf16[16,512,128]{2,1,0:T(8,128)(2,1)}, u32[]{:S(2)}, u32[]{:S(2)}) async-start(bf16[16,512,128]{2,1,0:T(8,128)(2,1)} %pack_signal.2), calls=%async_computation | async-start | bytes 4194304 | tf_op jit(solution)/shard_map/all_to_all | solution.py:313
  184.9 0.0 copy-done
  184.9 0.6 gather_fusion
  185.5 0.1 select_multiply_fusion
  185.5 0.1 add.116
  185.6 0.1 add.117
  185.7 0.1 add.119
  185.8 0.1 fusion.22
  186.0 0.1 copy.8.twist_ref
  186.2 2.3 negate_convert_fusion
  188.4 0.1 maximum_maximum_fusion.1.back_ref
  188.5 2.5 fusion.15
  191.0 0.1 maximum_maximum_fusion.ahead_ref
  191.2 20.6 %convolve.3 = bf16[16,512,128]{2,1,0:T(8,128)(2,1)S(1)} custom-call(f32[512,32]{1,0:T(8,128)S(1)} %copy.8.twist_ref, bf16[2,256,1024]{2,1,0:T(8,128)(2,1)S(1)} %maximum_maximum_fusion.ahead_ref, bf16[2,1024,256]{2,1,0:T(8,128)(2,1)S(1)} %maximum_maximum_fusion.1.back_ref, bf16[16,512,128]{2,1,0:T(8,128)(2,1)} %all-to-all-done.3.x_ref, ...), custom_call_target="tpu_custom_call" | custom-call | flops 2147483648 | bytes 16777216 | tf_op jit(solution)/shard_map/convolve/pallas_call | solution.py:147
  211.7 0.0 copy-start.3
  211.7 1.4 copy-done.3
  213.1 41.7 %all-to-all-done.x_ref = bf16[16,512,128]{2,1,0:T(8,128)(2,1)} async-done(((bf16[16,512,128]{2,1,0:T(8,128)(2,1)}), bf16[16,512,128]{2,1,0:T(8,128)(2,1)}, u32[]{:S(2)}, u32[]{:S(2)}) %all-to-all-start) | async-done | bytes 2097184 | tf_op jit(solution)/shard_map/all_to_all | solution.py:313
  254.8 8.1 %all-to-all-start.4 = ((bf16[16,512,128]{2,1,0:T(8,128)(2,1)}), bf16[16,512,128]{2,1,0:T(8,128)(2,1)}, u32[]{:S(2)}, u32[]{:S(2)}) async-start(bf16[16,512,128]{2,1,0:T(8,128)(2,1)} %copy-done.3), calls=%async_computation.4 | async-start | bytes 4194304 | tf_op jit(solution)/shard_map/all_to_all | solution.py:339
  262.9 20.6 %convolve.2 = bf16[16,512,128]{2,1,0:T(8,128)(2,1)S(1)} custom-call(f32[512,32]{1,0:T(8,128)S(1)} %copy.8.twist_ref, bf16[2,256,1024]{2,1,0:T(8,128)(2,1)S(1)} %maximum_maximum_fusion.ahead_ref, bf16[2,1024,256]{2,1,0:T(8,128)(2,1)S(1)} %maximum_maximum_fusion.1.back_ref, bf16[16,512,128]{2,1,0:T(8,128)(2,1)} %all-to-all-done.x_ref, ...), custom_call_target="tpu_custom_call" | custom-call | flops 2147483648 | bytes 16777216 | tf_op jit(solution)/shard_map/convolve/pallas_call | solution.py:147
  283.5 1.3 copy-done.2
  284.8 48.0 %all-to-all-done.4.c_ref = bf16[16,512,128]{2,1,0:T(8,128)(2,1)} async-done(((bf16[16,512,128]{2,1,0:T(8,128)(2,1)}), bf16[16,512,128]{2,1,0:T(8,128)(2,1)}, u32[]{:S(2)}, u32[]{:S(2)}) %all-to-all-start.4) | async-done | bytes 2097184 | tf_op jit(solution)/shard_map/all_to_all | solution.py:339
  332.8 6.1 %all-to-all-start.2 = ((bf16[16,512,128]{2,1,0:T(8,128)(2,1)}), bf16[16,512,128]{2,1,0:T(8,128)(2,1)S(1)}, u32[]{:S(2)}, u32[]{:S(2)}) async-start(bf16[16,512,128]{2,1,0:T(8,128)(2,1)} %copy-done.2), calls=%async_computation.2 | async-start | bytes 4194304 | tf_op jit(solution)/shard_map/all_to_all | solution.py:339
  338.9 5.2 gate.3.refs_2_
  344.1 1.2 collective-permute-start.1
  345.3 61.6 %all-to-all-done.2.c_ref = bf16[16,512,128]{2,1,0:T(8,128)(2,1)S(1)} async-done(((bf16[16,512,128]{2,1,0:T(8,128)(2,1)}), bf16[16,512,128]{2,1,0:T(8,128)(2,1)S(1)}, u32[]{:S(2)}, u32[]{:S(2)}) %all-to-all-start.2) | async-done | bytes 2097184 | tf_op jit(solution)/shard_map/all_to_all | solution.py:339
  406.9 4.6 gate.2.refs_0_
  411.5 1.2 collective-permute-start
  412.7 0.1 pad_add_fusion.start_ref
  412.8 0.0 collective-permute-done.1.refs_3_
  412.8 45.3 %collective-permute-done.refs_1_ = bf16[512,2048]{1,0:T(8,128)(2,1)S(1)} collective-permute-done((bf16[512,2048]{1,0:T(8,128)(2,1)}, bf16[512,2048]{1,0:T(8,128)(2,1)S(1)}, u32[]{:S(2)}, u32[]{:S(2)}) %collective-permute-start) | collective-permute-done | bytes 2097184 | tf_op jit(solution)/shard_map/ppermute | solution.py:345
  458.0 28.8 %mix.2.refs_5_ = bf16[512,4096]{1,0:T(8,128)(2,1)} custom-call(s32[4]{0:T(128)S(1)} %pad_add_fusion.start_ref, bf16[512,2048]{1,0:T(8,128)(2,1)} %gate.2.refs_0_, bf16[512,2048]{1,0:T(8,128)(2,1)S(1)} %collective-permute-done.refs_1_, bf16[512,2048]{1,0:T(8,128)(2,1)} %gate.3.refs_2_, bf16[512,2048]{1,0:T(8,128)(2,1)} %collective-permute-done.1.refs_3_, ...), custom_call_target="tpu_custom_call" | custom-call | flops 21474836480 | bytes 41943040 | tf_op jit(solution)/shard_map/mix/pallas_call | solution.py:271
  486.8 86.5 %all-gather.3.cloned.1.call-done.refs_4_ = bf16[8192,1536]{1,0:T(8,128)(2,1)} async-done(((bf16[512,1536]{1,0:T(8,128)(2,1)}), bf16[8192,1536]{1,0:T(8,128)(2,1)}) %all-gather.3.cloned.1.call-update) | async-done | bytes 25165840 | tf_op jit(solution)/shard_map/all_gather | solution.py:306
  573.3 19.0 %mix.3 = bf16[512,4096]{1,0:T(8,128)(2,1)} custom-call(s32[4]{0:T(128)S(1)} %pad_add_fusion.start_ref, bf16[512,2048]{1,0:T(8,128)(2,1)} %gate.2.refs_0_, bf16[512,2048]{1,0:T(8,128)(2,1)S(1)} %collective-permute-done.refs_1_, bf16[512,2048]{1,0:T(8,128)(2,1)} %gate.3.refs_2_, ...), custom_call_target="tpu_custom_call", output_to_operand_aliasing={{}: (6, {})} | custom-call | flops 12884901888 | bytes 25165824 | tf_op jit(solution)/shard_map/mix/pallas_call | solution.py:271
  (13 shorter events, 0.1 us)
Async XLA Ops:
  6.5 178.4 %copy-start = (s32[32,32]{1,0:T(8,128)S(1)}, s32[32,32]{1,0:T(8,128)}, u32[]{:S(2)}) copy-start(s32[32,32]{1,0:T(8,128)} %param.10) | copy-start | bytes 12292
  6.5 451.5 %all-gather.5.cloned.1.call-start = ((), (), s32[]{:S(2)}) async-start(), calls=%async_computation.6 | async-start | bytes 44564480 | tf_op jit(solution)/shard_map/all_gather | solution.py:306
  10.0 563.3 %all-gather.3.cloned.1.call-start = ((), (), s32[]{:S(2)}) async-start(), calls=%async_computation.5 | async-start | bytes 26738688 | tf_op jit(solution)/shard_map/all_gather | solution.py:306
  21.0 76.4 %all-to-all-start.1 = ((bf16[16,2,256,128]{3,2,1,0:T(8,128)(2,1)}), bf16[16,2,256,128]{3,2,1,0:T(8,128)(2,1)S(1)}, u32[]{:S(2)}, u32[]{:S(2)}) async-start(bf16[16,2,256,128]{3,2,1,0:T(8,128)(2,1)} %pack_filters.1), calls=%async_computation.1 | async-start | bytes 4194304 | tf_op jit(solution)/shard_map/all_to_all | solution.py:314
  97.4 1.4 copy-start.5
  98.7 78.0 %all-to-all-start.3 = ((bf16[16,512,128]{2,1,0:T(8,128)(2,1)}), bf16[16,512,128]{2,1,0:T(8,128)(2,1)}, u32[]{:S(2)}, u32[]{:S(2)}) async-start(bf16[16,512,128]{2,1,0:T(8,128)(2,1)} %pack_signal.3), calls=%async_computation.3 | async-start | bytes 4194304 | tf_op jit(solution)/shard_map/all_to_all | solution.py:313
  176.7 78.0 %all-to-all-start = ((bf16[16,512,128]{2,1,0:T(8,128)(2,1)}), bf16[16,512,128]{2,1,0:T(8,128)(2,1)}, u32[]{:S(2)}, u32[]{:S(2)}) async-start(bf16[16,512,128]{2,1,0:T(8,128)(2,1)} %pack_signal.2), calls=%async_computation | async-start | bytes 4194304 | tf_op jit(solution)/shard_map/all_to_all | solution.py:313
  211.7 1.4 copy-start.3
  254.8 78.0 %all-to-all-start.4 = ((bf16[16,512,128]{2,1,0:T(8,128)(2,1)}), bf16[16,512,128]{2,1,0:T(8,128)(2,1)}, u32[]{:S(2)}, u32[]{:S(2)}) async-start(bf16[16,512,128]{2,1,0:T(8,128)(2,1)} %copy-done.3), calls=%async_computation.4 | async-start | bytes 4194304 | tf_op jit(solution)/shard_map/all_to_all | solution.py:339
  283.5 1.3 copy-start.2
  284.8 54.1 %copy-start.4 = (f32[4096]{0:T(1024)S(1)}, f32[4096]{0:T(1024)}, u32[]{:S(2)}) copy-start(f32[4096]{0:T(1024)} %param.8) | copy-start | bytes 49156
  332.8 74.1 %all-to-all-start.2 = ((bf16[16,512,128]{2,1,0:T(8,128)(2,1)}), bf16[16,512,128]{2,1,0:T(8,128)(2,1)S(1)}, u32[]{:S(2)}, u32[]{:S(2)}) async-start(bf16[16,512,128]{2,1,0:T(8,128)(2,1)} %copy-done.2), calls=%async_computation.2 | async-start | bytes 4194304 | tf_op jit(solution)/shard_map/all_to_all | solution.py:339
  344.1 68.7 %collective-permute-start.1 = (bf16[512,2048]{1,0:T(8,128)(2,1)}, bf16[512,2048]{1,0:T(8,128)(2,1)}, u32[]{:S(2)}, u32[]{:S(2)}) collective-permute-start(bf16[512,2048]{1,0:T(8,128)(2,1)} %gate.3.refs_2_), channel_id=1, source_target_pairs={{0,1},{1,0},{2,3},{3,2},{4,5},{5,4},{6,7},{7,6},{8,9},{9,8},{10,11... | collective-permute-start | bytes 6291464 | tf_op jit(solution)/shard_map/ppermute | solution.py:345
  411.5 46.5 %collective-permute-start = (bf16[512,2048]{1,0:T(8,128)(2,1)}, bf16[512,2048]{1,0:T(8,128)(2,1)S(1)}, u32[]{:S(2)}, u32[]{:S(2)}) collective-permute-start(bf16[512,2048]{1,0:T(8,128)(2,1)} %gate.2.refs_0_), channel_id=1, source_target_pairs={{0,1},{1,0},{2,3},{3,2},{4,5},{5,4},{6,7},{7,6},{8,9},{9,8},{10,11... | collective-permute-start | bytes 6291464 | tf_op jit(solution)/shard_map/ppermute | solution.py:345
  573.3 19.0 %copy-start.1 = (s32[32,32]{1,0:T(8,128)S(1)}, s32[32,32]{1,0:T(8,128)}, u32[]{:S(2)}) copy-start(s32[32,32]{1,0:T(8,128)} %param.10) | copy-start | bytes 12292
Sparse Core Ops, SparseCore 0:
  10.1 433.8 all-gather.4
  445.6 127.6 all-gather.2

commit v11 on v10

--- a/solution.py
+++ b/solution.py
@@ -264,7 +264,7 @@
 def mix(hidden, starts, weight, low, columns, result):
     tokens = hidden[0].shape[0]
     depth, part = weight.shape
-    tile = min(256, part)
+    tile = min(512, part)
     first = low // tile
     pieces = len(hidden)
     before = [] if result is None else [result]
@@ -278,7 +278,7 @@
         + [pl.BlockSpec(memory_space=pl.ANY) for _ in before],
         out_specs=pl.BlockSpec((tokens, tile), lambda i: (0, first + i)),
         input_output_aliases={pieces + 2: 0} if before else {},
-        compiler_params=pltpu.CompilerParams(vmem_limit_bytes=32 * 2**20),
+        compiler_params=pltpu.CompilerParams(vmem_limit_bytes=40 * 2**20),
         cost_estimate=pl.CostEstimate(
             flops=2 * tokens * depth * part, bytes_accessed=2 * depth * part, transcendentals=0
         ),

time: 601 us -> 602 us (level)
  no operation moved by 1% of the time
where the time goes in v11:
time: 602 us; the launch traced here: 600 us
  waiting for transfers between devices  415 us (69%)
  Pallas kernels  116 us (19%)
  starting transfers between devices  39.3 us (7%)
  between operations  13.5 us (2%)
  local copies, waits for them, and re-layouts  11.1 us (2%)
    all_to_all x2, waiting for transfers between devices, body(): done = exchange(convolve(g, twist, ahead, back, signals[g], filters))  110 us
    all_to_all x2, waiting for transfers between devices, body(): exchange(pack_signal(keyval, g, cycle, unit))  108 us
    all_gather x2, waiting for transfers between devices, body(): lax.all_gather(out_weight[:, low:high], 'seq', axis=0, tiled=True)  86.4 us
    all_to_all x1, waiting for transfers between devices, body(): filters = exchange(pack_filters(filter_values, cycle, chunks, unit))  65.8 us
    pallas_call x2, Pallas kernels, mix(): pl.pallas_call(functools.partial(mix_kernel, pieces), grid=(part // tile,...  48.4 us
    ppermute x2, waiting for transfers between devices, body(): lax.ppermute(own, 'tensor', [(t, (t + shift) % peers) for t in range(peer...  45.3 us
    pallas_call x2, Pallas kernels, convolve(): pl.pallas_call(conv_kernel, grid=(1,), out_shape=jax.ShapeDtypeStruct(sig...  41.2 us
    all_to_all x2, starting transfers between devices, body(): exchange(pack_signal(keyval, g, cycle, unit))  16.2 us
  transfers between devices with their start and end apart: 9, of which 7 were waited for; matrix products, arithmetic and copies ran while one was open for 1% of the time, Pallas kernels for 16%

profile of v11, /device:TPU:9, one launch (start us, length us, event | category | flops | bytes accessed | tf_op | source)
XLA Modules:
  0.0 599.7 jit_solution(10243516997113458977)
XLA Ops:
  6.5 0.0 copy-start
  6.5 0.0 all-gather.5.cloned.1.call-start
  6.5 3.4 slice.7
  9.9 0.0 all-gather.5.cloned.1.call-update
  10.0 0.0 all-gather.3.cloned.1.call-start
  10.0 2.7 slice.6
  12.7 0.0 all-gather.3.cloned.1.call-update
  12.7 8.3 %pack_filters.1 = bf16[16,2,256,128]{3,2,1,0:T(8,128)(2,1)} custom-call(f32[256,1,4096]{2,1,0:T(1,128)} %bitcast.10), custom_call_target="tpu_custom_call" | custom-call | bytes 6291456 | tf_op jit(solution)/shard_map/pack_filters/pallas_call | solution.py:205
  21.0 6.6 %all-to-all-start.1 = ((bf16[16,2,256,128]{3,2,1,0:T(8,128)(2,1)}), bf16[16,2,256,128]{3,2,1,0:T(8,128)(2,1)S(1)}, u32[]{:S(2)}, u32[]{:S(2)}) async-start(bf16[16,2,256,128]{3,2,1,0:T(8,128)(2,1)} %pack_filters.1), calls=%async_computation.1 | async-start | bytes 4194304 | tf_op jit(solution)/shard_map/all_to_all | solution.py:314
  27.5 4.0 pack_signal.3
  31.6 65.8 %all-to-all-done.1.filter_ref = bf16[16,2,256,128]{3,2,1,0:T(8,128)(2,1)S(1)} async-done(((bf16[16,2,256,128]{3,2,1,0:T(8,128)(2,1)}), bf16[16,2,256,128]{3,2,1,0:T(8,128)(2,1)S(1)}, u32[]{:S(2)}, u32[]{:S(2)}) %all-to-all-start.1) | async-done | bytes 2097184 | tf_op jit(solution)/shard_map/all_to_all | solution.py:314
  97.4 1.4 copy-done.5
  98.7 8.1 %all-to-all-start.3 = ((bf16[16,512,128]{2,1,0:T(8,128)(2,1)}), bf16[16,512,128]{2,1,0:T(8,128)(2,1)}, u32[]{:S(2)}, u32[]{:S(2)}) async-start(bf16[16,512,128]{2,1,0:T(8,128)(2,1)} %pack_signal.3), calls=%async_computation.3 | async-start | bytes 4194304 | tf_op jit(solution)/shard_map/all_to_all | solution.py:313
  106.8 3.9 pack_signal.2
  110.7 66.0 %all-to-all-done.3.x_ref = bf16[16,512,128]{2,1,0:T(8,128)(2,1)} async-done(((bf16[16,512,128]{2,1,0:T(8,128)(2,1)}), bf16[16,512,128]{2,1,0:T(8,128)(2,1)}, u32[]{:S(2)}, u32[]{:S(2)}) %all-to-all-start.3) | async-done | bytes 2097184 | tf_op jit(solution)/shard_map/all_to_all | solution.py:313
  176.7 8.1 %all-to-all-start = ((bf16[16,512,128]{2,1,0:T(8,128)(2,1)}), bf16[16,512,128]{2,1,0:T(8,128)(2,1)}, u32[]{:S(2)}, u32[]{:S(2)}) async-start(bf16[16,512,128]{2,1,0:T(8,128)(2,1)} %pack_signal.2), calls=%async_computation | async-start | bytes 4194304 | tf_op jit(solution)/shard_map/all_to_all | solution.py:313
  184.9 0.6 gather_fusion
  185.5 0.1 select_multiply_fusion
  185.5 0.1 add.116
  185.6 0.1 add.117
  185.7 0.1 add.119
  185.8 0.1 fusion.22
  186.0 0.1 copy.8.twist_ref
  186.2 2.3 negate_convert_fusion
  188.4 0.1 maximum_maximum_fusion.1.back_ref
  188.5 2.5 fusion.15
  191.0 0.1 maximum_maximum_fusion.ahead_ref
  191.2 20.6 %convolve.3 = bf16[16,512,128]{2,1,0:T(8,128)(2,1)S(1)} custom-call(f32[512,32]{1,0:T(8,128)S(1)} %copy.8.twist_ref, bf16[2,256,1024]{2,1,0:T(8,128)(2,1)S(1)} %maximum_maximum_fusion.ahead_ref, bf16[2,1024,256]{2,1,0:T(8,128)(2,1)S(1)} %maximum_maximum_fusion.1.back_ref, bf16[16,512,128]{2,1,0:T(8,128)(2,1)} %all-to-all-done.3.x_ref, ...), custom_call_target="tpu_custom_call" | custom-call | flops 2147483648 | bytes 16777216 | tf_op jit(solution)/shard_map/convolve/pallas_call | solution.py:147
  211.7 1.4 copy-done.3
  213.1 41.7 %all-to-all-done.x_ref = bf16[16,512,128]{2,1,0:T(8,128)(2,1)} async-done(((bf16[16,512,128]{2,1,0:T(8,128)(2,1)}), bf16[16,512,128]{2,1,0:T(8,128)(2,1)}, u32[]{:S(2)}, u32[]{:S(2)}) %all-to-all-start) | async-done | bytes 2097184 | tf_op jit(solution)/shard_map/all_to_all | solution.py:313
  254.8 8.1 %all-to-all-start.4 = ((bf16[16,512,128]{2,1,0:T(8,128)(2,1)}), bf16[16,512,128]{2,1,0:T(8,128)(2,1)}, u32[]{:S(2)}, u32[]{:S(2)}) async-start(bf16[16,512,128]{2,1,0:T(8,128)(2,1)} %copy-done.3), calls=%async_computation.4 | async-start | bytes 4194304 | tf_op jit(solution)/shard_map/all_to_all | solution.py:339
  262.9 20.6 %convolve.2 = bf16[16,512,128]{2,1,0:T(8,128)(2,1)S(1)} custom-call(f32[512,32]{1,0:T(8,128)S(1)} %copy.8.twist_ref, bf16[2,256,1024]{2,1,0:T(8,128)(2,1)S(1)} %maximum_maximum_fusion.ahead_ref, bf16[2,1024,256]{2,1,0:T(8,128)(2,1)S(1)} %maximum_maximum_fusion.1.back_ref, bf16[16,512,128]{2,1,0:T(8,128)(2,1)} %all-to-all-done.x_ref, ...), custom_call_target="tpu_custom_call" | custom-call | flops 2147483648 | bytes 16777216 | tf_op jit(solution)/shard_map/convolve/pallas_call | solution.py:147
  283.5 0.0 copy-start.2
  283.5 1.3 copy-done.2
  284.8 48.0 %all-to-all-done.4.c_ref = bf16[16,512,128]{2,1,0:T(8,128)(2,1)} async-done(((bf16[16,512,128]{2,1,0:T(8,128)(2,1)}), bf16[16,512,128]{2,1,0:T(8,128)(2,1)}, u32[]{:S(2)}, u32[]{:S(2)}) %all-to-all-start.4) | async-done | bytes 2097184 | tf_op jit(solution)/shard_map/all_to_all | solution.py:339
  332.8 6.1 %all-to-all-start.2 = ((bf16[16,512,128]{2,1,0:T(8,128)(2,1)}), bf16[16,512,128]{2,1,0:T(8,128)(2,1)S(1)}, u32[]{:S(2)}, u32[]{:S(2)}) async-start(bf16[16,512,128]{2,1,0:T(8,128)(2,1)} %copy-done.2), calls=%async_computation.2 | async-start | bytes 4194304 | tf_op jit(solution)/shard_map/all_to_all | solution.py:339
  338.9 0.0 copy-done.4
  338.9 5.2 gate.3.refs_2_
  344.1 1.2 collective-permute-start.1
  345.3 61.6 %all-to-all-done.2.c_ref = bf16[16,512,128]{2,1,0:T(8,128)(2,1)S(1)} async-done(((bf16[16,512,128]{2,1,0:T(8,128)(2,1)}), bf16[16,512,128]{2,1,0:T(8,128)(2,1)S(1)}, u32[]{:S(2)}, u32[]{:S(2)}) %all-to-all-start.2) | async-done | bytes 2097184 | tf_op jit(solution)/shard_map/all_to_all | solution.py:339
  406.9 4.6 gate.2.refs_0_
  411.5 1.2 collective-permute-start
  412.7 0.1 pad_add_fusion.start_ref
  412.8 0.0 collective-permute-done.1.refs_3_
  412.8 45.3 %collective-permute-done.refs_1_ = bf16[512,2048]{1,0:T(8,128)(2,1)S(1)} collective-permute-done((bf16[512,2048]{1,0:T(8,128)(2,1)}, bf16[512,2048]{1,0:T(8,128)(2,1)S(1)}, u32[]{:S(2)}, u32[]{:S(2)}) %collective-permute-start) | collective-permute-done | bytes 2097184 | tf_op jit(solution)/shard_map/ppermute | solution.py:345
  458.0 28.8 %mix.2.refs_5_ = bf16[512,4096]{1,0:T(8,128)(2,1)} custom-call(s32[4]{0:T(128)S(1)} %pad_add_fusion.start_ref, bf16[512,2048]{1,0:T(8,128)(2,1)} %gate.2.refs_0_, bf16[512,2048]{1,0:T(8,128)(2,1)S(1)} %collective-permute-done.refs_1_, bf16[512,2048]{1,0:T(8,128)(2,1)} %gate.3.refs_2_, bf16[512,2048]{1,0:T(8,128)(2,1)} %collective-permute-done.1.refs_3_, ...), custom_call_target="tpu_custom_call" | custom-call | flops 21474836480 | bytes 41943040 | tf_op jit(solution)/shard_map/mix/pallas_call | solution.py:271
  486.9 86.4 %all-gather.3.cloned.1.call-done.refs_4_ = bf16[8192,1536]{1,0:T(8,128)(2,1)} async-done(((bf16[512,1536]{1,0:T(8,128)(2,1)}), bf16[8192,1536]{1,0:T(8,128)(2,1)}) %all-gather.3.cloned.1.call-update) | async-done | bytes 25165840 | tf_op jit(solution)/shard_map/all_gather | solution.py:306
  573.3 19.5 %mix.3 = bf16[512,4096]{1,0:T(8,128)(2,1)} custom-call(s32[4]{0:T(128)S(1)} %pad_add_fusion.start_ref, bf16[512,2048]{1,0:T(8,128)(2,1)} %gate.2.refs_0_, bf16[512,2048]{1,0:T(8,128)(2,1)S(1)} %collective-permute-done.refs_1_, bf16[512,2048]{1,0:T(8,128)(2,1)} %gate.3.refs_2_, ...), custom_call_target="tpu_custom_call", output_to_operand_aliasing={{}: (6, {})} | custom-call | flops 12884901888 | bytes 25165824 | tf_op jit(solution)/shard_map/mix/pallas_call | solution.py:271
  (13 shorter events, 0.1 us)
Async XLA Ops:
  6.5 178.4 %copy-start = (s32[32,32]{1,0:T(8,128)S(1)}, s32[32,32]{1,0:T(8,128)}, u32[]{:S(2)}) copy-start(s32[32,32]{1,0:T(8,128)} %param.10) | copy-start | bytes 12292
  6.5 451.5 %all-gather.5.cloned.1.call-start = ((), (), s32[]{:S(2)}) async-start(), calls=%async_computation.6 | async-start | bytes 44564480 | tf_op jit(solution)/shard_map/all_gather | solution.py:306
  10.0 563.3 %all-gather.3.cloned.1.call-start = ((), (), s32[]{:S(2)}) async-start(), calls=%async_computation.5 | async-start | bytes 26738688 | tf_op jit(solution)/shard_map/all_gather | solution.py:306
  21.0 76.4 %all-to-all-start.1 = ((bf16[16,2,256,128]{3,2,1,0:T(8,128)(2,1)}), bf16[16,2,256,128]{3,2,1,0:T(8,128)(2,1)S(1)}, u32[]{:S(2)}, u32[]{:S(2)}) async-start(bf16[16,2,256,128]{3,2,1,0:T(8,128)(2,1)} %pack_filters.1), calls=%async_computation.1 | async-start | bytes 4194304 | tf_op jit(solution)/shard_map/all_to_all | solution.py:314
  97.4 1.4 copy-start.5
  98.7 78.0 %all-to-all-start.3 = ((bf16[16,512,128]{2,1,0:T(8,128)(2,1)}), bf16[16,512,128]{2,1,0:T(8,128)(2,1)}, u32[]{:S(2)}, u32[]{:S(2)}) async-start(bf16[16,512,128]{2,1,0:T(8,128)(2,1)} %pack_signal.3), calls=%async_computation.3 | async-start | bytes 4194304 | tf_op jit(solution)/shard_map/all_to_all | solution.py:313
  176.7 78.0 %all-to-all-start = ((bf16[16,512,128]{2,1,0:T(8,128)(2,1)}), bf16[16,512,128]{2,1,0:T(8,128)(2,1)}, u32[]{:S(2)}, u32[]{:S(2)}) async-start(bf16[16,512,128]{2,1,0:T(8,128)(2,1)} %pack_signal.2), calls=%async_computation | async-start | bytes 4194304 | tf_op jit(solution)/shard_map/all_to_all | solution.py:313
  211.7 1.4 copy-start.3
  254.8 78.0 %all-to-all-start.4 = ((bf16[16,512,128]{2,1,0:T(8,128)(2,1)}), bf16[16,512,128]{2,1,0:T(8,128)(2,1)}, u32[]{:S(2)}, u32[]{:S(2)}) async-start(bf16[16,512,128]{2,1,0:T(8,128)(2,1)} %copy-done.3), calls=%async_computation.4 | async-start | bytes 4194304 | tf_op jit(solution)/shard_map/all_to_all | solution.py:339
  283.5 1.3 copy-start.2
  284.8 54.1 %copy-start.4 = (f32[4096]{0:T(1024)S(1)}, f32[4096]{0:T(1024)}, u32[]{:S(2)}) copy-start(f32[4096]{0:T(1024)} %param.8) | copy-start | bytes 49156
  332.8 74.1 %all-to-all-start.2 = ((bf16[16,512,128]{2,1,0:T(8,128)(2,1)}), bf16[16,512,128]{2,1,0:T(8,128)(2,1)S(1)}, u32[]{:S(2)}, u32[]{:S(2)}) async-start(bf16[16,512,128]{2,1,0:T(8,128)(2,1)} %copy-done.2), calls=%async_computation.2 | async-start | bytes 4194304 | tf_op jit(solution)/shard_map/all_to_all | solution.py:339
  344.1 68.7 %collective-permute-start.1 = (bf16[512,2048]{1,0:T(8,128)(2,1)}, bf16[512,2048]{1,0:T(8,128)(2,1)}, u32[]{:S(2)}, u32[]{:S(2)}) collective-permute-start(bf16[512,2048]{1,0:T(8,128)(2,1)} %gate.3.refs_2_), channel_id=1, source_target_pairs={{0,1},{1,0},{2,3},{3,2},{4,5},{5,4},{6,7},{7,6},{8,9},{9,8},{10,11... | collective-permute-start | bytes 6291464 | tf_op jit(solution)/shard_map/ppermute | solution.py:345
  411.5 46.5 %collective-permute-start = (bf16[512,2048]{1,0:T(8,128)(2,1)}, bf16[512,2048]{1,0:T(8,128)(2,1)S(1)}, u32[]{:S(2)}, u32[]{:S(2)}) collective-permute-start(bf16[512,2048]{1,0:T(8,128)(2,1)} %gate.2.refs_0_), channel_id=1, source_target_pairs={{0,1},{1,0},{2,3},{3,2},{4,5},{5,4},{6,7},{7,6},{8,9},{9,8},{10,11... | collective-permute-start | bytes 6291464 | tf_op jit(solution)/shard_map/ppermute | solution.py:345
  573.3 19.5 %copy-start.1 = (s32[32,32]{1,0:T(8,128)S(1)}, s32[32,32]{1,0:T(8,128)}, u32[]{:S(2)}) copy-start(s32[32,32]{1,0:T(8,128)} %param.10) | copy-start | bytes 12292
Sparse Core Ops, SparseCore 0:
  10.1 433.8 all-gather.4
  445.6 127.6 all-gather.2

commit v12 on v9

--- a/solution.py
+++ b/solution.py
@@ -301,7 +301,7 @@
 
     columns = out_weight.shape[1]
     eighth = columns // 8
-    bounds = [0, 5 * eighth, columns] if eighth % 256 == 0 else [0, columns]
+    bounds = [0, eighth, 5 * eighth, columns] if eighth % 256 == 0 else [0, columns]
     weights = [
         lax.all_gather(out_weight[:, low:high], "seq", axis=0, tiled=True)
         for low, high in zip(bounds[:-1], bounds[1:])

time: 601 us -> 622 us (1.035)
  waiting for transfers between devices: 415 us -> 424 us
    all_to_all x1, waiting for transfers between devices: 65.8 us -> 79.1 us  [body(): filters = exchange(pack_filters(filter_values, cycle, chunks, unit))]
    pallas_call x2 -> x3, Pallas kernels: 47.8 us -> 55.2 us  [mix(): pl.pallas_call(functools.partial(mix_kernel, pieces), grid=(part // tile,...]
    all_gather x2 -> x3, waiting for transfers between devices: 86.5 us -> 86.8 us  [body(): lax.all_gather(out_weight[:, low:high], 'seq', axis=0, tiled=True)]
  transfers between devices with their start and end apart: 9 -> 10, of which waited for: 7 -> 7; matrix products, arithmetic and copies ran while one was open for 1% -> 2% of each run, Pallas kernels for 16% -> 16%
where the time goes in v12:
time: 622 us; the launch traced here: 620 us
  waiting for transfers between devices  424 us (68%)
  Pallas kernels  121 us (19%)
  starting transfers between devices  43.1 us (7%)
  between operations  13.3 us (2%)
  local copies, waits for them, and re-layouts  12.7 us (2%)
    all_to_all x2, waiting for transfers between devices, body(): done = exchange(convolve(g, twist, ahead, back, signals[g], filters))  111 us
    all_to_all x2, waiting for transfers between devices, body(): exchange(pack_signal(keyval, g, cycle, unit))  102 us
    all_gather x3, waiting for transfers between devices, body(): lax.all_gather(out_weight[:, low:high], 'seq', axis=0, tiled=True)  86.8 us
    all_to_all x1, waiting for transfers between devices, body(): filters = exchange(pack_filters(filter_values, cycle, chunks, unit))  79.1 us
    pallas_call x3, Pallas kernels, mix(): pl.pallas_call(functools.partial(mix_kernel, pieces), grid=(part // tile,...  55.2 us
    ppermute x2, waiting for transfers between devices, body(): lax.ppermute(own, 'tensor', [(t, (t + shift) % peers) for t in range(peer...  45.1 us
    pallas_call x2, Pallas kernels, convolve(): pl.pallas_call(conv_kernel, grid=(1,), out_shape=jax.ShapeDtypeStruct(sig...  41.1 us
    all_to_all x2, starting transfers between devices, body(): exchange(pack_signal(keyval, g, cycle, unit))  17.9 us
  transfers between devices with their start and end apart: 10, of which 7 were waited for; matrix products, arithmetic and copies ran while one was open for 2% of the time, Pallas kernels for 16%

profile of v12, /device:TPU:9, one launch (start us, length us, event | category | flops | bytes accessed | tf_op | source)
XLA Modules:
  0.0 619.9 jit_solution(10000065827721715851)
XLA Ops:
  6.5 1.9 slice.11
  8.5 0.0 all-gather.8.cloned.1.call-update
  8.5 0.0 all-gather.6.cloned.1.call-start
  8.6 3.2 slice.10
  11.8 0.0 all-gather.6.cloned.1.call-update
  11.8 0.0 all-gather.4.cloned.1.call-start
  11.8 2.7 slice.9
  14.5 0.0 all-gather.4.cloned.1.call-update
  14.5 8.1 %pack_filters.1 = bf16[16,2,256,128]{3,2,1,0:T(8,128)(2,1)} custom-call(f32[256,1,4096]{2,1,0:T(1,128)} %bitcast.10), custom_call_target="tpu_custom_call" | custom-call | bytes 6291456 | tf_op jit(solution)/shard_map/pack_filters/pallas_call | solution.py:205
  22.6 6.6 %all-to-all-start.1 = ((bf16[16,2,256,128]{3,2,1,0:T(8,128)(2,1)}), bf16[16,2,256,128]{3,2,1,0:T(8,128)(2,1)S(1)}, u32[]{:S(2)}, u32[]{:S(2)}) async-start(bf16[16,2,256,128]{3,2,1,0:T(8,128)(2,1)} %pack_filters.1), calls=%async_computation.1 | async-start | bytes 4194304 | tf_op jit(solution)/shard_map/all_to_all | solution.py:314
  29.2 3.9 pack_signal.3
  33.2 79.1 %all-to-all-done.1.filter_ref = bf16[16,2,256,128]{3,2,1,0:T(8,128)(2,1)S(1)} async-done(((bf16[16,2,256,128]{3,2,1,0:T(8,128)(2,1)}), bf16[16,2,256,128]{3,2,1,0:T(8,128)(2,1)S(1)}, u32[]{:S(2)}, u32[]{:S(2)}) %all-to-all-start.1) | async-done | bytes 2097184 | tf_op jit(solution)/shard_map/all_to_all | solution.py:314
  112.3 1.3 copy-done.6
  113.6 8.8 %all-to-all-start.3 = ((bf16[16,512,128]{2,1,0:T(8,128)(2,1)}), bf16[16,512,128]{2,1,0:T(8,128)(2,1)}, u32[]{:S(2)}, u32[]{:S(2)}) async-start(bf16[16,512,128]{2,1,0:T(8,128)(2,1)} %pack_signal.3), calls=%async_computation.3 | async-start | bytes 4194304 | tf_op jit(solution)/shard_map/all_to_all | solution.py:313
  122.4 3.9 pack_signal.2
  126.3 60.6 %all-to-all-done.3.x_ref = bf16[16,512,128]{2,1,0:T(8,128)(2,1)} async-done(((bf16[16,512,128]{2,1,0:T(8,128)(2,1)}), bf16[16,512,128]{2,1,0:T(8,128)(2,1)}, u32[]{:S(2)}, u32[]{:S(2)}) %all-to-all-start.3) | async-done | bytes 2097184 | tf_op jit(solution)/shard_map/all_to_all | solution.py:313
  186.9 9.2 %all-to-all-start = ((bf16[16,512,128]{2,1,0:T(8,128)(2,1)}), bf16[16,512,128]{2,1,0:T(8,128)(2,1)}, u32[]{:S(2)}, u32[]{:S(2)}) async-start(bf16[16,512,128]{2,1,0:T(8,128)(2,1)} %pack_signal.2), calls=%async_computation | async-start | bytes 4194304 | tf_op jit(solution)/shard_map/all_to_all | solution.py:313
  196.1 0.6 gather_fusion
  196.7 0.1 select_multiply_fusion
  196.7 0.1 add.116
  196.8 0.1 add.117
  196.9 0.1 add.119
  197.0 0.1 fusion.22
  197.2 0.1 copy.9.twist_ref
  197.4 2.3 negate_convert_fusion
  199.6 0.1 maximum_maximum_fusion.1.back_ref
  199.7 2.5 fusion.15
  202.2 0.1 maximum_maximum_fusion.ahead_ref
  202.4 20.6 %convolve.3 = bf16[16,512,128]{2,1,0:T(8,128)(2,1)S(1)} custom-call(f32[512,32]{1,0:T(8,128)S(1)} %copy.9.twist_ref, bf16[2,256,1024]{2,1,0:T(8,128)(2,1)S(1)} %maximum_maximum_fusion.ahead_ref, bf16[2,1024,256]{2,1,0:T(8,128)(2,1)S(1)} %maximum_maximum_fusion.1.back_ref, bf16[16,512,128]{2,1,0:T(8,128)(2,1)} %all-to-all-done.3.x_ref, ...), custom_call_target="tpu_custom_call" | custom-call | flops 2147483648 | bytes 16777216 | tf_op jit(solution)/shard_map/convolve/pallas_call | solution.py:147
  222.9 1.3 copy-done.4
  224.2 41.8 %all-to-all-done.x_ref = bf16[16,512,128]{2,1,0:T(8,128)(2,1)} async-done(((bf16[16,512,128]{2,1,0:T(8,128)(2,1)}), bf16[16,512,128]{2,1,0:T(8,128)(2,1)}, u32[]{:S(2)}, u32[]{:S(2)}) %all-to-all-start) | async-done | bytes 2097184 | tf_op jit(solution)/shard_map/all_to_all | solution.py:313
  266.0 8.0 %all-to-all-start.4 = ((bf16[16,512,128]{2,1,0:T(8,128)(2,1)}), bf16[16,512,128]{2,1,0:T(8,128)(2,1)}, u32[]{:S(2)}, u32[]{:S(2)}) async-start(bf16[16,512,128]{2,1,0:T(8,128)(2,1)} %copy-done.4), calls=%async_computation.4 | async-start | bytes 4194304 | tf_op jit(solution)/shard_map/all_to_all | solution.py:339
  274.0 20.6 %convolve.2 = bf16[16,512,128]{2,1,0:T(8,128)(2,1)S(1)} custom-call(f32[512,32]{1,0:T(8,128)S(1)} %copy.9.twist_ref, bf16[2,256,1024]{2,1,0:T(8,128)(2,1)S(1)} %maximum_maximum_fusion.ahead_ref, bf16[2,1024,256]{2,1,0:T(8,128)(2,1)S(1)} %maximum_maximum_fusion.1.back_ref, bf16[16,512,128]{2,1,0:T(8,128)(2,1)} %all-to-all-done.x_ref, ...), custom_call_target="tpu_custom_call" | custom-call | flops 2147483648 | bytes 16777216 | tf_op jit(solution)/shard_map/convolve/pallas_call | solution.py:147
  294.6 0.0 copy-start.3
  294.6 1.3 copy-done.3
  295.9 48.0 %all-to-all-done.4.c_ref = bf16[16,512,128]{2,1,0:T(8,128)(2,1)} async-done(((bf16[16,512,128]{2,1,0:T(8,128)(2,1)}), bf16[16,512,128]{2,1,0:T(8,128)(2,1)}, u32[]{:S(2)}, u32[]{:S(2)}) %all-to-all-start.4) | async-done | bytes 2097184 | tf_op jit(solution)/shard_map/all_to_all | solution.py:339
  343.9 8.1 %all-to-all-start.2 = ((bf16[16,512,128]{2,1,0:T(8,128)(2,1)}), bf16[16,512,128]{2,1,0:T(8,128)(2,1)}, u32[]{:S(2)}, u32[]{:S(2)}) async-start(bf16[16,512,128]{2,1,0:T(8,128)(2,1)} %copy-done.3), calls=%async_computation.2 | async-start | bytes 4194304 | tf_op jit(solution)/shard_map/all_to_all | solution.py:339
  352.0 4.0 gate.3.refs_2_
  356.0 1.2 collective-permute-start.1
  357.2 62.8 %all-to-all-done.2.c_ref = bf16[16,512,128]{2,1,0:T(8,128)(2,1)} async-done(((bf16[16,512,128]{2,1,0:T(8,128)(2,1)}), bf16[16,512,128]{2,1,0:T(8,128)(2,1)}, u32[]{:S(2)}, u32[]{:S(2)}) %all-to-all-start.2) | async-done | bytes 2097184 | tf_op jit(solution)/shard_map/all_to_all | solution.py:339
  420.1 5.0 gate.2.refs_0_
  425.0 1.2 collective-permute-start
  426.2 0.1 pad_add_fusion.start_ref
  426.3 45.1 %collective-permute-done.refs_1_ = bf16[512,2048]{1,0:T(8,128)(2,1)} collective-permute-done((bf16[512,2048]{1,0:T(8,128)(2,1)}, bf16[512,2048]{1,0:T(8,128)(2,1)}, u32[]{:S(2)}, u32[]{:S(2)}) %collective-permute-start) | collective-permute-done | bytes 2097184 | tf_op jit(solution)/shard_map/ppermute | solution.py:345
  471.4 10.8 %mix.3.refs_5_ = bf16[512,4096]{1,0:T(8,128)(2,1)} custom-call(s32[4]{0:T(128)S(1)} %pad_add_fusion.start_ref, bf16[512,2048]{1,0:T(8,128)(2,1)} %gate.2.refs_0_, bf16[512,2048]{1,0:T(8,128)(2,1)} %collective-permute-done.refs_1_, bf16[512,2048]{1,0:T(8,128)(2,1)} %copy-done.2, bf16[512,2048]{1,0:T(8,128)(2,1)} %collective-permute-done.1.refs_3_, ...), custom_call_target="tpu_custom_call" | custom-call | flops 4294967296 | bytes 8388608 | tf_op jit(solution)/shard_map/mix/pallas_call | solution.py:271
  482.2 24.7 %mix.4.refs_5_ = bf16[512,4096]{1,0:T(8,128)(2,1)} custom-call(s32[4]{0:T(128)S(1)} %pad_add_fusion.start_ref, bf16[512,2048]{1,0:T(8,128)(2,1)} %gate.2.refs_0_, bf16[512,2048]{1,0:T(8,128)(2,1)} %collective-permute-done.refs_1_, bf16[512,2048]{1,0:T(8,128)(2,1)} %copy-done.2, ...), custom_call_target="tpu_custom_call", output_to_operand_aliasing={{}: (6, {})} | custom-call | flops 17179869184 | bytes 33554432 | tf_op jit(solution)/shard_map/mix/pallas_call | solution.py:271
  506.9 86.8 %all-gather.4.cloned.1.call-done.refs_4_ = bf16[8192,1536]{1,0:T(8,128)(2,1)} async-done(((bf16[512,1536]{1,0:T(8,128)(2,1)}), bf16[8192,1536]{1,0:T(8,128)(2,1)}) %all-gather.4.cloned.1.call-update) | async-done | bytes 25165840 | tf_op jit(solution)/shard_map/all_gather | solution.py:306
  593.7 19.6 %mix.5 = bf16[512,4096]{1,0:T(8,128)(2,1)} custom-call(s32[4]{0:T(128)S(1)} %pad_add_fusion.start_ref, bf16[512,2048]{1,0:T(8,128)(2,1)} %gate.2.refs_0_, bf16[512,2048]{1,0:T(8,128)(2,1)} %collective-permute-done.refs_1_, bf16[512,2048]{1,0:T(8,128)(2,1)} %copy-done.2, ...), custom_call_target="tpu_custom_call", output_to_operand_aliasing={{}: (6, {})} | custom-call | flops 12884901888 | bytes 25165824 | tf_op jit(solution)/shard_map/mix/pallas_call | solution.py:271
  (20 shorter events, 0.1 us)
Async XLA Ops:
  6.5 189.5 %copy-start = (s32[32,32]{1,0:T(8,128)S(1)}, s32[32,32]{1,0:T(8,128)}, u32[]{:S(2)}) copy-start(s32[32,32]{1,0:T(8,128)} %param.10) | copy-start | bytes 12292
  6.5 464.8 %all-gather.8.cloned.1.call-start = ((), (), s32[]{:S(2)}) async-start(), calls=%async_computation.7 | async-start | bytes 8912896 | tf_op jit(solution)/shard_map/all_gather | solution.py:306
  8.5 473.7 %all-gather.6.cloned.1.call-start = ((), (), s32[]{:S(2)}) async-start(), calls=%async_computation.6 | async-start | bytes 35651584 | tf_op jit(solution)/shard_map/all_gather | solution.py:306
  11.8 581.9 %all-gather.4.cloned.1.call-start = ((), (), s32[]{:S(2)}) async-start(), calls=%async_computation.5 | async-start | bytes 26738688 | tf_op jit(solution)/shard_map/all_gather | solution.py:306
  22.6 89.6 %all-to-all-start.1 = ((bf16[16,2,256,128]{3,2,1,0:T(8,128)(2,1)}), bf16[16,2,256,128]{3,2,1,0:T(8,128)(2,1)S(1)}, u32[]{:S(2)}, u32[]{:S(2)}) async-start(bf16[16,2,256,128]{3,2,1,0:T(8,128)(2,1)} %pack_filters.1), calls=%async_computation.1 | async-start | bytes 4194304 | tf_op jit(solution)/shard_map/all_to_all | solution.py:314
  112.3 1.3 copy-start.6
  113.6 73.3 %all-to-all-start.3 = ((bf16[16,512,128]{2,1,0:T(8,128)(2,1)}), bf16[16,512,128]{2,1,0:T(8,128)(2,1)}, u32[]{:S(2)}, u32[]{:S(2)}) async-start(bf16[16,512,128]{2,1,0:T(8,128)(2,1)} %pack_signal.3), calls=%async_computation.3 | async-start | bytes 4194304 | tf_op jit(solution)/shard_map/all_to_all | solution.py:313
  186.9 79.1 %all-to-all-start = ((bf16[16,512,128]{2,1,0:T(8,128)(2,1)}), bf16[16,512,128]{2,1,0:T(8,128)(2,1)}, u32[]{:S(2)}, u32[]{:S(2)}) async-start(bf16[16,512,128]{2,1,0:T(8,128)(2,1)} %pack_signal.2), calls=%async_computation | async-start | bytes 4194304 | tf_op jit(solution)/shard_map/all_to_all | solution.py:313
  222.9 1.3 copy-start.4
  266.0 77.9 %all-to-all-start.4 = ((bf16[16,512,128]{2,1,0:T(8,128)(2,1)}), bf16[16,512,128]{2,1,0:T(8,128)(2,1)}, u32[]{:S(2)}, u32[]{:S(2)}) async-start(bf16[16,512,128]{2,1,0:T(8,128)(2,1)} %copy-done.4), calls=%async_computation.4 | async-start | bytes 4194304 | tf_op jit(solution)/shard_map/all_to_all | solution.py:339
  294.6 1.3 copy-start.3
  295.9 56.1 %copy-start.5 = (f32[4096]{0:T(1024)S(1)}, f32[4096]{0:T(1024)}, u32[]{:S(2)}) copy-start(f32[4096]{0:T(1024)} %param.8) | copy-start | bytes 49156
  343.9 76.1 %all-to-all-start.2 = ((bf16[16,512,128]{2,1,0:T(8,128)(2,1)}), bf16[16,512,128]{2,1,0:T(8,128)(2,1)}, u32[]{:S(2)}, u32[]{:S(2)}) async-start(bf16[16,512,128]{2,1,0:T(8,128)(2,1)} %copy-done.3), calls=%async_computation.2 | async-start | bytes 4194304 | tf_op jit(solution)/shard_map/all_to_all | solution.py:339
  356.0 69.0 %copy-start.2 = (bf16[512,2048]{1,0:T(8,128)(2,1)}, bf16[512,2048]{1,0:T(8,128)(2,1)S(1)}, u32[]{:S(2)}) copy-start(bf16[512,2048]{1,0:T(8,128)(2,1)S(1)} %gate.3.refs_2_) | copy-start | bytes 6291460
  356.0 70.3 %collective-permute-start.1 = (bf16[512,2048]{1,0:T(8,128)(2,1)S(1)}, bf16[512,2048]{1,0:T(8,128)(2,1)}, u32[]{:S(2)}, u32[]{:S(2)}) collective-permute-start(bf16[512,2048]{1,0:T(8,128)(2,1)S(1)} %gate.3.refs_2_), channel_id=1, source_target_pairs={{0,1},{1,0},{2,3},{3,2},{4,5},{5,4},{6,7},{7,6},{8,9},{9,8},{10,11... | collective-permute-start | bytes 6291464 | tf_op jit(solution)/shard_map/ppermute | solution.py:345
  425.0 46.3 %collective-permute-start = (bf16[512,2048]{1,0:T(8,128)(2,1)}, bf16[512,2048]{1,0:T(8,128)(2,1)}, u32[]{:S(2)}, u32[]{:S(2)}) collective-permute-start(bf16[512,2048]{1,0:T(8,128)(2,1)} %gate.2.refs_0_), channel_id=1, source_target_pairs={{0,1},{1,0},{2,3},{3,2},{4,5},{5,4},{6,7},{7,6},{8,9},{9,8},{10,11... | collective-permute-start | bytes 6291464 | tf_op jit(solution)/shard_map/ppermute | solution.py:345
  593.7 19.6 %copy-start.1 = (s32[32,32]{1,0:T(8,128)S(1)}, s32[32,32]{1,0:T(8,128)}, u32[]{:S(2)}) copy-start(s32[32,32]{1,0:T(8,128)} %param.10) | copy-start | bytes 12292
Sparse Core Ops, SparseCore 0:
  9.5 107.7 all-gather.7
  118.9 345.5 all-gather.5
  466.1 127.5 all-gather.3

commit v13 on v12

--- a/solution.py
+++ b/solution.py
@@ -301,7 +301,7 @@
 
     columns = out_weight.shape[1]
     eighth = columns // 8
-    bounds = [0, eighth, 5 * eighth, columns] if eighth % 256 == 0 else [0, columns]
+    bounds = [0, 9 * (eighth // 2), columns] if eighth % 512 == 0 else [0, columns]
     weights = [
         lax.all_gather(out_weight[:, low:high], "seq", axis=0, tiled=True)
         for low, high in zip(bounds[:-1], bounds[1:])

time: 622 us -> 604 us (0.971)
  waiting for transfers between devices: 424 us -> 417 us
    all_to_all x1, waiting for transfers between devices: 79.1 us -> 65.9 us  [body(): filters = exchange(pack_filters(filter_values, cycle, chunks, unit))]
    pallas_call x3 -> x2, Pallas kernels: 55.2 us -> 47.8 us  [mix(): pl.pallas_call(functools.partial(mix_kernel, pieces), grid=(part // tile,...]
    all_gather x3 -> x2, waiting for transfers between devices: 86.8 us -> 89.5 us  [body(): lax.all_gather(out_weight[:, low:high], 'seq', axis=0, tiled=True)]
  transfers between devices with their start and end apart: 10 -> 9, of which waited for: 7 -> 7; matrix products, arithmetic and copies ran while one was open for 2% -> 2% of each run, Pallas kernels for 16% -> 16%
where the time goes in v13:
time: 604 us; the launch traced here: 601 us
  waiting for transfers between devices  417 us (69%)
  Pallas kernels  115 us (19%)
  starting transfers between devices  39.8 us (7%)
  between operations  13.5 us (2%)
  local copies, waits for them, and re-layouts  11.2 us (2%)
    all_to_all x2, waiting for transfers between devices, body(): done = exchange(convolve(g, twist, ahead, back, signals[g], filters))  108 us
    all_to_all x2, waiting for transfers between devices, body(): exchange(pack_signal(keyval, g, cycle, unit))  108 us
    all_gather x2, waiting for transfers between devices, body(): lax.all_gather(out_weight[:, low:high], 'seq', axis=0, tiled=True)  89.5 us
    all_to_all x1, waiting for transfers between devices, body(): filters = exchange(pack_filters(filter_values, cycle, chunks, unit))  65.9 us
    pallas_call x2, Pallas kernels, mix(): pl.pallas_call(functools.partial(mix_kernel, pieces), grid=(part // tile,...  47.8 us
    ppermute x2, waiting for transfers between devices, body(): lax.ppermute(own, 'tensor', [(t, (t + shift) % peers) for t in range(peer...  45.2 us
    pallas_call x2, Pallas kernels, convolve(): pl.pallas_call(conv_kernel, grid=(1,), out_shape=jax.ShapeDtypeStruct(sig...  41.2 us
    all_to_all x2, starting transfers between devices, body(): exchange(pack_signal(keyval, g, cycle, unit))  16.1 us
  transfers between devices with their start and end apart: 9, of which 7 were waited for; matrix products, arithmetic and copies ran while one was open for 2% of the time, Pallas kernels for 16%

profile of v13, /device:TPU:9, one launch (start us, length us, event | category | flops | bytes accessed | tf_op | source)
XLA Modules:
  0.0 601.4 jit_solution(3613636413683600948)
XLA Ops:
  6.5 0.0 copy-start
  6.5 0.0 all-gather.5.cloned.1.call-start
  6.5 3.2 slice.7
  9.8 0.0 all-gather.5.cloned.1.call-update
  9.8 0.0 all-gather.3.cloned.1.call-start
  9.8 2.9 slice.6
  12.8 0.0 all-gather.3.cloned.1.call-update
  12.8 8.3 %pack_filters.1 = bf16[16,2,256,128]{3,2,1,0:T(8,128)(2,1)} custom-call(f32[256,1,4096]{2,1,0:T(1,128)} %bitcast.10), custom_call_target="tpu_custom_call" | custom-call | bytes 6291456 | tf_op jit(solution)/shard_map/pack_filters/pallas_call | solution.py:205
  21.1 6.6 %all-to-all-start.1 = ((bf16[16,2,256,128]{3,2,1,0:T(8,128)(2,1)}), bf16[16,2,256,128]{3,2,1,0:T(8,128)(2,1)S(1)}, u32[]{:S(2)}, u32[]{:S(2)}) async-start(bf16[16,2,256,128]{3,2,1,0:T(8,128)(2,1)} %pack_filters.1), calls=%async_computation.1 | async-start | bytes 4194304 | tf_op jit(solution)/shard_map/all_to_all | solution.py:314
  27.6 3.9 pack_signal.3
  31.5 65.9 %all-to-all-done.1.filter_ref = bf16[16,2,256,128]{3,2,1,0:T(8,128)(2,1)S(1)} async-done(((bf16[16,2,256,128]{3,2,1,0:T(8,128)(2,1)}), bf16[16,2,256,128]{3,2,1,0:T(8,128)(2,1)S(1)}, u32[]{:S(2)}, u32[]{:S(2)}) %all-to-all-start.1) | async-done | bytes 2097184 | tf_op jit(solution)/shard_map/all_to_all | solution.py:314
  97.4 1.4 copy-done.5
  98.8 8.0 %all-to-all-start.3 = ((bf16[16,512,128]{2,1,0:T(8,128)(2,1)}), bf16[16,512,128]{2,1,0:T(8,128)(2,1)}, u32[]{:S(2)}, u32[]{:S(2)}) async-start(bf16[16,512,128]{2,1,0:T(8,128)(2,1)} %pack_signal.3), calls=%async_computation.3 | async-start | bytes 4194304 | tf_op jit(solution)/shard_map/all_to_all | solution.py:313
  106.8 3.9 pack_signal.2
  110.7 66.0 %all-to-all-done.3.x_ref = bf16[16,512,128]{2,1,0:T(8,128)(2,1)} async-done(((bf16[16,512,128]{2,1,0:T(8,128)(2,1)}), bf16[16,512,128]{2,1,0:T(8,128)(2,1)}, u32[]{:S(2)}, u32[]{:S(2)}) %all-to-all-start.3) | async-done | bytes 2097184 | tf_op jit(solution)/shard_map/all_to_all | solution.py:313
  176.8 8.1 %all-to-all-start = ((bf16[16,512,128]{2,1,0:T(8,128)(2,1)}), bf16[16,512,128]{2,1,0:T(8,128)(2,1)}, u32[]{:S(2)}, u32[]{:S(2)}) async-start(bf16[16,512,128]{2,1,0:T(8,128)(2,1)} %pack_signal.2), calls=%async_computation | async-start | bytes 4194304 | tf_op jit(solution)/shard_map/all_to_all | solution.py:313
  184.9 0.0 copy-done
  184.9 0.6 gather_fusion
  185.5 0.1 select_multiply_fusion
  185.6 0.1 add.116
  185.6 0.1 add.117
  185.7 0.1 add.119
  185.9 0.1 fusion.22
  186.0 0.1 copy.8.twist_ref
  186.2 2.3 negate_convert_fusion
  188.4 0.1 maximum_maximum_fusion.1.back_ref
  188.5 2.5 fusion.15
  191.0 0.1 maximum_maximum_fusion.ahead_ref
  191.2 20.6 %convolve.3 = bf16[16,512,128]{2,1,0:T(8,128)(2,1)S(1)} custom-call(f32[512,32]{1,0:T(8,128)S(1)} %copy.8.twist_ref, bf16[2,256,1024]{2,1,0:T(8,128)(2,1)S(1)} %maximum_maximum_fusion.ahead_ref, bf16[2,1024,256]{2,1,0:T(8,128)(2,1)S(1)} %maximum_maximum_fusion.1.back_ref, bf16[16,512,128]{2,1,0:T(8,128)(2,1)} %all-to-all-done.3.x_ref, ...), custom_call_target="tpu_custom_call" | custom-call | flops 2147483648 | bytes 16777216 | tf_op jit(solution)/shard_map/convolve/pallas_call | solution.py:147
  211.7 0.0 copy-start.3
  211.7 1.4 copy-done.3
  213.1 41.7 %all-to-all-done.x_ref = bf16[16,512,128]{2,1,0:T(8,128)(2,1)} async-done(((bf16[16,512,128]{2,1,0:T(8,128)(2,1)}), bf16[16,512,128]{2,1,0:T(8,128)(2,1)}, u32[]{:S(2)}, u32[]{:S(2)}) %all-to-all-start) | async-done | bytes 2097184 | tf_op jit(solution)/shard_map/all_to_all | solution.py:313
  254.8 8.1 %all-to-all-start.4 = ((bf16[16,512,128]{2,1,0:T(8,128)(2,1)}), bf16[16,512,128]{2,1,0:T(8,128)(2,1)}, u32[]{:S(2)}, u32[]{:S(2)}) async-start(bf16[16,512,128]{2,1,0:T(8,128)(2,1)} %copy-done.3), calls=%async_computation.4 | async-start | bytes 4194304 | tf_op jit(solution)/shard_map/all_to_all | solution.py:339
  262.9 20.6 %convolve.2 = bf16[16,512,128]{2,1,0:T(8,128)(2,1)S(1)} custom-call(f32[512,32]{1,0:T(8,128)S(1)} %copy.8.twist_ref, bf16[2,256,1024]{2,1,0:T(8,128)(2,1)S(1)} %maximum_maximum_fusion.ahead_ref, bf16[2,1024,256]{2,1,0:T(8,128)(2,1)S(1)} %maximum_maximum_fusion.1.back_ref, bf16[16,512,128]{2,1,0:T(8,128)(2,1)} %all-to-all-done.x_ref, ...), custom_call_target="tpu_custom_call" | custom-call | flops 2147483648 | bytes 16777216 | tf_op jit(solution)/shard_map/convolve/pallas_call | solution.py:147
  283.5 1.3 copy-done.2
  284.8 46.8 %all-to-all-done.4.c_ref = bf16[16,512,128]{2,1,0:T(8,128)(2,1)} async-done(((bf16[16,512,128]{2,1,0:T(8,128)(2,1)}), bf16[16,512,128]{2,1,0:T(8,128)(2,1)}, u32[]{:S(2)}, u32[]{:S(2)}) %all-to-all-start.4) | async-done | bytes 2097184 | tf_op jit(solution)/shard_map/all_to_all | solution.py:339
  331.6 6.4 %all-to-all-start.2 = ((bf16[16,512,128]{2,1,0:T(8,128)(2,1)}), bf16[16,512,128]{2,1,0:T(8,128)(2,1)S(1)}, u32[]{:S(2)}, u32[]{:S(2)}) async-start(bf16[16,512,128]{2,1,0:T(8,128)(2,1)} %copy-done.2), calls=%async_computation.2 | async-start | bytes 4194304 | tf_op jit(solution)/shard_map/all_to_all | solution.py:339
  338.0 5.1 gate.3.refs_2_
  343.1 1.3 collective-permute-start.1
  344.4 61.7 %all-to-all-done.2.c_ref = bf16[16,512,128]{2,1,0:T(8,128)(2,1)S(1)} async-done(((bf16[16,512,128]{2,1,0:T(8,128)(2,1)}), bf16[16,512,128]{2,1,0:T(8,128)(2,1)S(1)}, u32[]{:S(2)}, u32[]{:S(2)}) %all-to-all-start.2) | async-done | bytes 2097184 | tf_op jit(solution)/shard_map/all_to_all | solution.py:339
  406.1 4.6 gate.2.refs_0_
  410.7 1.2 collective-permute-start
  412.0 0.1 pad_add_fusion.start_ref
  412.0 0.0 collective-permute-done.1.refs_3_
  412.0 45.2 %collective-permute-done.refs_1_ = bf16[512,2048]{1,0:T(8,128)(2,1)S(1)} collective-permute-done((bf16[512,2048]{1,0:T(8,128)(2,1)}, bf16[512,2048]{1,0:T(8,128)(2,1)S(1)}, u32[]{:S(2)}, u32[]{:S(2)}) %collective-permute-start) | collective-permute-done | bytes 2097184 | tf_op jit(solution)/shard_map/ppermute | solution.py:345
  457.2 26.4 %mix.2.refs_5_ = bf16[512,4096]{1,0:T(8,128)(2,1)} custom-call(s32[4]{0:T(128)S(1)} %pad_add_fusion.start_ref, bf16[512,2048]{1,0:T(8,128)(2,1)} %gate.2.refs_0_, bf16[512,2048]{1,0:T(8,128)(2,1)S(1)} %collective-permute-done.refs_1_, bf16[512,2048]{1,0:T(8,128)(2,1)} %gate.3.refs_2_, bf16[512,2048]{1,0:T(8,128)(2,1)} %collective-permute-done.1.refs_3_, ...), custom_call_target="tpu_custom_call" | custom-call | flops 19327352832 | bytes 37748736 | tf_op jit(solution)/shard_map/mix/pallas_call | solution.py:271
  483.7 89.5 %all-gather.3.cloned.1.call-done.refs_4_ = bf16[8192,1792]{1,0:T(8,128)(2,1)} async-done(((bf16[512,1792]{1,0:T(8,128)(2,1)}), bf16[8192,1792]{1,0:T(8,128)(2,1)}) %all-gather.3.cloned.1.call-update) | async-done | bytes 29360144 | tf_op jit(solution)/shard_map/all_gather | solution.py:306
  573.2 21.4 %mix.3 = bf16[512,4096]{1,0:T(8,128)(2,1)} custom-call(s32[4]{0:T(128)S(1)} %pad_add_fusion.start_ref, bf16[512,2048]{1,0:T(8,128)(2,1)} %gate.2.refs_0_, bf16[512,2048]{1,0:T(8,128)(2,1)S(1)} %collective-permute-done.refs_1_, bf16[512,2048]{1,0:T(8,128)(2,1)} %gate.3.refs_2_, ...), custom_call_target="tpu_custom_call", output_to_operand_aliasing={{}: (6, {})} | custom-call | flops 15032385536 | bytes 29360128 | tf_op jit(solution)/shard_map/mix/pallas_call | solution.py:271
  (13 shorter events, 0.1 us)
Async XLA Ops:
  6.5 178.4 %copy-start = (s32[32,32]{1,0:T(8,128)S(1)}, s32[32,32]{1,0:T(8,128)}, u32[]{:S(2)}) copy-start(s32[32,32]{1,0:T(8,128)} %param.10) | copy-start | bytes 12292
  6.5 450.7 %all-gather.5.cloned.1.call-start = ((), (), s32[]{:S(2)}) async-start(), calls=%async_computation.6 | async-start | bytes 40108032 | tf_op jit(solution)/shard_map/all_gather | solution.py:306
  9.8 563.4 %all-gather.3.cloned.1.call-start = ((), (), s32[]{:S(2)}) async-start(), calls=%async_computation.5 | async-start | bytes 31195136 | tf_op jit(solution)/shard_map/all_gather | solution.py:306
  21.1 76.4 %all-to-all-start.1 = ((bf16[16,2,256,128]{3,2,1,0:T(8,128)(2,1)}), bf16[16,2,256,128]{3,2,1,0:T(8,128)(2,1)S(1)}, u32[]{:S(2)}, u32[]{:S(2)}) async-start(bf16[16,2,256,128]{3,2,1,0:T(8,128)(2,1)} %pack_filters.1), calls=%async_computation.1 | async-start | bytes 4194304 | tf_op jit(solution)/shard_map/all_to_all | solution.py:314
  97.4 1.4 copy-start.5
  98.8 77.9 %all-to-all-start.3 = ((bf16[16,512,128]{2,1,0:T(8,128)(2,1)}), bf16[16,512,128]{2,1,0:T(8,128)(2,1)}, u32[]{:S(2)}, u32[]{:S(2)}) async-start(bf16[16,512,128]{2,1,0:T(8,128)(2,1)} %pack_signal.3), calls=%async_computation.3 | async-start | bytes 4194304 | tf_op jit(solution)/shard_map/all_to_all | solution.py:313
  176.8 78.0 %all-to-all-start = ((bf16[16,512,128]{2,1,0:T(8,128)(2,1)}), bf16[16,512,128]{2,1,0:T(8,128)(2,1)}, u32[]{:S(2)}, u32[]{:S(2)}) async-start(bf16[16,512,128]{2,1,0:T(8,128)(2,1)} %pack_signal.2), calls=%async_computation | async-start | bytes 4194304 | tf_op jit(solution)/shard_map/all_to_all | solution.py:313
  211.7 1.4 copy-start.3
  254.8 76.8 %all-to-all-start.4 = ((bf16[16,512,128]{2,1,0:T(8,128)(2,1)}), bf16[16,512,128]{2,1,0:T(8,128)(2,1)}, u32[]{:S(2)}, u32[]{:S(2)}) async-start(bf16[16,512,128]{2,1,0:T(8,128)(2,1)} %copy-done.3), calls=%async_computation.4 | async-start | bytes 4194304 | tf_op jit(solution)/shard_map/all_to_all | solution.py:339
  283.5 1.3 copy-start.2
  284.8 53.2 %copy-start.4 = (f32[4096]{0:T(1024)S(1)}, f32[4096]{0:T(1024)}, u32[]{:S(2)}) copy-start(f32[4096]{0:T(1024)} %param.8) | copy-start | bytes 49156
  331.6 74.5 %all-to-all-start.2 = ((bf16[16,512,128]{2,1,0:T(8,128)(2,1)}), bf16[16,512,128]{2,1,0:T(8,128)(2,1)S(1)}, u32[]{:S(2)}, u32[]{:S(2)}) async-start(bf16[16,512,128]{2,1,0:T(8,128)(2,1)} %copy-done.2), calls=%async_computation.2 | async-start | bytes 4194304 | tf_op jit(solution)/shard_map/all_to_all | solution.py:339
  343.1 68.9 %collective-permute-start.1 = (bf16[512,2048]{1,0:T(8,128)(2,1)}, bf16[512,2048]{1,0:T(8,128)(2,1)}, u32[]{:S(2)}, u32[]{:S(2)}) collective-permute-start(bf16[512,2048]{1,0:T(8,128)(2,1)} %gate.3.refs_2_), channel_id=1, source_target_pairs={{0,1},{1,0},{2,3},{3,2},{4,5},{5,4},{6,7},{7,6},{8,9},{9,8},{10,11... | collective-permute-start | bytes 6291464 | tf_op jit(solution)/shard_map/ppermute | solution.py:345
  410.7 46.5 %collective-permute-start = (bf16[512,2048]{1,0:T(8,128)(2,1)}, bf16[512,2048]{1,0:T(8,128)(2,1)S(1)}, u32[]{:S(2)}, u32[]{:S(2)}) collective-permute-start(bf16[512,2048]{1,0:T(8,128)(2,1)} %gate.2.refs_0_), channel_id=1, source_target_pairs={{0,1},{1,0},{2,3},{3,2},{4,5},{5,4},{6,7},{7,6},{8,9},{9,8},{10,11... | collective-permute-start | bytes 6291464 | tf_op jit(solution)/shard_map/ppermute | solution.py:345
  573.2 21.4 %copy-start.1 = (s32[32,32]{1,0:T(8,128)S(1)}, s32[32,32]{1,0:T(8,128)}, u32[]{:S(2)}) copy-start(s32[32,32]{1,0:T(8,128)} %param.10) | copy-start | bytes 12292
Sparse Core Ops, SparseCore 0:
  9.9 414.1 all-gather.4
  425.7 147.4 all-gather.2
